TPU v7x, 32 devices: a whole 2x2x4 slice. The times are simulated.
32 devices in a mesh: node: 8 (over z, x), tm: 4 (over y, core).
Axes of the slice: x: 2, y: 2, z: 4, core: 2. Of those that a mesh axis runs over, the one named last changes fastest.
Arguments:
- codes: int32 [32768, 512], P('node', 'tm'), may hold values from -127 to 127
- node_scale: float32 [32768], P('node'), may hold values from 0.002 to 0.02
- basis: bfloat16 [32768, 128], P('node'), may hold values from -0.03125 to 0.03125
- regular: float32 [8384], replicated, may hold values from 0.05 to 0.5
- feature_order: int32 [8384], replicated, may hold values from 0 to 8383, each once
- panel_inverse: float32 [2, 262, 262], replicated, may hold values from -0.06 to 1.2
Outputs:
- schur: float32 [8384, 8384], P('node', 'tm')
Inputs may be any that keep to these rules, and one draw needn't show every extreme that they name: `feature_order`: a permutation: every feature stands at exactly one position.
All inputs are finite; a program needn't handle non-finite values.
Results may differ from a plain program's by a relative error of at most 0.0051.
Values sent between devices are 32-bit elements; how exact they have to be, the bound alone decides.
No kernel may reach another device: no remote copies, remote signals or barrier semaphores. Data moves between devices by JAX's collectives and lax.ppermute only.
A program may use at most 64 MiB of HBM per device.

v0:
```python
import jax
import jax.numpy as jnp
import numpy as np
from jax import lax
from jax.sharding import PartitionSpec as P


def from_root(block, axis, source):
    block = jnp.where(lax.axis_index(axis) == source, block, jnp.zeros_like(block))
    return lax.psum(block, axis)


def pair_tables(rank_count):
    former_list = []
    latter_list = []
    for leading in range(rank_count + 1):
        for trailing in range(leading, rank_count + 1):
            if leading < rank_count or trailing < rank_count:
                former_list.append(leading)
                latter_list.append(trailing)
    return (np.array(former_list, np.int32), np.array(latter_list, np.int32))


def selectors(chosen, rank_count):
    former, latter = pair_tables(rank_count)
    leading = jnp.take(jnp.asarray(former), chosen)
    trailing = jnp.take(jnp.asarray(latter), chosen)
    lead_index = jnp.minimum(leading, rank_count - 1)
    trail_index = jnp.minimum(trailing, rank_count - 1)
    lead_keep = (leading < rank_count).astype(jnp.float32)
    trail_keep = (trailing < rank_count).astype(jnp.float32)
    return (lead_index, lead_keep, trail_index, trail_keep)


def make_features(window, picks):
    lead_index, lead_keep, trail_index, trail_keep = picks
    lead_vals = (
        jnp.take(window, lead_index, axis=1) * lead_keep[None, :] + (1.0 - lead_keep)[None, :]
    )
    trail_vals = (
        jnp.take(window, trail_index, axis=1) * trail_keep[None, :] + (1.0 - trail_keep)[None, :]
    )
    return (lead_vals * trail_vals).astype(jnp.bfloat16)


def contract(left_feats, right_feats):
    return lax.dot_general(
        left_feats, right_feats, (((0,), (0,)), ((), ())), preferred_element_type=jnp.float32
    )


def highest(left_mat, right_mat):
    return jnp.dot(
        left_mat, right_mat, precision=lax.Precision.HIGHEST, preferred_element_type=jnp.float32
    )


def per_device(codes, node_scale, basis, regular, feature_order, panel_inverse):
    rank_count = basis.shape[1]
    snap_local = codes.shape[1]
    nfeat = regular.shape[0]
    row_size = nfeat // lax.axis_size("node")
    col_size = nfeat // lax.axis_size("tm")
    snap_total = snap_local * lax.axis_size("tm")
    panel_count = panel_inverse.shape[0]
    panel_width = panel_inverse.shape[1]
    scaled_basis = (basis.astype(jnp.float32) * node_scale[:, None]).astype(jnp.bfloat16)
    code_values = codes.astype(jnp.bfloat16)
    row_offset = lax.axis_index("node") * row_size
    col_offset = lax.axis_index("tm") * col_size
    row_picks = selectors(lax.dynamic_slice_in_dim(feature_order, row_offset, row_size), rank_count)
    col_picks = selectors(lax.dynamic_slice_in_dim(feature_order, col_offset, col_size), rank_count)
    empty_tile = jnp.zeros((row_size, col_size), jnp.float32)
    window = code_values
    summed = lax.psum(
        lax.dot_general(
            window, scaled_basis, (((0,), (0,)), ((), ())), preferred_element_type=jnp.float32
        ),
        "node",
    )
    running = empty_tile
    portion = lax.all_gather(summed, "tm", axis=0, tiled=True)
    length = portion.shape[0]
    stride = min(length, 1024)
    for anchor in range(0, length, stride):
        window = portion[anchor : anchor + stride]
        running = running + contract(
            make_features(window, row_picks), make_features(window, col_picks)
        )
    row_global = row_offset + jnp.arange(row_size, dtype=jnp.int32)
    col_global = col_offset + jnp.arange(col_size, dtype=jnp.int32)
    on_diagonal = (row_global[:, None] == col_global[None, :]).astype(jnp.float32)
    row_regular = lax.dynamic_slice_in_dim(regular, row_offset, row_size)
    matrix = running / snap_total + on_diagonal * row_regular[:, None]

    def local_starts(panel_number):
        panel_lower = panel_number * panel_width
        col_start = panel_lower - panel_lower // col_size * col_size
        row_start = panel_lower - panel_lower // row_size * row_size
        return (col_start, row_start)

    def send_slabs(column_slab, row_slab, panel_number):
        panel_lower = panel_number * panel_width
        left_part = from_root(column_slab, "tm", panel_lower // col_size)
        upper_part = from_root(row_slab, "node", panel_lower // row_size)
        return (left_part, upper_part)

    col_start, row_start = local_starts(0)
    left_part, upper_part = send_slabs(
        matrix[:, col_start : col_start + panel_width],
        matrix[row_start : row_start + panel_width, :],
        0,
    )
    for panel_number in range(panel_count):
        scaled_left = highest(left_part, panel_inverse[panel_number])
        if panel_number + 1 < panel_count:
            next_col, next_row = local_starts(panel_number + 1)
            next_columns = matrix[:, next_col : next_col + panel_width] - highest(
                scaled_left, upper_part[:, next_col : next_col + panel_width]
            )
            next_rows = matrix[next_row : next_row + panel_width, :] - highest(
                scaled_left[next_row : next_row + panel_width], upper_part
            )
        matrix = matrix - highest(scaled_left, upper_part)
        if panel_number + 1 < panel_count:
            left_part, upper_part = send_slabs(next_columns, next_rows, panel_number + 1)
    return matrix


def solution(mesh):
    placed = (P("node", "tm"), P("node"), P("node", None), P(), P(), P())
    return jax.shard_map(
        per_device, mesh=mesh, in_specs=placed, out_specs=P("node", "tm"), check_vma=False
    )
```

profile of v0, /device:TPU:0, one launch (start us, length us, event | category | flops | bytes accessed | tf_op | source)
XLA Modules:
  0.0 466.8 jit_solution(14562613058606793020)
XLA Ops:
  6.5 0.0 all-reduce.6.cloned.1.call-start
  6.5 3.7 convolution_bitcast_fusion
  10.2 0.0 all-reduce.6.cloned.1.call-update
  10.2 0.0 all-reduce.8.cloned.1.call-start
  10.3 0.0 copy-done.6
  10.3 0.1 compare_select_fusion.5
  10.4 0.0 copy-done.1
  10.4 0.0 copy-start
  10.4 6.2 %gather_fusion.2 = s32[1048]{0:T(1024)S(1)} fusion(s32[8384]{0:T(1024)S(1)} %copy-done.1, s32[2048]{0:T(1024)S(1)} %pad_clamp_fusion.5), kind=kCustom, calls=%fused_computation.4.clone | custom fusion | bytes 12576 | tf_op jit(solution)/shard_map/jit(_take)/gather | solution.py:27
  16.6 0.0 copy-done
  16.6 6.2 %gather_fusion = s32[1048]{0:T(1024)S(1)} fusion(s32[8384]{0:T(1024)S(1)} %copy-done, s32[2048]{0:T(1024)S(1)} %pad_clamp_fusion.5), kind=kCustom, calls=%fused_computation.clone | custom fusion | bytes 12576 | tf_op jit(solution)/shard_map/jit(_take)/gather | solution.py:26
  22.8 0.1 compare_select_fusion.2
  22.9 11.4 %gather_fusion.6 = s32[2096]{0:T(1024)S(1)} fusion(s32[8384]{0:T(1024)S(1)} %copy-done.1, s32[3072]{0:T(1024)S(1)} %pad_clamp_fusion.2), kind=kCustom, calls=%fused_computation.6.clone | custom fusion | bytes 25152 | tf_op jit(solution)/shard_map/jit(_take)/gather | solution.py:27
  34.3 11.4 %gather_fusion.4 = s32[2096]{0:T(1024)S(1)} fusion(s32[8384]{0:T(1024)S(1)} %copy-done, s32[3072]{0:T(1024)S(1)} %pad_clamp_fusion.2), kind=kCustom, calls=%fused_computation.2.clone | custom fusion | bytes 25152 | tf_op jit(solution)/shard_map/jit(_take)/gather | solution.py:26
  45.7 0.1 compare_and_fusion.4
  45.9 0.1 compare_and_fusion.1
  46.0 0.8 dynamic_slice.11
  46.8 35.2 %all-reduce.6.cloned.1.call-done = f32[128,128]{0,1:T(8,128)} async-done(((f32[128,128]{0,1:T(8,128)}), f32[128,128]{0,1:T(8,128)}) %all-reduce.6.cloned.1.call-update) | async-done | bytes 65552 | tf_op jit(solution)/shard_map/psum | solution.py:75
  82.0 6.0 %all_gather.3 = f32[512,128]{0,1:T(8,128)S(1)} all-gather(f32[128,128]{0,1:T(8,128)} %all-reduce.6.cloned.1.call-done), channel_id=1, replica_groups=mesh['node'=8,'tm'=4] {'tm'}, dimensions={0}, use_global_device_ids=true | all-gather | bytes 327680 | tf_op jit(solution)/shard_map/all_gather | solution.py:82
  88.0 3.2 gather_fusion.3
  91.2 4.2 gather_fusion.1
  95.5 6.8 %gather_fusion.7 = f32[2096,512]{1,0:T(8,128)} fusion(f32[512,128]{0,1:T(8,128)S(1)} %all_gather.3, s32[3072]{0:T(1024)S(1)} %pad_clamp_fusion), kind=kCustom, calls=%fused_computation.7.clone | custom fusion | bytes 8593600 | tf_op jit(solution)/shard_map/jit(_take)/gather | solution.py:41
  102.2 6.8 %gather_fusion.5 = f32[2096,512]{1,0:T(8,128)} fusion(f32[512,128]{0,1:T(8,128)S(1)} %all_gather.3, s32[3072]{0:T(1024)S(1)} %pad_clamp_fusion.1), kind=kCustom, calls=%fused_computation.3.clone | custom fusion | bytes 8593600 | tf_op jit(solution)/shard_map/jit(_take)/gather | solution.py:38
  109.1 6.0 %fusion.49 = bf16[512,2096]{0,1:T(8,128)(2,1)S(1)} fusion(f32[2096,512]{1,0:T(8,128)} %gather_fusion.7, f32[2096,512]{1,0:T(8,128)} %gather_fusion.5, f32[2096]{0:T(1024)S(1)} %get-tuple-element.29, f32[2096]{0:T(1024)S(1)} %get-tuple-element.30, f32[2096]{0:T(1024)S(1)} %get-tuple-element.23, f32[2096]{0:T(1024)S(1)} %get-tuple-element.24, ...), kind=kLoop, calls=%fused_computation.15.clone.clone.2 | loop fusion | flops 8585216 | bytes 10769248 | tf_op jit(solution)/shard_map/dot_general | solution.py:47
  115.1 3.4 fusion
  118.5 0.0 copy-start.2
  118.5 3.6 copy-done.2
  122.1 1.3 slice_select_fusion.1
  123.4 0.0 all-reduce.8.cloned.1.call-update
  123.4 0.0 all-reduce.10.cloned.1.call-start
  123.5 3.2 slice_select_fusion
  126.7 0.0 all-reduce.10.cloned.1.call-update
  126.7 0.2 all-reduce.12.cloned.1.call-start
  127.0 0.9 copy-done.5
  127.8 1.4 fusion.34
  129.2 38.1 %all-reduce.8.cloned.1.call-done = f32[1048,262]{1,0:T(8,128)} async-done(((f32[1048,262]{1,0:T(8,128)}), f32[1048,262]{1,0:T(8,128)}) %all-reduce.8.cloned.1.call-update) | async-done | bytes 1098320 | tf_op jit(solution)/shard_map/psum | solution.py:10
  167.3 3.8 fusion.32
  171.2 107.8 %all-reduce.10.cloned.1.call-done = f32[262,2096]{1,0:T(8,128)} async-done(((f32[262,2096]{1,0:T(8,128)}), f32[262,2096]{1,0:T(8,128)}) %all-reduce.10.cloned.1.call-update) | async-done | bytes 2196624 | tf_op jit(solution)/shard_map/psum | solution.py:10
  279.0 6.9 %fusion.6 = f32[1048,262]{1,0:T(8,128)} fusion(f32[1048,262]{0,1:T(8,128)S(1)} %fusion.32, f32[1048,2096]{1,0:T(8,128)} %copy-done.2, pred[]{:T(512)S(6)} %eq.24, f32[262,2096]{1,0:T(8,128)} %all-reduce.10.cloned.1.call-done), kind=kOutput, calls=%fused_computation.21 | convolution fusion | flops 863816064 | bytes 4211841 | tf_op jit(solution)/shard_map/dot_general | solution.py:53
  285.9 0.0 all-reduce.12.cloned.1.call-update
  285.9 0.0 all-reduce.14.cloned.1.call-start
  285.9 7.5 %fusion.5 = f32[262,2096]{1,0:T(8,128)} fusion(f32[262,2096]{1,0:T(8,128)S(1)} %copy-done.3, f32[1048,2096]{1,0:T(8,128)} %copy-done.2, pred[]{:T(512)S(6)} %eq.25, f32[1048,262]{0,1:T(8,128)S(1)} %fusion.32), kind=kOutput, calls=%fused_computation.19 | convolution fusion | flops 1727632128 | bytes 7096577 | tf_op jit(solution)/shard_map/dot_general | solution.py:53
  293.4 0.0 all-reduce.14.cloned.1.call-update
  293.4 19.9 %convolution_subtract_fusion = f32[1048,2096]{1,0:T(8,128)} fusion(f32[1048,2096]{1,0:T(8,128)} %copy-done.2, f32[1048,262]{0,1:T(8,128)S(1)} %fusion.32, f32[262,2096]{1,0:T(8,128)S(1)} %copy-done.3), kind=kOutput, calls=%fused_computation.8 | convolution fusion | flops 6908332032 | bytes 20867776 | tf_op jit(solution)/shard_map/dot_general | solution.py:53
  313.3 15.5 %all-reduce.12.cloned.1.call-done = f32[1048,262]{1,0:T(8,128)} async-done(((f32[1048,262]{1,0:T(8,128)}), f32[1048,262]{1,0:T(8,128)}) %all-reduce.12.cloned.1.call-update) | async-done | bytes 1098320 | tf_op jit(solution)/shard_map/psum | solution.py:10
  328.9 5.0 %fusion.31 = f32[1048,262]{1,0:T(8,128)S(1)} fusion(f32[1048,262]{1,0:T(8,128)} %all-reduce.12.cloned.1.call-done, f32[1,262,262]{2,0,1:T(1,128)} %get-tuple-element.27), kind=kOutput, calls=%fused_computation.51 | convolution fusion | flops 863266944 | bytes 2471184 | tf_op jit(solution)/shard_map/dot_general | solution.py:53
  333.9 106.5 %all-reduce.14.cloned.1.call-done = f32[262,2096]{1,0:T(8,128)} async-done(((f32[262,2096]{1,0:T(8,128)}), f32[262,2096]{1,0:T(8,128)}) %all-reduce.14.cloned.1.call-update) | async-done | bytes 2196624 | tf_op jit(solution)/shard_map/psum | solution.py:10
  440.4 19.9 %convolution_subtract_fusion.1 = f32[1048,2096]{1,0:T(8,128)} fusion(f32[1048,2096]{1,0:T(8,128)} %convolution_subtract_fusion, f32[1048,262]{1,0:T(8,128)S(1)} %fusion.31, f32[262,2096]{1,0:T(8,128)} %all-reduce.14.cloned.1.call-done), kind=kOutput, calls=%fused_computation.10 | convolution fusion | flops 6908332032 | bytes 20867776 | tf_op jit(solution)/shard_map/dot_general | solution.py:53
  (19 shorter events, 0.1 us)
Async XLA Ops:
  6.5 3.9 copy-start.1
  6.5 3.8 copy-start.6
  6.5 75.5 %all-reduce.6.cloned.1.call-start = ((), (), s32[]{:S(2)}) async-start(), calls=%async_computation | async-start | bytes 131072 | tf_op jit(solution)/shard_map/psum | solution.py:75
  10.2 157.1 %all-reduce.8.cloned.1.call-start = ((), (), s32[]{:S(2)}) async-start(), calls=%async_computation.1 | async-start | bytes 3219456 | tf_op jit(solution)/shard_map/psum | solution.py:10
  10.4 6.2 %copy-start = (s32[8384]{0:T(1024)S(1)}, s32[8384]{0:T(1024)}, u32[]{:S(2)}) copy-start(s32[8384]{0:T(1024)} %constant.58.clone2.2) | copy-start | bytes 100612
  109.1 6.0 %copy-start.4 = (f32[1048,512]{1,0:T(8,128)S(1)}, f32[1048,512]{1,0:T(8,128)}, u32[]{:S(2)}) copy-start(f32[1048,512]{1,0:T(8,128)} %gather_fusion.1) | copy-start | bytes 6438916
  118.5 3.6 copy-start.2
  123.4 155.6 %all-reduce.10.cloned.1.call-start = ((), (), s32[]{:S(2)}) async-start(), calls=%async_computation.2 | async-start | bytes 4595712 | tf_op jit(solution)/shard_map/psum | solution.py:10
  126.7 1.1 copy-start.5
  126.7 202.1 %all-reduce.12.cloned.1.call-start = ((), (), s32[]{:S(2)}) async-start(), calls=%async_computation.3 | async-start | bytes 3219456 | tf_op jit(solution)/shard_map/psum | solution.py:10
  279.0 6.9 %copy-start.3 = (f32[262,2096]{1,0:T(8,128)S(1)}, f32[262,2096]{1,0:T(8,128)}, u32[]{:S(2)}) copy-start(f32[262,2096]{1,0:T(8,128)} %all-reduce.10.cloned.1.call-done) | copy-start | bytes 6589828
  285.9 154.5 %all-reduce.14.cloned.1.call-start = ((), (), s32[]{:S(2)}) async-start(), calls=%async_computation.4 | async-start | bytes 4595712 | tf_op jit(solution)/shard_map/psum | solution.py:10
Sparse Core Ops, SparseCore 0:
  10.8 71.1 all-reduce.5
  123.5 43.7 all-reduce.7
  171.4 107.5 all-reduce.9
  286.0 42.8 all-reduce.11
  332.8 107.5 all-reduce.13
where the time goes:
time: 467 us
  waiting for transfers between devices  303 us (65%)
  matrix products  70 us (15%)
  local copies, waits for them, and re-layouts  63 us (13%)
  between operations  13.4 us (3%)
  other arithmetic  11 us (2%)
  blocking collectives  5.98 us (1%)
    psum x4, waiting for transfers between devices, from_root(): return lax.psum(block, axis)  268 us
    dot_general x6, matrix products, highest(): jnp.dot(left_mat, right_mat, precision=lax.Precision.HIGHEST, preferred_e...  62.9 us
    psum x1, waiting for transfers between devices, per_device(): lax.psum(lax.dot_general(window, scaled_basis, (((0,), (0,)), ((), ())),...  35.2 us
    gather x2, local copies, waits for them, and re-layouts, selectors(): trailing = jnp.take(jnp.asarray(latter), chosen)  17.6 us
    gather x2, local copies, waits for them, and re-layouts, selectors(): leading = jnp.take(jnp.asarray(former), chosen)  17.6 us
    gather x2, local copies, waits for them, and re-layouts, make_features(): jnp.take(window, lead_index, axis=1) * lead_keep[None, :]  11.1 us
    gather x2, local copies, waits for them, and re-layouts, make_features(): jnp.take(window, trail_index, axis=1) * trail_keep[None, :]  10 us
  transfers between devices with their start and end apart: 5, of which 5 were waited for; matrix products, arithmetic and copies ran while one was open for 17% of the time, Pallas kernels for 0%

commit v1 on v0

v1 whole, which is shorter than its diff:
```python
import functools

import jax
import jax.numpy as jnp
from jax import lax
from jax.experimental import pallas as pl
from jax.experimental.pallas import tpu as pltpu
from jax.sharding import PartitionSpec as P

F32 = jnp.float32
BF16 = jnp.bfloat16
LANES = 128
VMEM_LIMIT = 56 * 1024 * 1024


def round_up(size, multiple):
    return -(-size // multiple) * multiple


def mm(left, right):
    return lax.dot_general(left, right, (((1,), (0,)), ((), ())), preferred_element_type=F32)


def mm_nt(left, right):
    return lax.dot_general(left, right, (((1,), (1,)), ((), ())), preferred_element_type=F32)


def mm_tn(left, right):
    return lax.dot_general(left, right, (((0,), (0,)), ((), ())), preferred_element_type=F32)


def project_kernel(codes_ref, scale_ref, basis_ref, out_ref):
    @pl.when(pl.program_id(0) == 0)
    def _():
        out_ref[...] = jnp.zeros_like(out_ref)

    modes = basis_ref[...].astype(F32).T * scale_ref[...]
    out_ref[...] += mm(modes.astype(BF16), codes_ref[...].astype(F32).astype(BF16))


def project(codes, node_scale, basis):
    nodes, snaps = codes.shape
    rank = basis.shape[1]
    block = 1024 if nodes % 1024 == 0 else nodes
    return pl.pallas_call(
        project_kernel,
        grid=(nodes // block,),
        in_specs=[
            pl.BlockSpec((block, snaps), lambda i: (i, 0)),
            pl.BlockSpec((1, block), lambda i: (0, i)),
            pl.BlockSpec((block, rank), lambda i: (i, 0)),
        ],
        out_specs=pl.BlockSpec((rank, snaps), lambda i: (0, 0)),
        out_shape=jax.ShapeDtypeStruct((rank, snaps), F32),
        name="project",
    )(codes, node_scale.reshape(1, nodes), basis)


def starts(index, rank):
    return (index * (2 * rank + 3 - index)) // 2


def decode(order, rank):
    modes = lax.broadcasted_iota(jnp.int32, (rank, order.shape[1]), 0)
    first = starts(modes, rank)
    reached = first <= order
    leading = jnp.sum(reached.astype(jnp.int32), axis=0, keepdims=True) - 1
    trailing = order - jnp.max(jnp.where(reached, first - modes, 0), axis=0, keepdims=True)
    return leading, jnp.where(order < 0, -1, trailing)


def prepare_kernel(rank, rows_ref, cols_ref, diag_ref, lead_r, trail_r, one_r, lead_c, trail_c, one_c, diag_col):
    def column(row):
        return jnp.broadcast_to(row, (LANES, row.shape[1])).T

    count = rows_ref.shape[1]
    leading, trailing = decode(rows_ref[...], rank)
    leading, trailing = column(leading.astype(F32)), column(trailing.astype(F32))
    lane = lax.broadcasted_iota(jnp.int32, (count, LANES), 1).astype(F32)
    lead_r[...] = (leading == lane).astype(F32).astype(BF16)
    trail_r[...] = (trailing == lane).astype(F32).astype(BF16)
    one_r[...] = (trailing == float(rank)).astype(F32)
    leading, trailing = decode(cols_ref[...], rank)
    mode = lax.broadcasted_iota(jnp.int32, (rank, cols_ref.shape[1]), 0)
    lead_c[...] = (leading == mode).astype(F32).astype(BF16)
    trail_c[...] = (trailing == mode).astype(F32).astype(BF16)
    one_c[...] = (trailing == rank).astype(F32)
    diag_col[...] = column(diag_ref[...])


def prepare(order_rows, order_cols, diag_panel, rank):
    rows, cols, diag = order_rows.shape[1], order_cols.shape[1], diag_panel.shape[1]
    return pl.pallas_call(
        functools.partial(prepare_kernel, rank),
        out_shape=[
            jax.ShapeDtypeStruct((rows, rank), BF16),
            jax.ShapeDtypeStruct((rows, rank), BF16),
            jax.ShapeDtypeStruct((rows, LANES), F32),
            jax.ShapeDtypeStruct((rank, cols), BF16),
            jax.ShapeDtypeStruct((rank, cols), BF16),
            jax.ShapeDtypeStruct((1, cols), F32),
            jax.ShapeDtypeStruct((diag, LANES), F32),
        ],
        compiler_params=pltpu.CompilerParams(vmem_limit_bytes=VMEM_LIMIT),
        cost_estimate=pl.CostEstimate(flops=6_000_000, bytes_accessed=4_000_000, transcendentals=0),
        name="prepare",
    )(order_rows, order_cols, diag_panel)


def split(values):
    upper = values.astype(BF16)
    return upper, (values - upper.astype(F32)).astype(BF16)


def eliminate_kernel(size, *refs):
    parts, refs = refs[: size.parts], refs[size.parts :]
    (where, lead_r, trail_r, one_r, lead_c, trail_c, one_c, diag_col, inverse, diag_panel, diag_cols) = refs[:11]
    (out_ref, modes2, modes2_t, feats_p, feats_r, weights, scaled, scaled16, schur_q) = refs[11:]
    step = pl.program_id(0)
    snaps, block = size.snaps, size.block
    inv_snaps = 1.0 / size.snaps

    def row_features(start, count):
        lead = lead_r[pl.ds(start, count), :]
        trail = trail_r[pl.ds(start, count), :]
        one = one_r[pl.ds(start, count), :]
        both = modes2_t[...]
        former = mm(jnp.concatenate([lead, lead], axis=1), both)
        latter = mm(jnp.concatenate([trail, trail], axis=1), both)
        return (former * (latter + jnp.concatenate([one] * (snaps // LANES), axis=1))).astype(BF16)

    @pl.when(step == 0)
    def _():
        modes_t = jnp.concatenate([part[...] for part in parts], axis=1)
        modes2_t[...] = jnp.concatenate(split(modes_t), axis=0)
        modes2[...] = jnp.concatenate(split(modes_t.T), axis=1)
        pad, chunk = size.panel_pad, size.chunk
        for start in range(0, 2 * pad, pad):
            feats_p[pl.ds(start, pad), :] = row_features(size.rows_pad + start, pad)
        first, second = feats_p[pl.ds(0, pad), :], feats_p[pl.ds(pad, pad), :]
        inv0, inv1 = inverse[0], inverse[1]
        inv0_16, inv1_16 = inv0.astype(BF16), inv1.astype(BF16)
        cross = (mm_nt(first, second) * inv_snaps).astype(BF16)
        coupling = mm(inv0_16, cross).astype(BF16)
        q01 = -mm(coupling, inv1_16)
        q10 = -mm_nt(inv1_16, coupling)
        q00 = inv0 - mm_nt(q01.astype(BF16), coupling)
        top = mm(q00.astype(BF16), first) + mm(q01.astype(BF16), second)
        bottom = mm(q10.astype(BF16), first) + mm(inv1_16, second)
        joint = size.panel_width // LANES * LANES
        over = pad - joint

        def pack(upper, lower, axis):
            lead_part = lax.slice_in_dim(upper, 0, joint, axis=axis)
            shared = lax.slice_in_dim(upper, joint, pad, axis=axis) + lax.slice_in_dim(lower, 0, over, axis=axis)
            tail = lax.slice_in_dim(lower, over, pad, axis=axis)
            return jnp.concatenate([lead_part, shared, tail], axis=axis)

        packed = pack(top, bottom, 0) * inv_snaps
        scaled[...] = packed
        scaled16[...] = jnp.zeros_like(scaled16)
        scaled16[pl.ds(0, size.packed), :] = packed.astype(BF16)
        schur_q[...] = jnp.zeros_like(schur_q)
        schur_q[:, pl.ds(0, size.packed)] = pack(pack(q00, q01, 1), pack(q10, inv1, 1), 0)
        spread = mm_tn(feats_p[...], jnp.concatenate([top, bottom], axis=0).astype(BF16))
        spread = (spread * inv_snaps).astype(BF16)
        for start in range(0, size.rows_feats, chunk):
            feats = row_features(start, chunk)
            feats_r[pl.ds(start, chunk), :] = feats
            weight = (feats.astype(F32) - mm(feats, spread)) * inv_snaps
            inside = min(chunk, size.packed - start)
            if inside > 0:
                own = scaled[pl.ds(start, inside), :]
                diag = jnp.concatenate([diag_col[pl.ds(start, inside), :]] * (snaps // LANES), axis=1)
                own = own * diag
                if inside < chunk:
                    own = jnp.concatenate([own, jnp.zeros((chunk - inside, snaps), F32)], axis=0)
                weight = weight - own
            weights[pl.ds(start, chunk), :] = weight.astype(BF16)

    lead, trail, both = lead_c[...], trail_c[...], modes2[...]
    former = mm(both, jnp.concatenate([lead, lead], axis=0))
    latter = mm(both, jnp.concatenate([trail, trail], axis=0)) + one_c[...]
    feats_c = (former * latter).astype(BF16)
    rows = size.rows
    product = mm(weights[...], feats_c)[:rows]
    row_id = lax.broadcasted_iota(jnp.int32, (rows, block), 0) + where[0]
    col_id = lax.broadcasted_iota(jnp.int32, (rows, block), 1) + (where[1] + step * block)
    out_ref[...] = jnp.where(row_id == col_id, product + diag_cols[...], product)

    @pl.when((where[1] == 0) & (step * block < size.panel_total))
    def _():
        at = pl.multiple_of(step * block, block)
        diag = diag_panel[:, pl.ds(at, block)]
        left = mm_nt(feats_r[...], scaled16[pl.ds(at, block), :])[:rows]
        out_ref[...] -= left * diag
        inside = min(rows, size.packed)
        own = jnp.concatenate([diag_col[pl.ds(0, inside), :]] * (block // LANES), axis=1)
        out_ref[pl.ds(0, inside), :] -= own * schur_q[pl.ds(0, inside), pl.ds(at, block)] * diag


class Sizes:
    def __init__(self, **entries):
        self.__dict__.update(entries)


def eliminate(size, parts, where, tables, inverse, diag_panel, diag_cols):
    rank, snaps, block = size.rank, size.snaps, size.block
    whole = pl.BlockSpec(memory_space=pltpu.VMEM)
    lead_r, trail_r, one_r, lead_c, trail_c, one_c, diag_col = tables
    column = lambda height: pl.BlockSpec((height, block), lambda i: (0, i))
    packed_cols = round_up(size.packed, block)
    return pl.pallas_call(
        functools.partial(eliminate_kernel, size),
        grid=(size.cols_pad // block,),
        in_specs=[whole] * size.parts
        + [pl.BlockSpec(memory_space=pltpu.SMEM)]
        + [whole] * 3
        + [column(rank), column(rank), column(1)]
        + [whole] * 3
        + [column(1)],
        out_specs=column(size.rows),
        out_shape=jax.ShapeDtypeStruct((size.rows, size.cols), F32),
        scratch_shapes=[
            pltpu.VMEM((snaps, 2 * rank), BF16),
            pltpu.VMEM((2 * rank, snaps), BF16),
            pltpu.VMEM((2 * size.panel_pad, snaps), BF16),
            pltpu.VMEM((size.rows_feats, snaps), BF16),
            pltpu.VMEM((size.rows_feats, snaps), BF16),
            pltpu.VMEM((size.packed, snaps), F32),
            pltpu.VMEM((packed_cols, snaps), BF16),
            pltpu.VMEM((size.packed, packed_cols), F32),
        ],
        compiler_params=pltpu.CompilerParams(vmem_limit_bytes=VMEM_LIMIT),
        name="eliminate",
    )(*parts, where, lead_r, trail_r, one_r, lead_c, trail_c, one_c, diag_col, inverse, diag_panel, diag_cols)


def partner(values, axis, distance):
    count = lax.axis_size(axis)
    return lax.ppermute(values, axis, [(i, i ^ distance) for i in range(count)])


def distances(axis):
    count = lax.axis_size(axis)
    assert count & (count - 1) == 0
    return [1 << bit for bit in range(count.bit_length() - 1)]


def per_device(codes, node_scale, basis, regular, feature_order, panel_inverse):
    rank = basis.shape[1]
    count = regular.shape[0]
    rows, cols = count // lax.axis_size("node"), count // lax.axis_size("tm")
    snaps = codes.shape[1] * lax.axis_size("tm")
    panels, width = panel_inverse.shape[:2]
    assert panels == 2 and panels * width <= min(rows, cols) and rank == LANES
    shift = width % LANES
    panel_pad = round_up(width + shift, LANES)
    block = 256
    size = Sizes(
        rank=rank,
        snaps=snaps,
        rows=rows,
        cols=cols,
        block=block,
        parts=lax.axis_size("tm"),
        panel_width=width,
        panel_pad=panel_pad,
        panel_total=panels * width,
        packed=width // LANES * LANES + panel_pad,
        rows_pad=round_up(rows, LANES),
        cols_pad=round_up(cols, block),
        chunk=176,
    )
    size.rows_feats = round_up(rows, size.chunk)
    row_offset = lax.axis_index("node") * rows
    col_offset = lax.axis_index("tm") * cols

    total = project(codes, node_scale, basis)

    def window(values, offset, length, padded, fill):
        taken = lax.dynamic_slice_in_dim(values, offset, length)
        return jnp.pad(taken, (0, padded - length), constant_values=fill)

    def panel_positions(values, fill):
        return [
            jnp.pad(values[:width], (0, panel_pad - width), constant_values=fill),
            jnp.pad(values[width : 2 * width], (shift, panel_pad - width - shift), constant_values=fill),
        ]

    order_rows = jnp.concatenate(
        [window(feature_order, row_offset, rows, size.rows_pad, -1)] + panel_positions(feature_order, -1)
    )
    order_cols = window(feature_order, col_offset, cols, size.cols_pad, -1)
    diag_cols = window(regular, col_offset, cols, size.cols_pad, 0)
    packed_cols = round_up(size.packed, block)
    diag_panel = jnp.pad(regular[: size.panel_total], (0, packed_cols - size.panel_total))
    diag_own = diag_panel[: size.packed] * (row_offset == 0).astype(F32)
    gaps = [(0, panel_pad - width)], [(shift, panel_pad - width - shift)]
    inverse = jnp.stack([jnp.pad(panel_inverse[k], gaps[k] * 2) for k in range(2)])
    where = jnp.stack([row_offset, col_offset]).astype(jnp.int32)
    tables = prepare(order_rows[None], order_cols[None], diag_own[None], rank)

    for distance in distances("node"):
        total = total + partner(total, "node", distance)
    parts = [total]
    for distance in reversed(distances("tm")):
        parts = parts + [partner(part, "tm", distance) for part in parts]
    return eliminate(size, parts, where, tables, inverse, diag_panel[None], diag_cols[None])


def solution(mesh):
    placed = (P("node", "tm"), P("node"), P("node", None), P(), P(), P())
    return jax.shard_map(per_device, mesh=mesh, in_specs=placed, out_specs=P("node", "tm"), check_vma=False)
```

time: 467 us -> 47.1 us (0.10)
  waiting for transfers between devices: 303 us -> 3.29 us
  matrix products: 70 us -> 0 us
  local copies, waits for them, and re-layouts: 63 us -> 5.55 us
  Pallas kernels: 0 us -> 24.4 us
  between operations: 13.4 us -> 0.11 us
  starting transfers between devices: 0.35 us -> 10.4 us
  other arithmetic: 11 us -> 2.58 us
  blocking collectives: 5.98 us -> 0 us
    psum x5 -> x0, waiting for transfers between devices: 303 us -> none  [the longest x4 268 us: from_root(): return lax.psum(block, axis)]
    dot_general x8 -> x0, matrix products: 70 us -> none  [the longest x6 62.9 us: highest(): jnp.dot(left_mat, right_mat, precision=lax.Precision.HIGHEST, preferred_e...]
    gather x8 -> x0, local copies, waits for them, and re-layouts: 56.3 us -> none  [the longest x2 17.6 us: selectors(): trailing = jnp.take(jnp.asarray(latter), chosen)]
    pallas_call x0 -> x3, Pallas kernels: none -> 24.4 us  [the longest x1 17 us: eliminate(): pl.pallas_call(functools.partial(eliminate_kernel, size), grid=(size.cols...]
    ppermute x0 -> x6, starting transfers between devices: none -> 10.4 us  [partner(): return lax.ppermute(values, axis, [(i, i ^ distance) for i in range(count)])]
    dot_general x1 -> x0, other arithmetic: 5.99 us -> none  [contract(): lax.dot_general(left_feats, right_feats, (((0,), (0,)), ((), ())), prefer...]
    all_gather x1 -> x0, blocking collectives: 5.98 us -> none  [per_device(): portion = lax.all_gather(summed, 'tm', axis=0, tiled=True)]
    select_n x4 -> x0, other arithmetic: 4.68 us -> none  [the longest x2 4.51 us: from_root(): jnp.where(lax.axis_index(axis) == source, block, jnp.zeros_like(block))]
  transfers between devices with their start and end apart: 5 -> 6, of which waited for: 5 -> 4; matrix products, arithmetic and copies ran while one was open for 17% -> 16% of each run, Pallas kernels for 0% -> 7%
where the time goes in v1:
time: 47.1 us; the launch traced here: 46.3 us
  Pallas kernels  24.4 us (52%)
  starting transfers between devices  10.4 us (22%)
  local copies, waits for them, and re-layouts  5.55 us (12%)
  waiting for transfers between devices  3.29 us (7%)
  other arithmetic  2.58 us (5%)
    pallas_call x1, Pallas kernels, eliminate(): pl.pallas_call(functools.partial(eliminate_kernel, size), grid=(size.cols...  17 us
    ppermute x6, starting transfers between devices, partner(): return lax.ppermute(values, axis, [(i, i ^ distance) for i in range(count)])  10.4 us
    pallas_call x1, Pallas kernels, project(): pl.pallas_call(project_kernel, grid=(nodes // block,), in_specs=[pl.Block...  3.91 us
    pallas_call x1, Pallas kernels, prepare(): pl.pallas_call(functools.partial(prepare_kernel, rank), out_shape=[jax.Sh...  3.47 us
    ppermute x6, waiting for transfers between devices, partner(): return lax.ppermute(values, axis, [(i, i ^ distance) for i in range(count)])  3.29 us
    broadcast_in_dim x3, local copies, waits for them, and re-layouts, per_device(): tables = prepare(order_rows[None], order_cols[None], diag_own[None], rank)  1.81 us
    another operation x1, other arithmetic, per_device(): jnp.stack([jnp.pad(panel_inverse[k], gaps[k] * 2) for k in range(2)])  1.12 us
    dynamic_slice x3, local copies, waits for them, and re-layouts, window(): taken = lax.dynamic_slice_in_dim(values, offset, length)  0.94 us
  transfers between devices with their start and end apart: 6, of which 4 were waited for; matrix products, arithmetic and copies ran while one was open for 16% of the time, Pallas kernels for 7%

profile of v1, /device:TPU:0, one launch (start us, length us, event | category | flops | bytes accessed | tf_op | source)
XLA Modules:
  0.0 46.3 jit_solution(8868554130680707031)
XLA Ops:
  0.0 0.0 copy-start
  0.0 3.9 %project.1 = f32[128,128]{1,0:T(8,128)} custom-call(s32[4096,128]{1,0:T(8,128)} %codes_ref.1, f32[1,4096]{1,0:T(1,128)} %bitcast.11, bf16[4096,128]{1,0:T(8,128)(2,1)} %basis_ref.1), custom_call_target="tpu_custom_call" | custom-call | tf_op jit(solution)/shard_map/project/pallas_call | solution.py:45
  3.9 0.0 copy-start.6
  3.9 0.0 copy-start.8
  3.9 0.0 copy-start.7
  3.9 3.0 %collective-permute-start = (f32[128,128]{1,0:T(8,128)}, f32[128,128]{1,0:T(8,128)S(1)}, u32[]{:S(2)}, u32[]{:S(2)}) collective-permute-start(f32[128,128]{1,0:T(8,128)} %project.1), channel_id=1, source_target_pairs={{0,4},{4,0},{8,12},{12,8},{16,20},{20,16},{24,28},{28,24},{1,5},{5... | collective-permute-start | bytes 196616 | tf_op jit(solution)/shard_map/ppermute | solution.py:241
  6.9 0.0 copy-done
  6.9 0.6 %fusion = (f32[1,262,262]{2,0,1:T(1,128)S(1)}, f32[1,262,262]{2,0,1:T(1,128)S(1)}) fusion(f32[2,262,262]{2,0,1:T(2,128)S(1)} %copy-done), kind=kLoop, calls=%fused_computation.13 | loop fusion | bytes 1098304 | tf_op jit(solution)/shard_map/slice | solution.py:300
  7.5 0.0 copy-done.6
  7.6 0.0 copy-done.8
  7.6 0.0 copy-done.7
  7.6 0.7 %slice_select_fusion = f32[768]{0:T(1024)S(1)} fusion(pred[768]{0:T(1024)(128)(4,1)S(1)} %copy-done.7, f32[8384]{0:T(1024)} %param.9), kind=kLoop, calls=%fused_computation.10 | loop fusion | flops 768 | bytes 6912 | tf_op jit(solution)/shard_map/jit(_pad)/pad | solution.py:297
  8.3 0.0 copy-start.2
  8.3 0.1 copy_bitcast_fusion
  8.3 0.2 pad_bitcast_fusion
  8.5 0.8 %collective-permute-done = f32[128,128]{1,0:T(8,128)S(1)} collective-permute-done((f32[128,128]{1,0:T(8,128)}, f32[128,128]{1,0:T(8,128)S(1)}, u32[]{:S(2)}, u32[]{:S(2)}) %collective-permute-start) | collective-permute-done | bytes 65568 | tf_op jit(solution)/shard_map/ppermute | solution.py:241
  9.4 0.0 copy-done.2
  9.4 2.2 %collective-permute-start.1 = (f32[128,128]{1,0:T(8,128)S(1)}, f32[128,128]{1,0:T(8,128)S(1)}, u32[]{:S(2)}, u32[]{:S(2)}) collective-permute-start(f32[128,128]{1,0:T(8,128)S(1)} %add.28), channel_id=1, source_target_pairs={{0,8},{4,12},{8,0},{12,4},{16,24},{20,28},{24,16},{28,20},{1,9},{5... | collective-permute-start | bytes 196616 | tf_op jit(solution)/shard_map/ppermute | solution.py:241
  11.6 2.2 %collective-permute-done.1 = f32[128,128]{1,0:T(8,128)S(1)} collective-permute-done((f32[128,128]{1,0:T(8,128)S(1)}, f32[128,128]{1,0:T(8,128)S(1)}, u32[]{:S(2)}, u32[]{:S(2)}) %collective-permute-start.1) | collective-permute-done | bytes 65568 | tf_op jit(solution)/shard_map/ppermute | solution.py:241
  13.8 3.1 %collective-permute-start.2 = (f32[128,128]{1,0:T(8,128)S(1)}, f32[128,128]{1,0:T(8,128)S(1)}, u32[]{:S(2)}, u32[]{:S(2)}) collective-permute-start(f32[128,128]{1,0:T(8,128)S(1)} %add.29), channel_id=1, source_target_pairs={{0,16},{4,20},{8,24},{12,28},{16,0},{20,4},{24,8},{28,12},{1,17},{... | collective-permute-start | bytes 196616 | tf_op jit(solution)/shard_map/ppermute | solution.py:241
  16.9 1.1 %pad_maximum_fusion.refs_12_ = f32[2,384,384]{2,1,0:T(8,128)} fusion(f32[1,384,384]{2,1,0:T(8,128)S(1)} %pad_bitcast_fusion, f32[1,384,384]{2,1,0:T(8,128)S(1)} %pad_bitcast_fusion.1), kind=kLoop, calls=%fused_computation | loop fusion | flops 294912 | bytes 2359296 | tf_op jit(solution)/shard_map/stack | solution.py:300
  18.0 0.1 slice.21
  18.1 0.6 %broadcast_in_dim.18.refs_13_ = f32[1,768]{1,0:T(1,128)} reshape(f32[768]{0:T(1024)S(1)} %slice_select_fusion) | data formatting | bytes 6144 | tf_op jit(solution)/shard_map/broadcast_in_dim | solution.py:309
  18.7 0.8 %dynamic_slice.11 = f32[2096]{0:T(1024)S(1)} dynamic-slice(f32[8384]{0:T(1024)} %param.9, s32[]{:T(128)S(6)} %select_n.8), dynamic_slice_sizes={2096} | dynamic-slice | bytes 16772 | tf_op jit(solution)/shard_map/dynamic_slice | solution.py:282
  19.5 0.1 dynamic_slice.10
  19.6 0.6 %broadcast_in_dim.17.diag_ref = f32[1,640]{1,0:T(1,128)} reshape(f32[640]{0:T(1024)S(1)} %slice_multiply_fusion) | data formatting | bytes 5120 | tf_op jit(solution)/shard_map/broadcast_in_dim | solution.py:302
  20.1 0.1 dynamic_slice.9
  20.2 0.0 collective-permute-done.2
  20.2 0.0 copy-start.1
  20.3 1.6 %collective-permute-start.3 = (f32[128,128]{1,0:T(8,128)S(1)}, f32[128,128]{1,0:T(8,128)S(1)}, u32[]{:S(2)}, u32[]{:S(2)}) collective-permute-start(f32[128,128]{1,0:T(8,128)S(1)} %add.30.refs_0_), channel_id=1, source_target_pairs={{0,2},{1,3},{2,0},{3,1},{4,6},{5,7},{6,4},{7,5},{8,10},{9,11},{10,... | collective-permute-start | bytes 196616 | tf_op jit(solution)/shard_map/ppermute | solution.py:241
  21.8 0.1 select_add_fusion
  21.9 0.6 %broadcast_in_dim.15.rows_ref = s32[1,1920]{1,0:T(1,128)} reshape(s32[1920]{0:T(1024)S(1)} %select_add_fusion) | data formatting | bytes 15360 | tf_op jit(solution)/shard_map/broadcast_in_dim | solution.py:302
  22.5 0.6 %broadcast_in_dim.19.refs_14_ = f32[1,2304]{1,0:T(1,128)} reshape(f32[2304]{0:T(1024)S(1)} %pad.39) | data formatting | bytes 18432 | tf_op jit(solution)/shard_map/broadcast_in_dim | solution.py:309
  23.1 0.6 %broadcast_in_dim.16.cols_ref = s32[1,2304]{1,0:T(1,128)} reshape(s32[2304]{0:T(1024)S(1)} %pad.35) | data formatting | bytes 18432 | tf_op jit(solution)/shard_map/broadcast_in_dim | solution.py:302
  23.7 3.5 %prepare.1 = (bf16[1920,128]{1,0:T(8,128)(2,1)}, bf16[1920,128]{1,0:T(8,128)(2,1)}, f32[1920,128]{1,0:T(8,128)}, bf16[128,2304]{1,0:T(8,128)(2,1)}, bf16[128,230...) custom-call(s32[1,1920]{1,0:T(1,128)} %broadcast_in_dim.15.rows_ref, s32[1,2304]{1,0:T(1,128)} %broadcast_in_dim.16.cols_ref, ...), custom_call_target="tpu_custom_call" | custom-call | flops 6000000 | bytes 4000000 | tf_op jit(solution)/shard_map/prepare/pallas_call | solution.py:93
  27.2 0.0 collective-permute-start.4
  27.2 0.0 collective-permute-done.3.refs_1_
  27.2 0.0 copy-start.3
  27.2 0.5 %collective-permute-start.5 = (f32[128,128]{1,0:T(8,128)S(1)}, f32[128,128]{1,0:T(8,128)S(1)}, u32[]{:S(2)}, u32[]{:S(2)}) collective-permute-start(f32[128,128]{1,0:T(8,128)S(1)} %collective-permute-done.3.refs_1_), channel_id=1, source_target_pairs={{0,1},{1,0},{2,3},{3,2},{4,5},{5,4},{6,7},{7,6},{8,9},{9,8},{10,11... | collective-permute-start | bytes 196616 | tf_op jit(solution)/shard_map/ppermute | solution.py:241
  27.7 0.7 %pad_add_fusion.refs_4_ = s32[2]{0:T(128)} fusion(s32[1]{0:T(128)} %bitcast.2, s32[1]{0:T(128)} %bitcast.1), kind=kLoop, calls=%fused_computation.12 | loop fusion | flops 2 | bytes 16 | tf_op jit(solution)/shard_map/stack | solution.py:301
  28.4 0.1 collective-permute-done.4.refs_2_
  28.5 0.0 copy-start.4
  28.5 0.2 collective-permute-done.5.refs_3_
  28.6 0.0 copy-done.1
  28.6 0.0 copy-done.3
  28.6 0.4 copy-done.4
  29.1 0.2 copy-done.5
  29.2 17.0 %eliminate.1 = f32[1048,2096]{1,0:T(8,128)} custom-call(f32[128,128]{1,0:T(8,128)} %copy-done.1, f32[128,128]{1,0:T(8,128)} %copy-done.3, f32[128,128]{1,0:T(8,128)} %copy-done.4, f32[128,128]{1,0:T(8,128)} %copy-done.5, s32[2]{0:T(128)} %pad_add_fusion.refs_4_, bf16[1920,128]{1,0:T(8,128)(2,1)} %get-tuple-element.12.refs_5_, ...), custom_call_target="tpu_custom_call" | custom-call | tf_op jit(solution)/shard_map/eliminate/pallas_call | solution.py:213
  (9 shorter events, 0.1 us)
Async XLA Ops:
  0.0 6.9 %copy-start = (f32[2,262,262]{2,0,1:T(2,128)S(1)}, f32[2,262,262]{2,0,1:T(2,128)}, u32[]{:S(2)}) copy-start(f32[2,262,262]{2,0,1:T(2,128)} %param.11) | copy-start | bytes 1647460
  3.9 3.6 %copy-start.6 = (s32[8384]{0:T(1024)S(1)}, s32[8384]{0:T(1024)}, u32[]{:S(2)}) copy-start(s32[8384]{0:T(1024)} %param.10) | copy-start | bytes 100612
  3.9 3.6 %copy-start.8 = (pred[384]{0:T(512)(128)(4,1)S(1)}, pred[384]{0:T(512)(128)(4,1)}, u32[]{:S(2)}) copy-start(pred[384]{0:T(512)(128)(4,1)} %constant.22.clone.1) | copy-start | bytes 1156
  3.9 3.7 %copy-start.7 = (pred[768]{0:T(1024)(128)(4,1)S(1)}, pred[768]{0:T(1024)(128)(4,1)}, u32[]{:S(2)}) copy-start(pred[768]{0:T(1024)(128)(4,1)} %constant.23.clone.1) | copy-start | bytes 2308
  3.9 5.5 %collective-permute-start = (f32[128,128]{1,0:T(8,128)}, f32[128,128]{1,0:T(8,128)S(1)}, u32[]{:S(2)}, u32[]{:S(2)}) collective-permute-start(f32[128,128]{1,0:T(8,128)} %project.1), channel_id=1, source_target_pairs={{0,4},{4,0},{8,12},{12,8},{16,20},{20,16},{24,28},{28,24},{1,5},{5... | collective-permute-start | bytes 196616 | tf_op jit(solution)/shard_map/ppermute | solution.py:241
  8.3 1.1 %copy-start.2 = (f32[128,128]{1,0:T(8,128)S(1)}, f32[128,128]{1,0:T(8,128)}, u32[]{:S(2)}) copy-start(f32[128,128]{1,0:T(8,128)} %project.1) | copy-start | bytes 196612
  9.4 4.4 %collective-permute-start.1 = (f32[128,128]{1,0:T(8,128)S(1)}, f32[128,128]{1,0:T(8,128)S(1)}, u32[]{:S(2)}, u32[]{:S(2)}) collective-permute-start(f32[128,128]{1,0:T(8,128)S(1)} %add.28), channel_id=1, source_target_pairs={{0,8},{4,12},{8,0},{12,4},{16,24},{20,28},{24,16},{28,20},{1,9},{5... | collective-permute-start | bytes 196616 | tf_op jit(solution)/shard_map/ppermute | solution.py:241
  13.8 6.4 %collective-permute-start.2 = (f32[128,128]{1,0:T(8,128)S(1)}, f32[128,128]{1,0:T(8,128)S(1)}, u32[]{:S(2)}, u32[]{:S(2)}) collective-permute-start(f32[128,128]{1,0:T(8,128)S(1)} %add.29), channel_id=1, source_target_pairs={{0,16},{4,20},{8,24},{12,28},{16,0},{20,4},{24,8},{28,12},{1,17},{... | collective-permute-start | bytes 196616 | tf_op jit(solution)/shard_map/ppermute | solution.py:241
  20.2 8.4 %copy-start.1 = (f32[128,128]{1,0:T(8,128)}, f32[128,128]{1,0:T(8,128)S(1)}, u32[]{:S(2)}) copy-start(f32[128,128]{1,0:T(8,128)S(1)} %add.30.refs_0_) | copy-start | bytes 196612
  20.3 7.0 %collective-permute-start.3 = (f32[128,128]{1,0:T(8,128)S(1)}, f32[128,128]{1,0:T(8,128)S(1)}, u32[]{:S(2)}, u32[]{:S(2)}) collective-permute-start(f32[128,128]{1,0:T(8,128)S(1)} %add.30.refs_0_), channel_id=1, source_target_pairs={{0,2},{1,3},{2,0},{3,1},{4,6},{5,7},{6,4},{7,5},{8,10},{9,11},{10,... | collective-permute-start | bytes 196616 | tf_op jit(solution)/shard_map/ppermute | solution.py:241
  27.2 1.3 %collective-permute-start.4 = (f32[128,128]{1,0:T(8,128)S(1)}, f32[128,128]{1,0:T(8,128)S(1)}, u32[]{:S(2)}, u32[]{:S(2)}) collective-permute-start(f32[128,128]{1,0:T(8,128)S(1)} %add.30.refs_0_), channel_id=1, source_target_pairs={{0,1},{1,0},{2,3},{3,2},{4,5},{5,4},{6,7},{7,6},{8,9},{9,8},{10,11... | collective-permute-start | bytes 196616 | tf_op jit(solution)/shard_map/ppermute | solution.py:241
  27.2 1.4 %copy-start.3 = (f32[128,128]{1,0:T(8,128)}, f32[128,128]{1,0:T(8,128)S(1)}, u32[]{:S(2)}) copy-start(f32[128,128]{1,0:T(8,128)S(1)} %collective-permute-done.3.refs_1_) | copy-start | bytes 196612
  27.2 1.4 %collective-permute-start.5 = (f32[128,128]{1,0:T(8,128)S(1)}, f32[128,128]{1,0:T(8,128)S(1)}, u32[]{:S(2)}, u32[]{:S(2)}) collective-permute-start(f32[128,128]{1,0:T(8,128)S(1)} %collective-permute-done.3.refs_1_), channel_id=1, source_target_pairs={{0,1},{1,0},{2,3},{3,2},{4,5},{5,4},{6,7},{7,6},{8,9},{9,8},{10,11... | collective-permute-start | bytes 196616 | tf_op jit(solution)/shard_map/ppermute | solution.py:241
  28.5 0.6 %copy-start.4 = (f32[128,128]{1,0:T(8,128)}, f32[128,128]{1,0:T(8,128)S(1)}, u32[]{:S(2)}) copy-start(f32[128,128]{1,0:T(8,128)S(1)} %collective-permute-done.4.refs_2_) | copy-start | bytes 196612
  28.6 0.6 %copy-start.5 = (f32[128,128]{1,0:T(8,128)}, f32[128,128]{1,0:T(8,128)S(1)}, u32[]{:S(2)}) copy-start(f32[128,128]{1,0:T(8,128)S(1)} %collective-permute-done.5.refs_3_) | copy-start | bytes 196612

commit v2 on v1

v2 whole, which is shorter than its diff:
```python
import functools

import jax
import jax.numpy as jnp
from jax import lax
from jax.experimental import pallas as pl
from jax.experimental.pallas import tpu as pltpu
from jax.sharding import PartitionSpec as P

F32 = jnp.float32
BF16 = jnp.bfloat16
LANES = 128
VMEM_LIMIT = 32 * 1024 * 1024
PREPARE_VMEM = 16 * 1024 * 1024


def round_up(size, multiple):
    return -(-size // multiple) * multiple


def mm(left, right):
    return lax.dot_general(left, right, (((1,), (0,)), ((), ())), preferred_element_type=F32)


def mm_nt(left, right):
    return lax.dot_general(left, right, (((1,), (1,)), ((), ())), preferred_element_type=F32)


def mm_tn(left, right):
    return lax.dot_general(left, right, (((0,), (0,)), ((), ())), preferred_element_type=F32)


def project_kernel(codes_ref, scale_ref, basis_ref, out_ref):
    @pl.when(pl.program_id(0) == 0)
    def _():
        out_ref[...] = jnp.zeros_like(out_ref)

    modes = basis_ref[...].astype(F32).T * scale_ref[...]
    out_ref[...] += mm(modes.astype(BF16), codes_ref[...].astype(F32).astype(BF16))


def project(codes, node_scale, basis):
    nodes, snaps = codes.shape
    rank = basis.shape[1]
    block = nodes // 2 if nodes % 2048 == 0 else nodes
    return pl.pallas_call(
        project_kernel,
        grid=(nodes // block,),
        in_specs=[
            pl.BlockSpec((block, snaps), lambda i: (i, 0)),
            pl.BlockSpec((1, block), lambda i: (0, i)),
            pl.BlockSpec((block, rank), lambda i: (i, 0)),
        ],
        out_specs=pl.BlockSpec((rank, snaps), lambda i: (0, 0)),
        out_shape=jax.ShapeDtypeStruct((rank, snaps), F32),
        name="project",
    )(codes, node_scale.reshape(1, nodes), basis)


def starts(index, rank):
    return (index * (2 * rank + 3 - index)) // 2


def decode(order, rank):
    modes = lax.broadcasted_iota(jnp.int32, (rank, order.shape[1]), 0)
    first = starts(modes, rank)
    reached = first <= order
    leading = jnp.sum(reached.astype(jnp.int32), axis=0, keepdims=True) - 1
    trailing = order - jnp.max(jnp.where(reached, first - modes, 0), axis=0, keepdims=True)
    return leading, jnp.where(order < 0, -1, trailing)


def prepare_kernel(size, rows_ref, cols_ref, diag_ref, lead_r, trail_r, one_r, lead_c, trail_c, one_c, diag_col):
    def column(row):
        return jnp.broadcast_to(row, (LANES, row.shape[1])).T

    rank, count = size.rank, lead_r.shape[0]
    leading, trailing = decode(rows_ref[:, pl.ds(0, count)], rank)
    leading, trailing = column(leading.astype(F32)), column(trailing.astype(F32))
    lane = lax.broadcasted_iota(jnp.int32, (count, LANES), 1).astype(F32)
    lead_r[...] = (leading == lane).astype(F32).astype(BF16)
    trail_r[...] = (trailing == lane).astype(F32).astype(BF16)
    one_r[...] = (trailing == float(rank)).astype(F32)
    leading, trailing = decode(cols_ref[:, pl.ds(0, size.cols_pad)], rank)
    mode = lax.broadcasted_iota(jnp.int32, (rank, size.cols_pad), 0)
    lead_c[...] = (leading == mode).astype(F32).astype(BF16)
    trail_c[...] = (trailing == mode).astype(F32).astype(BF16)
    one_c[...] = (trailing == rank).astype(F32)
    diag_col[...] = column(diag_ref[:, pl.ds(0, size.packed)])


def prepare(size, order_rows, order_cols, diag_own):
    rank, cols, rows = size.rank, size.cols_pad, size.rows_pad + 2 * size.panel_pad
    return pl.pallas_call(
        functools.partial(prepare_kernel, size),
        out_shape=[
            jax.ShapeDtypeStruct((rows, rank), BF16),
            jax.ShapeDtypeStruct((rows, rank), BF16),
            jax.ShapeDtypeStruct((rows, LANES), F32),
            jax.ShapeDtypeStruct((rank, cols), BF16),
            jax.ShapeDtypeStruct((rank, cols), BF16),
            jax.ShapeDtypeStruct((1, cols), F32),
            jax.ShapeDtypeStruct((size.packed, LANES), F32),
        ],
        compiler_params=pltpu.CompilerParams(vmem_limit_bytes=PREPARE_VMEM),
        cost_estimate=pl.CostEstimate(flops=6_000_000, bytes_accessed=4_000_000, transcendentals=0),
        name="prepare",
    )(order_rows, order_cols, diag_own)


def split(values):
    upper = values.astype(BF16)
    return upper, (values - upper.astype(F32)).astype(BF16)


def eliminate_kernel(size, *refs):
    parts, refs = refs[: size.parts], refs[size.parts :]
    (where, lead_r, trail_r, one_r, lead_c, trail_c, one_c, diag_col, inverse0, inverse1, diag_panel, diag_cols) = refs[:12]
    (out, modes2, modes2_t, feats_p, feats_r, feats_c, weights, panel_w, panel_w16, schur_q, block_sum, sems) = refs[12:]
    snaps, block, rows, cols = size.snaps, size.block, size.rows, size.cols
    pad, chunk = size.panel_pad, size.chunk
    inv_snaps = 1.0 / size.snaps

    modes_t = jnp.concatenate([part[...] for part in parts], axis=1)
    modes2_t[...] = jnp.concatenate(split(modes_t), axis=0)
    modes2[...] = jnp.concatenate(split(modes_t.T), axis=1)

    def row_features(start, count):
        lead = lead_r[pl.ds(start, count), :]
        trail = trail_r[pl.ds(start, count), :]
        one = one_r[pl.ds(start, count), :]
        both = modes2_t[...]
        former = mm(jnp.concatenate([lead, lead], axis=1), both)
        latter = mm(jnp.concatenate([trail, trail], axis=1), both)
        return (former * (latter + jnp.concatenate([one] * (snaps // LANES), axis=1))).astype(BF16)

    def column_features(start, count):
        lead = lead_c[:, pl.ds(start, count)]
        trail = trail_c[:, pl.ds(start, count)]
        both = modes2[...]
        former = mm(both, jnp.concatenate([lead, lead], axis=0))
        latter = mm(both, jnp.concatenate([trail, trail], axis=0)) + one_c[:, pl.ds(start, count)]
        feats_c[:, pl.ds(start, count)] = (former * latter).astype(BF16)

    for start in range(0, 2 * pad, pad):
        feats_p[pl.ds(start, pad), :] = row_features(size.rows_pad + start, pad)
    first, second = feats_p[pl.ds(0, pad), :], feats_p[pl.ds(pad, pad), :]
    inv0, inv1 = inverse0[...], inverse1[...]
    inv0_16, inv1_16 = inv0.astype(BF16), inv1.astype(BF16)
    fillers = [functools.partial(column_features, start, min(block, size.cols_pad - start)) for start in range(0, size.cols_pad, block)]

    def fill():
        if fillers:
            fillers.pop(0)()

    cross = (mm_nt(first, second) * inv_snaps).astype(BF16)
    fill()
    coupling = mm(inv0_16, cross).astype(BF16)
    fill()
    q01 = -mm(coupling, inv1_16)
    q10 = -mm_nt(inv1_16, coupling)
    fill()
    q00 = inv0 - mm_nt(q01.astype(BF16), coupling)
    fill()
    top = mm(q00.astype(BF16), first) + mm(q01.astype(BF16), second)
    bottom = mm(q10.astype(BF16), first) + mm(inv1_16, second)
    while fillers:
        fill()
    joint = size.panel_width // LANES * LANES
    over = pad - joint

    def pack(upper, lower, axis):
        lead_part = lax.slice_in_dim(upper, 0, joint, axis=axis)
        shared = lax.slice_in_dim(upper, joint, pad, axis=axis) + lax.slice_in_dim(lower, 0, over, axis=axis)
        tail = lax.slice_in_dim(lower, over, pad, axis=axis)
        return jnp.concatenate([lead_part, shared, tail], axis=axis)

    packed = pack(top, bottom, 0) * inv_snaps
    panel_w[...] = packed
    panel_w16[pl.ds(0, size.packed), :] = packed.astype(BF16)
    if panel_w16.shape[0] > size.packed:
        panel_w16[pl.ds(size.packed, panel_w16.shape[0] - size.packed), :] = jnp.zeros(
            (panel_w16.shape[0] - size.packed, snaps), BF16
        )
    schur_q[...] = pack(pack(q00, q01, 1), pack(q10, inv1, 1), 0)
    spread = mm_tn(feats_p[...], jnp.concatenate([top, bottom], axis=0).astype(BF16))
    spread = (spread * inv_snaps).astype(BF16)
    for start in range(0, size.rows_feats, chunk):
        feats = row_features(start, chunk)
        feats_r[pl.ds(start, chunk), :] = feats
        weight = (feats.astype(F32) - mm(feats, spread)) * inv_snaps
        inside = min(chunk, size.packed - start)
        if inside > 0:
            own = panel_w[pl.ds(start, inside), :]
            own = own * jnp.concatenate([diag_col[pl.ds(start, inside), :]] * (snaps // LANES), axis=1)
            if inside < chunk:
                own = jnp.concatenate([own, jnp.zeros((chunk - inside, snaps), F32)], axis=0)
            weight = weight - own
        weights[pl.ds(start, chunk), :] = weight.astype(BF16)

    delta = where[0] - where[1]

    def write(first_panel):
        copies = []
        for index, (start, count) in enumerate(size.row_blocks):
            kept = min(count, rows - start)
            at = pl.ds(start, kept)
            full = mm(weights[pl.ds(start, count), :], feats_c[...])[:kept, :cols]
            row_id = lax.broadcasted_iota(jnp.int32, full.shape, 0)
            col_id = lax.broadcasted_iota(jnp.int32, full.shape, 1)
            full = full + jnp.where(col_id - row_id == delta + start, diag_cols[:, pl.ds(0, cols)], 0.0)
            if first_panel:
                used = min(size.packed, cols)
                diag = diag_panel[:, pl.ds(0, used)]
                left = mm_nt(feats_r[pl.ds(start, count), :], panel_w16[...])[:kept, :used]
                inside = min(kept, size.packed - start)
                if inside > 0:
                    own = jnp.concatenate([diag_col[pl.ds(start, inside), :]] * (size.packed // LANES), axis=1)
                    own = (own * schur_q[pl.ds(start, inside), :])[:, :used]
                    if inside < kept:
                        own = jnp.concatenate([own, jnp.zeros((kept - inside, used), F32)], axis=0)
                    left = left + own
                part = full[:, :used] - left * diag
                block_sum[at, pl.ds(0, used)] = part
                if used < cols:
                    block_sum[at, pl.ds(used, cols - used)] = full[:, used:]
            else:
                block_sum[at, :] = full
            copy = pltpu.make_async_copy(block_sum.at[at, :], out.at[at, :], sems.at[index])
            copy.start()
            copies.append(copy)
        for copy in copies:
            copy.wait()

    @pl.when(where[1] == 0)
    def _():
        write(True)

    @pl.when(where[1] != 0)
    def _():
        write(False)


class Sizes:
    def __init__(self, **entries):
        self.__dict__.update(entries)


def eliminate(size, parts, where, tables, inverses, diag_panel, diag_cols):
    rank, snaps, block = size.rank, size.snaps, size.block
    whole = pl.BlockSpec(memory_space=pltpu.VMEM)
    return pl.pallas_call(
        functools.partial(eliminate_kernel, size),
        in_specs=[whole] * size.parts + [pl.BlockSpec(memory_space=pltpu.SMEM)] + [whole] * 11,
        out_specs=pl.BlockSpec(memory_space=pl.ANY),
        out_shape=jax.ShapeDtypeStruct((size.rows, size.cols), F32),
        scratch_shapes=[
            pltpu.VMEM((snaps, 2 * rank), BF16),
            pltpu.VMEM((2 * rank, snaps), BF16),
            pltpu.VMEM((2 * size.panel_pad, snaps), BF16),
            pltpu.VMEM((size.rows_feats, snaps), BF16),
            pltpu.VMEM((snaps, size.cols_pad), BF16),
            pltpu.VMEM((size.rows_feats, snaps), BF16),
            pltpu.VMEM((size.packed, snaps), F32),
            pltpu.VMEM((round_up(size.packed, LANES), snaps), BF16),
            pltpu.VMEM((size.packed, size.packed), F32),
            pltpu.VMEM((size.rows, size.cols), F32),
            pltpu.SemaphoreType.DMA((len(size.row_blocks),)),
        ],
        compiler_params=pltpu.CompilerParams(vmem_limit_bytes=VMEM_LIMIT),
        name="eliminate",
    )(*parts, where, *tables, *inverses, diag_panel, diag_cols)


def partner(values, axis, distance):
    count = lax.axis_size(axis)
    return lax.ppermute(values, axis, [(i, i ^ distance) for i in range(count)])


def distances(axis):
    count = lax.axis_size(axis)
    assert count & (count - 1) == 0
    return [1 << bit for bit in range(count.bit_length() - 1)]


def row_blocks(rows):
    return [(start, min(176, rows - start)) for start in range(0, rows, 176)]


def per_device(codes, node_scale, basis, regular, feature_order, panel_inverse):
    rank = basis.shape[1]
    count = regular.shape[0]
    rows, cols = count // lax.axis_size("node"), count // lax.axis_size("tm")
    snaps = codes.shape[1] * lax.axis_size("tm")
    panels, width = panel_inverse.shape[:2]
    assert panels == 2 and panels * width <= min(rows, cols) and rank == LANES
    shift = width % LANES
    panel_pad = round_up(width + shift, LANES)
    block = 512
    size = Sizes(
        rank=rank,
        snaps=snaps,
        rows=rows,
        cols=cols,
        block=block,
        parts=lax.axis_size("tm"),
        panel_width=width,
        panel_pad=panel_pad,
        panel_total=panels * width,
        packed=width // LANES * LANES + panel_pad,
        rows_pad=round_up(rows, LANES),
        long=1024,
        cols_pad=round_up(cols, 256),
        chunk=176,
    )
    size.rows_feats = round_up(rows, size.chunk)
    size.row_blocks = row_blocks(size.rows_feats)
    row_offset = lax.axis_index("node") * rows
    col_offset = lax.axis_index("tm") * cols

    total = project(codes, node_scale, basis)

    def window(values, offset, length, padded, fill):
        taken = lax.dynamic_slice_in_dim(values, offset, length)
        return jnp.pad(taken, (0, padded - length), constant_values=fill)

    def panel_positions(values, fill):
        return [
            jnp.pad(values[:width], (0, panel_pad - width), constant_values=fill),
            jnp.pad(values[width : 2 * width], (shift, panel_pad - width - shift), constant_values=fill),
        ]

    def long_row(values, fill):
        length = values.shape[0]
        return jnp.pad(values, (0, round_up(length, size.long) - length), constant_values=fill)[None]

    order_rows = long_row(
        jnp.concatenate(
            [window(feature_order, row_offset, rows, size.rows_pad, -1)] + panel_positions(feature_order, -1)
        ),
        -1,
    )
    order_cols = long_row(lax.dynamic_slice_in_dim(feature_order, col_offset, cols), -1)
    diag_cols = long_row(lax.dynamic_slice_in_dim(regular, col_offset, cols), 0)
    diag_panel = long_row(regular[: size.panel_total], 0)
    diag_own = diag_panel * (row_offset == 0).astype(F32)
    gaps = [(0, panel_pad - width)], [(shift, panel_pad - width - shift)]
    inverses = [jnp.pad(panel_inverse[k], gaps[k] * 2) for k in range(2)]
    where = jnp.stack([row_offset, col_offset]).astype(jnp.int32)
    inputs = (order_rows, order_cols, diag_own, diag_panel, diag_cols, inverses, where)
    tables = None
    for turn, distance in enumerate(distances("node")):
        total = total + partner(total, "node", distance)
        if turn == 0:
            total, inputs = lax.optimization_barrier((total, inputs))
            order_rows, order_cols, diag_own, diag_panel, diag_cols, inverses, where = inputs
            tables = prepare(size, order_rows, order_cols, diag_own)
        elif turn == 1:
            total, tables = lax.optimization_barrier((total, tables))
    parts = [total]
    for distance in reversed(distances("tm")):
        parts = parts + [partner(part, "tm", distance) for part in parts]
    return eliminate(size, parts, where, tables, inverses, diag_panel, diag_cols)


def solution(mesh):
    placed = (P("node", "tm"), P("node"), P("node", None), P(), P(), P())
    return jax.shard_map(per_device, mesh=mesh, in_specs=placed, out_specs=P("node", "tm"), check_vma=False)
```

time: 47.1 us -> 41.6 us (0.88)
  Pallas kernels: 24.4 us -> 16.3 us
  waiting for transfers between devices: 3.29 us -> 7.65 us
  starting transfers between devices: 10.4 us -> 8.82 us
    pallas_call x2, Pallas kernels: 20.5 us -> 13.4 us  [the longest x1 11.8 us: eliminate(): pl.pallas_call(functools.partial(eliminate_kernel, size), in_specs=[whole...]
    ppermute x6, waiting for transfers between devices: 3.29 us -> 7.65 us  [partner(): return lax.ppermute(values, axis, [(i, i ^ distance) for i in range(count)])]
    broadcast_in_dim x5 -> x0, local copies, waits for them, and re-layouts: 2.99 us -> none  [the longest x3 1.81 us: per_device(): tables = prepare(order_rows[None], order_cols[None], diag_own[None], rank)]
    dynamic_slice x0 -> x2, local copies, waits for them, and re-layouts: none -> 1.58 us  [the longest x1 0.79 us: per_device(): lax.dynamic_slice_in_dim(feature_order, col_offset, cols)]
    slice x1, local copies, waits for them, and re-layouts: 0.62 us -> 2.17 us  [per_device(): inverses = [jnp.pad(panel_inverse[k], gaps[k] * 2) for k in range(2)]]
    ppermute x6, starting transfers between devices: 10.4 us -> 8.82 us  [partner(): return lax.ppermute(values, axis, [(i, i ^ distance) for i in range(count)])]
    another operation x1 -> x0, other arithmetic: 1.12 us -> none  [per_device(): jnp.stack([jnp.pad(panel_inverse[k], gaps[k] * 2) for k in range(2)])]
    pallas_call x1, Pallas kernels: 3.91 us -> 2.87 us  [project(): pl.pallas_call(project_kernel, grid=(nodes // block,), in_specs=[pl.Block...]
  transfers between devices with their start and end apart: 6 -> 6, of which waited for: 4 -> 4; matrix products, arithmetic and copies ran while one was open for 16% -> 18% of each run, Pallas kernels for 7% -> 4%
where the time goes in v2:
time: 41.6 us; the launch traced here: 41 us
  Pallas kernels  16.3 us (39%)
  starting transfers between devices  8.82 us (21%)
  waiting for transfers between devices  7.65 us (18%)
  local copies, waits for them, and re-layouts  5.62 us (14%)
  other arithmetic  2.44 us (6%)
    pallas_call x1, Pallas kernels, eliminate(): pl.pallas_call(functools.partial(eliminate_kernel, size), in_specs=[whole...  11.8 us
    ppermute x6, starting transfers between devices, partner(): return lax.ppermute(values, axis, [(i, i ^ distance) for i in range(count)])  8.82 us
    ppermute x6, waiting for transfers between devices, partner(): return lax.ppermute(values, axis, [(i, i ^ distance) for i in range(count)])  7.65 us
    pallas_call x1, Pallas kernels, project(): pl.pallas_call(project_kernel, grid=(nodes // block,), in_specs=[pl.Block...  2.87 us
    slice x1, local copies, waits for them, and re-layouts, per_device(): inverses = [jnp.pad(panel_inverse[k], gaps[k] * 2) for k in range(2)]  2.17 us
    pallas_call x1, Pallas kernels, prepare(): pl.pallas_call(functools.partial(prepare_kernel, size), out_shape=[jax.Sh...  1.6 us
    add x3, other arithmetic, per_device(): total = total + partner(total, 'node', distance)  0.87 us
  transfers between devices with their start and end apart: 6, of which 4 were waited for; matrix products, arithmetic and copies ran while one was open for 18% of the time, Pallas kernels for 4%

profile of v2, /device:TPU:0, one launch (start us, length us, event | category | flops | bytes accessed | tf_op | source)
XLA Modules:
  0.0 41.0 jit_solution(5733616805344337436)
XLA Ops:
  0.0 2.9 %project.1 = f32[128,128]{1,0:T(8,128)} custom-call(s32[4096,128]{1,0:T(8,128)} %codes_ref.1, f32[1,4096]{1,0:T(1,128)} %bitcast.17, bf16[4096,128]{1,0:T(8,128)(2,1)} %basis_ref.1), custom_call_target="tpu_custom_call" | custom-call | tf_op jit(solution)/shard_map/project/pallas_call | solution.py:46
  2.9 2.9 %collective-permute-start = (f32[128,128]{1,0:T(8,128)}, f32[128,128]{1,0:T(8,128)S(1)}, u32[]{:S(2)}, u32[]{:S(2)}) collective-permute-start(f32[128,128]{1,0:T(8,128)} %project.1), channel_id=1, source_target_pairs={{0,4},{4,0},{8,12},{12,8},{16,20},{20,16},{24,28},{28,24},{1,5},{5... | collective-permute-start | bytes 196616 | tf_op jit(solution)/shard_map/ppermute | solution.py:277
  5.8 0.8 %slice.18 = s32[262]{0:T(512)S(1)} slice(s32[8384]{0:T(1024)} %param.10), slice={[262:524]} | slice | bytes 2096 | tf_op jit(solution)/shard_map/slice | solution.py:330
  6.6 0.7 %slice_select_fusion.1 = s32[384]{0:T(512)S(1)} fusion(pred[384]{0:T(512)(128)(4,1)} %constant.20.clone.1, s32[8384]{0:T(1024)} %param.10), kind=kLoop, calls=%fused_computation.8 | loop fusion | flops 384 | bytes 3456 | tf_op jit(solution)/shard_map/jit(_pad)/pad | solution.py:329
  7.3 0.8 %dynamic_slice.9 = s32[1048]{0:T(1024)S(1)} dynamic-slice(s32[8384]{0:T(1024)} %param.10, s32[]{:T(128)S(6)} %select_n.7), dynamic_slice_sizes={1048} | dynamic-slice | bytes 8388 | tf_op jit(solution)/shard_map/dynamic_slice | solution.py:324
  8.1 0.8 %dynamic_slice.10 = s32[2096]{0:T(1024)S(1)} dynamic-slice(s32[8384]{0:T(1024)} %param.10, s32[]{:T(128)S(6)} %select_n.8), dynamic_slice_sizes={2096} | dynamic-slice | bytes 16772 | tf_op jit(solution)/shard_map/dynamic_slice | solution.py:343
  8.8 0.8 %dynamic_slice.11 = f32[2096]{0:T(1024)S(1)} dynamic-slice(f32[8384]{0:T(1024)} %param.9, s32[]{:T(128)S(6)} %select_n.8), dynamic_slice_sizes={2096} | dynamic-slice | bytes 16772 | tf_op jit(solution)/shard_map/dynamic_slice | solution.py:344
  9.6 0.1 select_add_fusion
  9.7 2.2 %fusion = (f32[1,262,262]{2,0,1:T(1,128)S(1)}, f32[1,262,262]{2,0,1:T(1,128)S(1)}) fusion(f32[2,262,262]{2,0,1:T(2,128)} %param.11), kind=kLoop, calls=%fused_computation.10 | loop fusion | bytes 1098304 | tf_op jit(solution)/shard_map/slice | solution.py:348
  11.9 0.1 copy_bitcast_fusion
  12.0 0.2 pad.44.refs_13_
  12.2 0.7 %slice_select_fusion = (f32[1024]{0:T(1024)S(1)}, f32[1024]{0:T(1024)S(1)}) fusion(pred[1024]{0:T(1024)(128)(4,1)} %constant.23.clone.1, f32[8384]{0:T(1024)} %param.9, f32[]{:T(128)S(6)} %convert_element_type.11), kind=kLoop, calls=%fused_computation.6 | loop fusion | flops 2048 | bytes 13316 | tf_op jit(solution)/shard_map/jit(_pad)/pad | solution.py:335
  12.9 0.1 pad_add_fusion.refs_4_
  13.0 0.0 collective-permute-done
  13.0 0.8 %add.30 = f32[128,128]{1,0:T(8,128)S(1)} add(f32[128,128]{1,0:T(8,128)} %project.1, f32[128,128]{1,0:T(8,128)S(1)} %collective-permute-done) | non-fusion elementwise | flops 16384 | bytes 196608 | tf_op jit(solution)/shard_map/add | solution.py:353
  13.9 1.6 %collective-permute-start.1 = (f32[128,128]{1,0:T(8,128)S(1)}, f32[128,128]{1,0:T(8,128)S(1)}, u32[]{:S(2)}, u32[]{:S(2)}) collective-permute-start(f32[128,128]{1,0:T(8,128)S(1)} %add.30), channel_id=1, source_target_pairs={{0,8},{4,12},{8,0},{12,4},{16,24},{20,28},{24,16},{28,20},{1,9},{5... | collective-permute-start | bytes 196616 | tf_op jit(solution)/shard_map/ppermute | solution.py:277
  15.5 1.6 %prepare.1 = (bf16[1920,128]{1,0:T(8,128)(2,1)S(1)}, bf16[1920,128]{1,0:T(8,128)(2,1)S(1)}, f32[1920,128]{1,0:T(8,128)S(1)}, bf16[128,2304]{1,0:T(8,128)(2,1)S(1...) custom-call(s32[1,2048]{1,0:T(1,128)S(1)} %bitcast.14, s32[1,3072]{1,0:T(1,128)S(1)} %bitcast.13, ...), custom_call_target="tpu_custom_call" | custom-call | flops 6000000 | bytes 4000000 | tf_op jit(solution)/shard_map/prepare/pallas_call | solution.py:94
  17.1 1.1 %collective-permute-done.1 = f32[128,128]{1,0:T(8,128)S(1)} collective-permute-done((f32[128,128]{1,0:T(8,128)S(1)}, f32[128,128]{1,0:T(8,128)S(1)}, u32[]{:S(2)}, u32[]{:S(2)}) %collective-permute-start.1) | collective-permute-done | bytes 65568 | tf_op jit(solution)/shard_map/ppermute | solution.py:277
  18.2 2.7 %collective-permute-start.2 = (f32[128,128]{1,0:T(8,128)S(1)}, f32[128,128]{1,0:T(8,128)S(1)}, u32[]{:S(2)}, u32[]{:S(2)}) collective-permute-start(f32[128,128]{1,0:T(8,128)S(1)} %add.33), channel_id=1, source_target_pairs={{0,16},{4,20},{8,24},{12,28},{16,0},{20,4},{24,8},{28,12},{1,17},{... | collective-permute-start | bytes 196616 | tf_op jit(solution)/shard_map/ppermute | solution.py:277
  20.9 2.6 %collective-permute-done.2 = f32[128,128]{1,0:T(8,128)S(1)} collective-permute-done((f32[128,128]{1,0:T(8,128)S(1)}, f32[128,128]{1,0:T(8,128)S(1)}, u32[]{:S(2)}, u32[]{:S(2)}) %collective-permute-start.2) | collective-permute-done | bytes 65568 | tf_op jit(solution)/shard_map/ppermute | solution.py:277
  23.5 1.6 %collective-permute-start.3 = (f32[128,128]{1,0:T(8,128)S(1)}, f32[128,128]{1,0:T(8,128)S(1)}, u32[]{:S(2)}, u32[]{:S(2)}) collective-permute-start(f32[128,128]{1,0:T(8,128)S(1)} %add.34.refs_0_), channel_id=1, source_target_pairs={{0,2},{1,3},{2,0},{3,1},{4,6},{5,7},{6,4},{7,5},{8,10},{9,11},{10,... | collective-permute-start | bytes 196616 | tf_op jit(solution)/shard_map/ppermute | solution.py:277
  25.0 0.0 collective-permute-start.4
  25.0 2.7 %collective-permute-done.3.refs_1_ = f32[128,128]{1,0:T(8,128)S(1)} collective-permute-done((f32[128,128]{1,0:T(8,128)S(1)}, f32[128,128]{1,0:T(8,128)S(1)}, u32[]{:S(2)}, u32[]{:S(2)}) %collective-permute-start.3) | collective-permute-done | bytes 65568 | tf_op jit(solution)/shard_map/ppermute | solution.py:277
  27.8 0.0 collective-permute-start.5
  27.8 0.0 collective-permute-done.4.refs_2_
  27.8 1.2 %collective-permute-done.5.refs_3_ = f32[128,128]{1,0:T(8,128)S(1)} collective-permute-done((f32[128,128]{1,0:T(8,128)S(1)}, f32[128,128]{1,0:T(8,128)S(1)}, u32[]{:S(2)}, u32[]{:S(2)}) %collective-permute-start.5) | collective-permute-done | bytes 65568 | tf_op jit(solution)/shard_map/ppermute | solution.py:277
  29.0 11.8 %eliminate.1 = f32[1048,2096]{1,0:T(8,128)} custom-call(f32[128,128]{1,0:T(8,128)S(1)} %add.34.refs_0_, f32[128,128]{1,0:T(8,128)S(1)} %collective-permute-done.3.refs_1_, f32[128,128]{1,0:T(8,128)S(1)} %collective-permute-done.4.refs_2_, f32[128,128]{1,0:T(8,128)S(1)} %collective-permute-done.5.refs_3_, s32[2]{0:T(128)S(1)} %pad_add_fusion.refs_4_, ...), custom_call_target="tpu_custom_call" | custom-call | tf_op jit(solution)/shard_map/eliminate/pallas_call | solution.py:252
  (6 shorter events, 0.1 us)
Async XLA Ops:
  2.9 10.2 %collective-permute-start = (f32[128,128]{1,0:T(8,128)}, f32[128,128]{1,0:T(8,128)S(1)}, u32[]{:S(2)}, u32[]{:S(2)}) collective-permute-start(f32[128,128]{1,0:T(8,128)} %project.1), channel_id=1, source_target_pairs={{0,4},{4,0},{8,12},{12,8},{16,20},{20,16},{24,28},{28,24},{1,5},{5... | collective-permute-start | bytes 196616 | tf_op jit(solution)/shard_map/ppermute | solution.py:277
  13.9 4.3 %collective-permute-start.1 = (f32[128,128]{1,0:T(8,128)S(1)}, f32[128,128]{1,0:T(8,128)S(1)}, u32[]{:S(2)}, u32[]{:S(2)}) collective-permute-start(f32[128,128]{1,0:T(8,128)S(1)} %add.30), channel_id=1, source_target_pairs={{0,8},{4,12},{8,0},{12,4},{16,24},{20,28},{24,16},{28,20},{1,9},{5... | collective-permute-start | bytes 196616 | tf_op jit(solution)/shard_map/ppermute | solution.py:277
  18.2 5.2 %collective-permute-start.2 = (f32[128,128]{1,0:T(8,128)S(1)}, f32[128,128]{1,0:T(8,128)S(1)}, u32[]{:S(2)}, u32[]{:S(2)}) collective-permute-start(f32[128,128]{1,0:T(8,128)S(1)} %add.33), channel_id=1, source_target_pairs={{0,16},{4,20},{8,24},{12,28},{16,0},{20,4},{24,8},{28,12},{1,17},{... | collective-permute-start | bytes 196616 | tf_op jit(solution)/shard_map/ppermute | solution.py:277
  23.5 4.3 %collective-permute-start.3 = (f32[128,128]{1,0:T(8,128)S(1)}, f32[128,128]{1,0:T(8,128)S(1)}, u32[]{:S(2)}, u32[]{:S(2)}) collective-permute-start(f32[128,128]{1,0:T(8,128)S(1)} %add.34.refs_0_), channel_id=1, source_target_pairs={{0,2},{1,3},{2,0},{3,1},{4,6},{5,7},{6,4},{7,5},{8,10},{9,11},{10,... | collective-permute-start | bytes 196616 | tf_op jit(solution)/shard_map/ppermute | solution.py:277
  25.0 2.8 %collective-permute-start.4 = (f32[128,128]{1,0:T(8,128)S(1)}, f32[128,128]{1,0:T(8,128)S(1)}, u32[]{:S(2)}, u32[]{:S(2)}) collective-permute-start(f32[128,128]{1,0:T(8,128)S(1)} %add.34.refs_0_), channel_id=1, source_target_pairs={{0,1},{1,0},{2,3},{3,2},{4,5},{5,4},{6,7},{7,6},{8,9},{9,8},{10,11... | collective-permute-start | bytes 196616 | tf_op jit(solution)/shard_map/ppermute | solution.py:277
  27.8 1.3 %collective-permute-start.5 = (f32[128,128]{1,0:T(8,128)S(1)}, f32[128,128]{1,0:T(8,128)S(1)}, u32[]{:S(2)}, u32[]{:S(2)}) collective-permute-start(f32[128,128]{1,0:T(8,128)S(1)} %collective-permute-done.3.refs_1_), channel_id=1, source_target_pairs={{0,1},{1,0},{2,3},{3,2},{4,5},{5,4},{6,7},{7,6},{8,9},{9,8},{10,11... | collective-permute-start | bytes 196616 | tf_op jit(solution)/shard_map/ppermute | solution.py:277

commit v3 on v2

--- a/solution.py
+++ b/solution.py
@@ -12,6 +12,8 @@
 LANES = 128
 VMEM_LIMIT = 32 * 1024 * 1024
 PREPARE_VMEM = 16 * 1024 * 1024
+FILL = (3, 4, 4, 4)
+JOIN = (0, 3, 6, 9)
 
 
 def round_up(size, multiple):
@@ -70,42 +72,73 @@
     return leading, jnp.where(order < 0, -1, trailing)
 
 
-def prepare_kernel(size, rows_ref, cols_ref, diag_ref, lead_r, trail_r, one_r, lead_c, trail_c, one_c, diag_col):
-    def column(row):
-        return jnp.broadcast_to(row, (LANES, row.shape[1])).T
-
-    rank, count = size.rank, lead_r.shape[0]
-    leading, trailing = decode(rows_ref[:, pl.ds(0, count)], rank)
+def column(row):
+    return jnp.broadcast_to(row, (LANES, row.shape[1])).T
+
+
+def take_window(values, offset, length, padded, fill):
+    total = round_up(values.shape[1], LANES)
+    values = jnp.pad(values, ((0, 0), (0, total - values.shape[1])))
+    moved = pltpu.roll(values, lax.rem(total - offset, total), 1)[:, :padded]
+    lane = lax.broadcasted_iota(jnp.int32, moved.shape, 1)
+    return jnp.where(lane < length, moved, fill)
+
+
+def prepare_rows_kernel(size, order_ref, regular_ref, lead, trail, one, diag_col, diag_panel):
+    count = lead.shape[0]
+    offset = lax.axis_index("node") * size.rows
+    order = order_ref[...].reshape(1, size.count)
+    parts = [take_window(order, offset, size.rows, size.rows_pad, -1)]
+    lane = lax.broadcasted_iota(jnp.int32, (1, size.panel_pad), 1)
+    for first in (0, size.panel_width):
+        tile, shift = first // LANES * LANES, first % LANES
+        inside = (lane >= shift) & (lane < shift + size.panel_width)
+        parts.append(jnp.where(inside, order[:, tile : tile + size.panel_pad], -1))
+    leading, trailing = decode(jnp.concatenate(parts, axis=1), size.rank)
     leading, trailing = column(leading.astype(F32)), column(trailing.astype(F32))
     lane = lax.broadcasted_iota(jnp.int32, (count, LANES), 1).astype(F32)
-    lead_r[...] = (leading == lane).astype(F32).astype(BF16)
-    trail_r[...] = (trailing == lane).astype(F32).astype(BF16)
-    one_r[...] = (trailing == float(rank)).astype(F32)
-    leading, trailing = decode(cols_ref[:, pl.ds(0, size.cols_pad)], rank)
-    mode = lax.broadcasted_iota(jnp.int32, (rank, size.cols_pad), 0)
-    lead_c[...] = (leading == mode).astype(F32).astype(BF16)
-    trail_c[...] = (trailing == mode).astype(F32).astype(BF16)
-    one_c[...] = (trailing == rank).astype(F32)
-    diag_col[...] = column(diag_ref[:, pl.ds(0, size.packed)])
-
-
-def prepare(size, order_rows, order_cols, diag_own):
-    rank, cols, rows = size.rank, size.cols_pad, size.rows_pad + 2 * size.panel_pad
+    lead[...] = (leading == lane).astype(F32).astype(BF16)
+    trail[...] = (trailing == lane).astype(F32).astype(BF16)
+    one[...] = (trailing == float(size.rank)).astype(F32)
+    regular = regular_ref[...].reshape(1, size.count)[:, : size.packed]
+    lane = lax.broadcasted_iota(jnp.int32, regular.shape, 1)
+    diag = jnp.where(lane < size.panel_total, regular, 0.0)
+    diag_panel[...] = diag
+    diag_col[...] = column(jnp.where(offset == 0, diag, 0.0))
+
+
+def prepare_cols_kernel(size, order_ref, regular_ref, lead, trail, one, diag_cols):
+    offset = lax.axis_index("tm") * size.cols
+    order = take_window(order_ref[...].reshape(1, size.count), offset, size.cols, size.cols_pad, -1)
+    diag_cols[...] = take_window(regular_ref[...].reshape(1, size.count), offset, size.cols, size.cols_pad, 0.0)
+    leading, trailing = decode(order, size.rank)
+    mode = lax.broadcasted_iota(jnp.int32, (size.rank, size.cols_pad), 0)
+    lead[...] = (leading == mode).astype(F32).astype(BF16)
+    trail[...] = (trailing == mode).astype(F32).astype(BF16)
+    one[...] = (trailing == size.rank).astype(F32)
+
+
+def prepare(kernel, name, size, shapes, feature_order, regular):
     return pl.pallas_call(
-        functools.partial(prepare_kernel, size),
-        out_shape=[
-            jax.ShapeDtypeStruct((rows, rank), BF16),
-            jax.ShapeDtypeStruct((rows, rank), BF16),
-            jax.ShapeDtypeStruct((rows, LANES), F32),
-            jax.ShapeDtypeStruct((rank, cols), BF16),
-            jax.ShapeDtypeStruct((rank, cols), BF16),
-            jax.ShapeDtypeStruct((1, cols), F32),
-            jax.ShapeDtypeStruct((size.packed, LANES), F32),
-        ],
+        functools.partial(kernel, size),
+        in_specs=[pl.BlockSpec(memory_space=pltpu.VMEM)] * 2,
+        out_shape=[jax.ShapeDtypeStruct(shape, dtype) for shape, dtype in shapes],
         compiler_params=pltpu.CompilerParams(vmem_limit_bytes=PREPARE_VMEM),
-        cost_estimate=pl.CostEstimate(flops=6_000_000, bytes_accessed=4_000_000, transcendentals=0),
-        name="prepare",
-    )(order_rows, order_cols, diag_own)
+        cost_estimate=pl.CostEstimate(flops=3_000_000, bytes_accessed=2_000_000, transcendentals=0),
+        name=name,
+    )(feature_order, regular)
+
+
+def prepare_rows(size, feature_order, regular):
+    rows = size.rows_pad + 2 * size.panel_pad
+    shapes = [((rows, size.rank), BF16)] * 2 + [((rows, LANES), F32)]
+    shapes += [((size.packed, LANES), F32), ((1, size.packed), F32)]
+    return prepare(prepare_rows_kernel, "prepare_rows", size, shapes, feature_order, regular)
+
+
+def prepare_cols(size, feature_order, regular):
+    shapes = [((size.rank, size.cols_pad), BF16)] * 2 + [((1, size.cols_pad), F32)] * 2
+    return prepare(prepare_cols_kernel, "prepare_cols", size, shapes, feature_order, regular)
 
 
 def split(values):
@@ -115,8 +148,10 @@
 
 def eliminate_kernel(size, *refs):
     parts, refs = refs[: size.parts], refs[size.parts :]
-    (where, lead_r, trail_r, one_r, lead_c, trail_c, one_c, diag_col, inverse0, inverse1, diag_panel, diag_cols) = refs[:12]
-    (out, modes2, modes2_t, feats_p, feats_r, feats_c, weights, panel_w, panel_w16, schur_q, block_sum, sems) = refs[12:]
+    lead_r, trail_r, one_r, diag_col, diag_panel, lead_c, trail_c, one_c, diag_cols, inverse0, inverse1 = refs[:11]
+    (out, modes2, modes2_t, feats_p, feats_r, feats_c, weights, panel_w, panel_w16, schur_q, block_sum, sems) = refs[11:]
+    row_offset = lax.axis_index("node") * size.rows
+    col_offset = lax.axis_index("tm") * size.cols
     snaps, block, rows, cols = size.snaps, size.block, size.rows, size.cols
     pad, chunk = size.panel_pad, size.chunk
     inv_snaps = 1.0 / size.snaps
@@ -142,30 +177,6 @@
         latter = mm(both, jnp.concatenate([trail, trail], axis=0)) + one_c[:, pl.ds(start, count)]
         feats_c[:, pl.ds(start, count)] = (former * latter).astype(BF16)
 
-    for start in range(0, 2 * pad, pad):
-        feats_p[pl.ds(start, pad), :] = row_features(size.rows_pad + start, pad)
-    first, second = feats_p[pl.ds(0, pad), :], feats_p[pl.ds(pad, pad), :]
-    inv0, inv1 = inverse0[...], inverse1[...]
-    inv0_16, inv1_16 = inv0.astype(BF16), inv1.astype(BF16)
-    fillers = [functools.partial(column_features, start, min(block, size.cols_pad - start)) for start in range(0, size.cols_pad, block)]
-
-    def fill():
-        if fillers:
-            fillers.pop(0)()
-
-    cross = (mm_nt(first, second) * inv_snaps).astype(BF16)
-    fill()
-    coupling = mm(inv0_16, cross).astype(BF16)
-    fill()
-    q01 = -mm(coupling, inv1_16)
-    q10 = -mm_nt(inv1_16, coupling)
-    fill()
-    q00 = inv0 - mm_nt(q01.astype(BF16), coupling)
-    fill()
-    top = mm(q00.astype(BF16), first) + mm(q01.astype(BF16), second)
-    bottom = mm(q10.astype(BF16), first) + mm(inv1_16, second)
-    while fillers:
-        fill()
     joint = size.panel_width // LANES * LANES
     over = pad - joint
 
@@ -175,19 +186,57 @@
         tail = lax.slice_in_dim(lower, over, pad, axis=axis)
         return jnp.concatenate([lead_part, shared, tail], axis=axis)
 
-    packed = pack(top, bottom, 0) * inv_snaps
+    fillers = []
+
+    def fill(count):
+        while fillers and count > 0:
+            fillers.pop(0)()
+            count -= 1
+
+    def make_rows(start):
+        feats_r[pl.ds(start, chunk), :] = row_features(start, chunk)
+
+    for start in range(0, 2 * pad, pad):
+        feats_p[pl.ds(start, pad), :] = row_features(size.rows_pad + start, pad)
+    for start in range(0, size.rows_feats, chunk):
+        fillers.append(functools.partial(make_rows, start))
+    for start in range(0, size.cols_pad, block):
+        fillers.append(functools.partial(column_features, start, min(block, size.cols_pad - start)))
+    first, second = feats_p[pl.ds(0, pad), :], feats_p[pl.ds(pad, pad), :]
+    inv0, inv1 = inverse0[...].astype(BF16), inverse1[...].astype(BF16)
+    cross = (mm_nt(second, first) * inv_snaps).astype(BF16)
+    inner = {}
+
+    def join(turn):
+        if turn == 0:
+            inner["coupling"] = mm_nt(inv0, cross).astype(BF16)
+        elif turn == 1:
+            inner["q01"] = -mm(inner["coupling"], inv1)
+        elif turn == 2:
+            inner["q10"] = -mm_nt(inv1, inner["coupling"])
+        else:
+            q00 = inverse0[...] - mm_nt(inner["q01"].astype(BF16), inner["coupling"])
+            schur_q[...] = pack(pack(q00, inner["q01"], 1), pack(inner["q10"], inverse1[...], 1), 0)
+
+    for turn, place in enumerate(JOIN):
+        fillers.insert(place, functools.partial(join, turn))
+    scaled0 = mm(inv0, first).astype(BF16)
+    fill(FILL[0])
+    left1 = (second.astype(F32) - mm(cross, scaled0)).astype(BF16)
+    fill(FILL[1])
+    scaled1 = mm(inv1, left1)
+    fill(FILL[2])
+    scaled1_16 = scaled1.astype(BF16)
+    spread = mm_tn(jnp.concatenate([first, left1], axis=0), jnp.concatenate([scaled0, scaled1_16], axis=0))
+    spread = (spread * inv_snaps).astype(BF16)
+    fill(FILL[3])
+    back = first.astype(F32) - mm_tn(cross, scaled1_16)
+    packed = pack(mm(inv0, back.astype(BF16)), scaled1, 0) * inv_snaps
     panel_w[...] = packed
-    panel_w16[pl.ds(0, size.packed), :] = packed.astype(BF16)
-    if panel_w16.shape[0] > size.packed:
-        panel_w16[pl.ds(size.packed, panel_w16.shape[0] - size.packed), :] = jnp.zeros(
-            (panel_w16.shape[0] - size.packed, snaps), BF16
-        )
-    schur_q[...] = pack(pack(q00, q01, 1), pack(q10, inv1, 1), 0)
-    spread = mm_tn(feats_p[...], jnp.concatenate([top, bottom], axis=0).astype(BF16))
-    spread = (spread * inv_snaps).astype(BF16)
+    panel_w16[...] = packed.astype(BF16)
+    fill(len(fillers))
     for start in range(0, size.rows_feats, chunk):
-        feats = row_features(start, chunk)
-        feats_r[pl.ds(start, chunk), :] = feats
+        feats = feats_r[pl.ds(start, chunk), :]
         weight = (feats.astype(F32) - mm(feats, spread)) * inv_snaps
         inside = min(chunk, size.packed - start)
         if inside > 0:
@@ -198,7 +247,7 @@
             weight = weight - own
         weights[pl.ds(start, chunk), :] = weight.astype(BF16)
 
-    delta = where[0] - where[1]
+    delta = row_offset - col_offset
 
     def write(first_panel):
         copies = []
@@ -232,11 +281,11 @@
         for copy in copies:
             copy.wait()
 
-    @pl.when(where[1] == 0)
+    @pl.when(col_offset == 0)
     def _():
         write(True)
 
-    @pl.when(where[1] != 0)
+    @pl.when(col_offset != 0)
     def _():
         write(False)
 
@@ -246,12 +295,12 @@
         self.__dict__.update(entries)
 
 
-def eliminate(size, parts, where, tables, inverses, diag_panel, diag_cols):
-    rank, snaps, block = size.rank, size.snaps, size.block
+def eliminate(size, parts, tables, inverses):
+    rank, snaps = size.rank, size.snaps
     whole = pl.BlockSpec(memory_space=pltpu.VMEM)
     return pl.pallas_call(
         functools.partial(eliminate_kernel, size),
-        in_specs=[whole] * size.parts + [pl.BlockSpec(memory_space=pltpu.SMEM)] + [whole] * 11,
+        in_specs=[whole] * (size.parts + 11),
         out_specs=pl.BlockSpec(memory_space=pl.ANY),
         out_shape=jax.ShapeDtypeStruct((size.rows, size.cols), F32),
         scratch_shapes=[
@@ -262,14 +311,14 @@
             pltpu.VMEM((snaps, size.cols_pad), BF16),
             pltpu.VMEM((size.rows_feats, snaps), BF16),
             pltpu.VMEM((size.packed, snaps), F32),
-            pltpu.VMEM((round_up(size.packed, LANES), snaps), BF16),
+            pltpu.VMEM((size.packed, snaps), BF16),
             pltpu.VMEM((size.packed, size.packed), F32),
             pltpu.VMEM((size.rows, size.cols), F32),
             pltpu.SemaphoreType.DMA((len(size.row_blocks),)),
         ],
         compiler_params=pltpu.CompilerParams(vmem_limit_bytes=VMEM_LIMIT),
         name="eliminate",
-    )(*parts, where, *tables, *inverses, diag_panel, diag_cols)
+    )(*parts, *tables, *inverses)
 
 
 def partner(values, axis, distance):
@@ -309,58 +358,28 @@
         panel_total=panels * width,
         packed=width // LANES * LANES + panel_pad,
         rows_pad=round_up(rows, LANES),
-        long=1024,
+        count=count,
         cols_pad=round_up(cols, 256),
         chunk=176,
     )
     size.rows_feats = round_up(rows, size.chunk)
     size.row_blocks = row_blocks(size.rows_feats)
-    row_offset = lax.axis_index("node") * rows
-    col_offset = lax.axis_index("tm") * cols
-
     total = project(codes, node_scale, basis)
-
-    def window(values, offset, length, padded, fill):
-        taken = lax.dynamic_slice_in_dim(values, offset, length)
-        return jnp.pad(taken, (0, padded - length), constant_values=fill)
-
-    def panel_positions(values, fill):
-        return [
-            jnp.pad(values[:width], (0, panel_pad - width), constant_values=fill),
-            jnp.pad(values[width : 2 * width], (shift, panel_pad - width - shift), constant_values=fill),
-        ]
-
-    def long_row(values, fill):
-        length = values.shape[0]
-        return jnp.pad(values, (0, round_up(length, size.long) - length), constant_values=fill)[None]
-
-    order_rows = long_row(
-        jnp.concatenate(
-            [window(feature_order, row_offset, rows, size.rows_pad, -1)] + panel_positions(feature_order, -1)
-        ),
-        -1,
-    )
-    order_cols = long_row(lax.dynamic_slice_in_dim(feature_order, col_offset, cols), -1)
-    diag_cols = long_row(lax.dynamic_slice_in_dim(regular, col_offset, cols), 0)
-    diag_panel = long_row(regular[: size.panel_total], 0)
-    diag_own = diag_panel * (row_offset == 0).astype(F32)
     gaps = [(0, panel_pad - width)], [(shift, panel_pad - width - shift)]
     inverses = [jnp.pad(panel_inverse[k], gaps[k] * 2) for k in range(2)]
-    where = jnp.stack([row_offset, col_offset]).astype(jnp.int32)
-    inputs = (order_rows, order_cols, diag_own, diag_panel, diag_cols, inverses, where)
-    tables = None
-    for turn, distance in enumerate(distances("node")):
+
+    makers = [prepare_rows, prepare_cols]
+    tables = []
+    for distance in distances("node"):
         total = total + partner(total, "node", distance)
-        if turn == 0:
-            total, inputs = lax.optimization_barrier((total, inputs))
-            order_rows, order_cols, diag_own, diag_panel, diag_cols, inverses, where = inputs
-            tables = prepare(size, order_rows, order_cols, diag_own)
-        elif turn == 1:
-            total, tables = lax.optimization_barrier((total, tables))
+        if makers:
+            made = makers.pop(0)(size, feature_order, regular)
+            total, made = lax.optimization_barrier((total, made))
+            tables += made
     parts = [total]
     for distance in reversed(distances("tm")):
         parts = parts + [partner(part, "tm", distance) for part in parts]
-    return eliminate(size, parts, where, tables, inverses, diag_panel, diag_cols)
+    return eliminate(size, parts, tables, inverses)
 
 
 def solution(mesh):

time: 41.6 us -> 35.7 us (0.86)
  waiting for transfers between devices: 7.65 us -> 4 us
  starting transfers between devices: 8.82 us -> 10.5 us
  local copies, waits for them, and re-layouts: 5.62 us -> 4 us
  other arithmetic: 2.44 us -> 0.87 us
  Pallas kernels: 16.3 us -> 15.8 us
    ppermute x6, waiting for transfers between devices: 7.65 us -> 4 us  [partner(): return lax.ppermute(values, axis, [(i, i ^ distance) for i in range(count)])]
    dynamic_slice x3 -> x0, local copies, waits for them, and re-layouts: 2.36 us -> none  [the longest x1 0.79 us: per_device(): lax.dynamic_slice_in_dim(feature_order, col_offset, cols)]
    ppermute x6, starting transfers between devices: 8.82 us -> 10.5 us  [partner(): return lax.ppermute(values, axis, [(i, i ^ distance) for i in range(count)])]
    unnamed x0 -> x4, local copies, waits for them, and re-layouts: none -> 1.53 us
    pad x2 -> x0, other arithmetic: 1.42 us -> none  [the longest x1 0.71 us: long_row(): jnp.pad(values, (0, round_up(length, size.long) - length), constant_value...]
    pallas_call x1, Pallas kernels: 11.8 us -> 10.8 us  [eliminate(): pl.pallas_call(functools.partial(eliminate_kernel, size), in_specs=[whole...]
    slice x1 -> x0, local copies, waits for them, and re-layouts: 0.76 us -> none  [panel_positions(): values[width:2 * width]]
    pallas_call x1 -> x2, Pallas kernels: 1.6 us -> 2.16 us  [prepare(): pl.pallas_call(functools.partial(kernel, size), in_specs=[pl.BlockSpec(me...]
  transfers between devices with their start and end apart: 6 -> 6, of which waited for: 4 -> 5; matrix products, arithmetic and copies ran while one was open for 18% -> 7% of each run, Pallas kernels for 4% -> 6%
where the time goes in v3:
time: 35.7 us; the launch traced here: 35.4 us
  Pallas kernels  15.8 us (44%)
  starting transfers between devices  10.5 us (29%)
  local copies, waits for them, and re-layouts  4 us (11%)
  waiting for transfers between devices  4 us (11%)
  other arithmetic  0.87 us (2%)
    pallas_call x1, Pallas kernels, eliminate(): pl.pallas_call(functools.partial(eliminate_kernel, size), in_specs=[whole...  10.8 us
    ppermute x6, starting transfers between devices, partner(): return lax.ppermute(values, axis, [(i, i ^ distance) for i in range(count)])  10.5 us
    ppermute x6, waiting for transfers between devices, partner(): return lax.ppermute(values, axis, [(i, i ^ distance) for i in range(count)])  4 us
    pallas_call x1, Pallas kernels, project(): pl.pallas_call(project_kernel, grid=(nodes // block,), in_specs=[pl.Block...  2.87 us
    slice x1, local copies, waits for them, and re-layouts, per_device(): inverses = [jnp.pad(panel_inverse[k], gaps[k] * 2) for k in range(2)]  2.17 us
    pallas_call x2, Pallas kernels, prepare(): pl.pallas_call(functools.partial(kernel, size), in_specs=[pl.BlockSpec(me...  2.16 us
    unnamed x4, local copies, waits for them, and re-layouts  1.53 us
    add x3, other arithmetic, per_device(): total = total + partner(total, 'node', distance)  0.87 us
  transfers between devices with their start and end apart: 6, of which 5 were waited for; matrix products, arithmetic and copies ran while one was open for 7% of the time, Pallas kernels for 6%

profile of v3, /device:TPU:0, one launch (start us, length us, event | category | flops | bytes accessed | tf_op | source)
XLA Modules:
  0.0 35.4 jit_solution(11203099594260579744)
XLA Ops:
  0.0 2.9 %project.1 = f32[128,128]{1,0:T(8,128)} custom-call(s32[4096,128]{1,0:T(8,128)} %codes_ref.1, f32[1,4096]{1,0:T(1,128)} %bitcast.5, bf16[4096,128]{1,0:T(8,128)(2,1)} %basis_ref.1), custom_call_target="tpu_custom_call" | custom-call | tf_op jit(solution)/shard_map/project/pallas_call | solution.py:48
  2.9 2.9 %collective-permute-start = (f32[128,128]{1,0:T(8,128)}, f32[128,128]{1,0:T(8,128)S(1)}, u32[]{:S(2)}, u32[]{:S(2)}) collective-permute-start(f32[128,128]{1,0:T(8,128)} %project.1), channel_id=1, source_target_pairs={{0,4},{4,0},{8,12},{12,8},{16,20},{20,16},{24,28},{28,24},{1,5},{5... | collective-permute-start | bytes 196616 | tf_op jit(solution)/shard_map/ppermute | solution.py:326
  5.8 0.0 copy-start
  5.8 0.8 %copy-done = s32[8384]{0:T(1024)S(1)} copy-done((s32[8384]{0:T(1024)S(1)}, s32[8384]{0:T(1024)}, u32[]{:S(2)}) %copy-start) | copy-done | bytes 33560
  6.6 0.0 copy-start.1
  6.6 0.8 %copy-done.1 = f32[8384]{0:T(1024)S(1)} copy-done((f32[8384]{0:T(1024)S(1)}, f32[8384]{0:T(1024)}, u32[]{:S(2)}) %copy-start.1) | copy-done | bytes 33560
  7.3 0.9 %prepare_rows.1 = (bf16[1920,128]{1,0:T(8,128)(2,1)S(1)}, bf16[1920,128]{1,0:T(8,128)(2,1)S(1)}, f32[1920,128]{1,0:T(8,128)S(1)}, f32[640,128]{1,0:T(8,128)S(1)}, f32[1,640]{1,0:T(1,128)S(1)}) custom-call(s32[8384]{0:T(1024)S(1)} %copy-done, f32[8384]{0:T(1024)S(1)} %copy-done.1), custom_call_target="tpu_custom_call" | custom-call | flops 3000000 | bytes 2000000 | tf_op jit(solution)/shard_map/prepare_rows/pallas_call | solution.py:122
  8.2 0.0 collective-permute-done
  8.3 0.8 %add.13 = f32[128,128]{1,0:T(8,128)S(1)} add(f32[128,128]{1,0:T(8,128)} %project.1, f32[128,128]{1,0:T(8,128)S(1)} %collective-permute-done) | non-fusion elementwise | flops 16384 | bytes 196608 | tf_op jit(solution)/shard_map/add | solution.py:374
  9.1 2.1 %collective-permute-start.1 = (f32[128,128]{1,0:T(8,128)S(1)}, f32[128,128]{1,0:T(8,128)S(1)}, u32[]{:S(2)}, u32[]{:S(2)}) collective-permute-start(f32[128,128]{1,0:T(8,128)S(1)} %add.13), channel_id=1, source_target_pairs={{0,8},{4,12},{8,0},{12,4},{16,24},{20,28},{24,16},{28,20},{1,9},{5... | collective-permute-start | bytes 196616 | tf_op jit(solution)/shard_map/ppermute | solution.py:326
  11.2 1.3 %prepare_cols.1 = (bf16[128,2304]{1,0:T(8,128)(2,1)S(1)}, bf16[128,2304]{1,0:T(8,128)(2,1)S(1)}, f32[1,2304]{1,0:T(1,128)S(1)}, f32[1,2304]{1,0:T(1,128)S(1)}) custom-call(s32[8384]{0:T(1024)S(1)} %copy-done, f32[8384]{0:T(1024)S(1)} %copy-done.1), custom_call_target="tpu_custom_call" | custom-call | flops 3000000 | bytes 2000000 | tf_op jit(solution)/shard_map/prepare_cols/pallas_call | solution.py:122
  12.5 1.0 %collective-permute-done.1 = f32[128,128]{1,0:T(8,128)S(1)} collective-permute-done((f32[128,128]{1,0:T(8,128)S(1)}, f32[128,128]{1,0:T(8,128)S(1)}, u32[]{:S(2)}, u32[]{:S(2)}) %collective-permute-start.1) | collective-permute-done | bytes 65568 | tf_op jit(solution)/shard_map/ppermute | solution.py:326
  13.5 3.1 %collective-permute-start.2 = (f32[128,128]{1,0:T(8,128)S(1)}, f32[128,128]{1,0:T(8,128)S(1)}, u32[]{:S(2)}, u32[]{:S(2)}) collective-permute-start(f32[128,128]{1,0:T(8,128)S(1)} %add.14), channel_id=1, source_target_pairs={{0,16},{4,20},{8,24},{12,28},{16,0},{20,4},{24,8},{28,12},{1,17},{... | collective-permute-start | bytes 196616 | tf_op jit(solution)/shard_map/ppermute | solution.py:326
  16.6 2.2 %collective-permute-done.2 = f32[128,128]{1,0:T(8,128)S(1)} collective-permute-done((f32[128,128]{1,0:T(8,128)S(1)}, f32[128,128]{1,0:T(8,128)S(1)}, u32[]{:S(2)}, u32[]{:S(2)}) %collective-permute-start.2) | collective-permute-done | bytes 65568 | tf_op jit(solution)/shard_map/ppermute | solution.py:326
  18.8 1.9 %collective-permute-start.3 = (f32[128,128]{1,0:T(8,128)S(1)}, f32[128,128]{1,0:T(8,128)S(1)}, u32[]{:S(2)}, u32[]{:S(2)}) collective-permute-start(f32[128,128]{1,0:T(8,128)S(1)} %add.15.refs_0_), channel_id=1, source_target_pairs={{0,2},{1,3},{2,0},{3,1},{4,6},{5,7},{6,4},{7,5},{8,10},{9,11},{10,... | collective-permute-start | bytes 196616 | tf_op jit(solution)/shard_map/ppermute | solution.py:326
  20.7 2.2 %fusion = (f32[1,262,262]{2,0,1:T(1,128)S(1)}, f32[1,262,262]{2,0,1:T(1,128)S(1)}) fusion(f32[2,262,262]{2,0,1:T(2,128)} %param.11), kind=kLoop, calls=%fused_computation.2 | loop fusion | bytes 1098304 | tf_op jit(solution)/shard_map/slice | solution.py:369
  22.9 0.1 collective-permute-start.4
  23.0 0.2 collective-permute-done.3.refs_1_
  23.2 0.3 collective-permute-start.5
  23.5 0.1 copy_bitcast_fusion
  23.6 0.2 pad.9.refs_14_
  23.8 0.4 %collective-permute-done.4.refs_2_ = f32[128,128]{1,0:T(8,128)S(1)} collective-permute-done((f32[128,128]{1,0:T(8,128)S(1)}, f32[128,128]{1,0:T(8,128)S(1)}, u32[]{:S(2)}, u32[]{:S(2)}) %collective-permute-start.4) | collective-permute-done | bytes 65568 | tf_op jit(solution)/shard_map/ppermute | solution.py:326
  24.2 0.2 collective-permute-done.5.refs_3_
  24.4 10.8 %eliminate.1 = f32[1048,2096]{1,0:T(8,128)} custom-call(f32[128,128]{1,0:T(8,128)S(1)} %add.15.refs_0_, f32[128,128]{1,0:T(8,128)S(1)} %collective-permute-done.3.refs_1_, f32[128,128]{1,0:T(8,128)S(1)} %collective-permute-done.4.refs_2_, f32[128,128]{1,0:T(8,128)S(1)} %collective-permute-done.5.refs_3_, bf16[1920,128]{1,0:T(8,128)(2,1)S(1)} %get-tuple-element.36.refs_4_, ...), custom_call_target="tpu_custom_call" | custom-call | tf_op jit(solution)/shard_map/eliminate/pallas_call | solution.py:301
  (3 shorter events, 0.1 us)
Async XLA Ops:
  2.9 5.4 %collective-permute-start = (f32[128,128]{1,0:T(8,128)}, f32[128,128]{1,0:T(8,128)S(1)}, u32[]{:S(2)}, u32[]{:S(2)}) collective-permute-start(f32[128,128]{1,0:T(8,128)} %project.1), channel_id=1, source_target_pairs={{0,4},{4,0},{8,12},{12,8},{16,20},{20,16},{24,28},{28,24},{1,5},{5... | collective-permute-start | bytes 196616 | tf_op jit(solution)/shard_map/ppermute | solution.py:326
  5.8 0.8 %copy-start = (s32[8384]{0:T(1024)S(1)}, s32[8384]{0:T(1024)}, u32[]{:S(2)}) copy-start(s32[8384]{0:T(1024)} %order_ref.3) | copy-start | bytes 100612
  6.6 0.8 %copy-start.1 = (f32[8384]{0:T(1024)S(1)}, f32[8384]{0:T(1024)}, u32[]{:S(2)}) copy-start(f32[8384]{0:T(1024)} %regular_ref.3) | copy-start | bytes 100612
  9.1 4.4 %collective-permute-start.1 = (f32[128,128]{1,0:T(8,128)S(1)}, f32[128,128]{1,0:T(8,128)S(1)}, u32[]{:S(2)}, u32[]{:S(2)}) collective-permute-start(f32[128,128]{1,0:T(8,128)S(1)} %add.13), channel_id=1, source_target_pairs={{0,8},{4,12},{8,0},{12,4},{16,24},{20,28},{24,16},{28,20},{1,9},{5... | collective-permute-start | bytes 196616 | tf_op jit(solution)/shard_map/ppermute | solution.py:326
  13.5 5.3 %collective-permute-start.2 = (f32[128,128]{1,0:T(8,128)S(1)}, f32[128,128]{1,0:T(8,128)S(1)}, u32[]{:S(2)}, u32[]{:S(2)}) collective-permute-start(f32[128,128]{1,0:T(8,128)S(1)} %add.14), channel_id=1, source_target_pairs={{0,16},{4,20},{8,24},{12,28},{16,0},{20,4},{24,8},{28,12},{1,17},{... | collective-permute-start | bytes 196616 | tf_op jit(solution)/shard_map/ppermute | solution.py:326
  18.8 4.3 %collective-permute-start.3 = (f32[128,128]{1,0:T(8,128)S(1)}, f32[128,128]{1,0:T(8,128)S(1)}, u32[]{:S(2)}, u32[]{:S(2)}) collective-permute-start(f32[128,128]{1,0:T(8,128)S(1)} %add.15.refs_0_), channel_id=1, source_target_pairs={{0,2},{1,3},{2,0},{3,1},{4,6},{5,7},{6,4},{7,5},{8,10},{9,11},{10,... | collective-permute-start | bytes 196616 | tf_op jit(solution)/shard_map/ppermute | solution.py:326
  22.9 1.3 %collective-permute-start.4 = (f32[128,128]{1,0:T(8,128)S(1)}, f32[128,128]{1,0:T(8,128)S(1)}, u32[]{:S(2)}, u32[]{:S(2)}) collective-permute-start(f32[128,128]{1,0:T(8,128)S(1)} %add.15.refs_0_), channel_id=1, source_target_pairs={{0,1},{1,0},{2,3},{3,2},{4,5},{5,4},{6,7},{7,6},{8,9},{9,8},{10,11... | collective-permute-start | bytes 196616 | tf_op jit(solution)/shard_map/ppermute | solution.py:326
  23.2 1.3 %collective-permute-start.5 = (f32[128,128]{1,0:T(8,128)S(1)}, f32[128,128]{1,0:T(8,128)S(1)}, u32[]{:S(2)}, u32[]{:S(2)}) collective-permute-start(f32[128,128]{1,0:T(8,128)S(1)} %collective-permute-done.3.refs_1_), channel_id=1, source_target_pairs={{0,1},{1,0},{2,3},{3,2},{4,5},{5,4},{6,7},{7,6},{8,9},{9,8},{10,11... | collective-permute-start | bytes 196616 | tf_op jit(solution)/shard_map/ppermute | solution.py:326

commit v4 on v3

--- a/solution.py
+++ b/solution.py
@@ -11,7 +11,7 @@
 BF16 = jnp.bfloat16
 LANES = 128
 VMEM_LIMIT = 32 * 1024 * 1024
-PREPARE_VMEM = 16 * 1024 * 1024
+SMALL_VMEM = 16 * 1024 * 1024
 FILL = (3, 4, 4, 4)
 JOIN = (0, 3, 6, 9)
 
@@ -30,6 +30,10 @@
 
 def mm_tn(left, right):
     return lax.dot_general(left, right, (((0,), (0,)), ((), ())), preferred_element_type=F32)
+
+
+def in_hbm(*arrays):
+    return [pltpu.with_memory_space_constraint(array, pltpu.HBM) for array in arrays]
 
 
 def project_kernel(codes_ref, scale_ref, basis_ref, out_ref):
@@ -45,6 +49,7 @@
     nodes, snaps = codes.shape
     rank = basis.shape[1]
     block = nodes // 2 if nodes % 2048 == 0 else nodes
+    codes, scale, basis = in_hbm(codes, node_scale.reshape(1, nodes), basis)
     return pl.pallas_call(
         project_kernel,
         grid=(nodes // block,),
@@ -55,8 +60,9 @@
         ],
         out_specs=pl.BlockSpec((rank, snaps), lambda i: (0, 0)),
         out_shape=jax.ShapeDtypeStruct((rank, snaps), F32),
+        compiler_params=pltpu.CompilerParams(vmem_limit_bytes=SMALL_VMEM),
         name="project",
-    )(codes, node_scale.reshape(1, nodes), basis)
+    )(codes, scale, basis)
 
 
 def starts(index, rank):
@@ -123,10 +129,10 @@
         functools.partial(kernel, size),
         in_specs=[pl.BlockSpec(memory_space=pltpu.VMEM)] * 2,
         out_shape=[jax.ShapeDtypeStruct(shape, dtype) for shape, dtype in shapes],
-        compiler_params=pltpu.CompilerParams(vmem_limit_bytes=PREPARE_VMEM),
+        compiler_params=pltpu.CompilerParams(vmem_limit_bytes=SMALL_VMEM),
         cost_estimate=pl.CostEstimate(flops=3_000_000, bytes_accessed=2_000_000, transcendentals=0),
         name=name,
-    )(feature_order, regular)
+    )(*in_hbm(feature_order, regular))
 
 
 def prepare_rows(size, feature_order, regular):
@@ -146,36 +152,74 @@
     return upper, (values - upper.astype(F32)).astype(BF16)
 
 
+def feature_makers(parts, lead_r, trail_r, one_r, lead_c, trail_c, one_c):
+    modes_t = jnp.concatenate([part[...] for part in parts], axis=1)
+    snaps = modes_t.shape[1]
+    modes2_t = jnp.concatenate(split(modes_t), axis=0)
+    modes2 = jnp.concatenate(split(modes_t.T), axis=1)
+
+    def row_features(start, count):
+        lead = lead_r[pl.ds(start, count), :]
+        trail = trail_r[pl.ds(start, count), :]
+        one = one_r[pl.ds(start, count), :]
+        former = mm(jnp.concatenate([lead, lead], axis=1), modes2_t)
+        latter = mm(jnp.concatenate([trail, trail], axis=1), modes2_t)
+        return (former * (latter + jnp.concatenate([one] * (snaps // LANES), axis=1))).astype(BF16)
+
+    def column_features(start, count):
+        lead = lead_c[:, pl.ds(start, count)]
+        trail = trail_c[:, pl.ds(start, count)]
+        former = mm(modes2, jnp.concatenate([lead, lead], axis=0))
+        latter = mm(modes2, jnp.concatenate([trail, trail], axis=0)) + one_c[:, pl.ds(start, count)]
+        return (former * latter).astype(BF16)
+
+    return row_features, column_features
+
+
+def features_kernel(size, *refs):
+    parts, refs = refs[: size.parts], refs[size.parts :]
+    tables, (feats_p, feats_r, feats_c) = refs[:6], refs[6:]
+    row_features, column_features = feature_makers(parts, *tables)
+    for start in range(0, 2 * size.panel_pad, size.panel_pad):
+        feats_p[pl.ds(start, size.panel_pad), :] = row_features(size.rows_pad + start, size.panel_pad)
+    for start in range(0, size.rows_feats, size.chunk):
+        feats_r[pl.ds(start, size.chunk), :] = row_features(start, size.chunk)
+    for start in range(0, size.cols_pad, size.block):
+        count = min(size.block, size.cols_pad - start)
+        feats_c[:, pl.ds(start, count)] = column_features(start, count)
+
+
+def feature_shapes(size):
+    half = size.snaps // 2
+    return [(2 * size.panel_pad, half), (size.rows_feats, half), (half, size.cols_pad)]
+
+
+def features(size, parts, tables):
+    return pl.pallas_call(
+        functools.partial(features_kernel, size),
+        in_specs=[pl.BlockSpec(memory_space=pltpu.VMEM)] * (size.parts + 6),
+        out_shape=[jax.ShapeDtypeStruct(shape, BF16) for shape in feature_shapes(size)],
+        compiler_params=pltpu.CompilerParams(vmem_limit_bytes=SMALL_VMEM),
+        cost_estimate=pl.CostEstimate(flops=1_000_000_000, bytes_accessed=2_000_000, transcendentals=0),
+        name="features",
+    )(*parts, *tables)
+
+
 def eliminate_kernel(size, *refs):
     parts, refs = refs[: size.parts], refs[size.parts :]
-    lead_r, trail_r, one_r, diag_col, diag_panel, lead_c, trail_c, one_c, diag_cols, inverse0, inverse1 = refs[:11]
-    (out, modes2, modes2_t, feats_p, feats_r, feats_c, weights, panel_w, panel_w16, schur_q, block_sum, sems) = refs[11:]
+    tables, refs = refs[:6], refs[6:]
+    diag_col, diag_panel, diag_cols, feats_p0, feats_r0, feats_c0, inverse0, inverse1 = refs[:8]
+    out, feats_p1, feats_r1, feats_c1, weights, panel_w, panel_w16, schur_q, block_sum, sems = refs[8:]
     row_offset = lax.axis_index("node") * size.rows
     col_offset = lax.axis_index("tm") * size.cols
     snaps, block, rows, cols = size.snaps, size.block, size.rows, size.cols
     pad, chunk = size.panel_pad, size.chunk
     inv_snaps = 1.0 / size.snaps
-
-    modes_t = jnp.concatenate([part[...] for part in parts], axis=1)
-    modes2_t[...] = jnp.concatenate(split(modes_t), axis=0)
-    modes2[...] = jnp.concatenate(split(modes_t.T), axis=1)
-
-    def row_features(start, count):
-        lead = lead_r[pl.ds(start, count), :]
-        trail = trail_r[pl.ds(start, count), :]
-        one = one_r[pl.ds(start, count), :]
-        both = modes2_t[...]
-        former = mm(jnp.concatenate([lead, lead], axis=1), both)
-        latter = mm(jnp.concatenate([trail, trail], axis=1), both)
-        return (former * (latter + jnp.concatenate([one] * (snaps // LANES), axis=1))).astype(BF16)
-
-    def column_features(start, count):
-        lead = lead_c[:, pl.ds(start, count)]
-        trail = trail_c[:, pl.ds(start, count)]
-        both = modes2[...]
-        former = mm(both, jnp.concatenate([lead, lead], axis=0))
-        latter = mm(both, jnp.concatenate([trail, trail], axis=0)) + one_c[:, pl.ds(start, count)]
-        feats_c[:, pl.ds(start, count)] = (former * latter).astype(BF16)
+    row_features, column_features = feature_makers(parts, *tables)
+
+    def row_block(start, count):
+        at = pl.ds(start, count)
+        return jnp.concatenate([feats_r0[at, :], feats_r1[at, :]], axis=1)
 
     joint = size.panel_width // LANES * LANES
     over = pad - joint
@@ -194,15 +238,21 @@
             count -= 1
 
     def make_rows(start):
-        feats_r[pl.ds(start, chunk), :] = row_features(start, chunk)
-
+        feats_r1[pl.ds(start, chunk), :] = row_features(start, chunk)
+
+    def make_columns(start, count):
+        feats_c1[:, pl.ds(start, count)] = column_features(start, count)
+
+    panels = []
     for start in range(0, 2 * pad, pad):
-        feats_p[pl.ds(start, pad), :] = row_features(size.rows_pad + start, pad)
+        at = pl.ds(start, pad)
+        feats_p1[at, :] = row_features(size.rows_pad + start, pad)
+        panels.append(jnp.concatenate([feats_p0[at, :], feats_p1[at, :]], axis=1))
     for start in range(0, size.rows_feats, chunk):
         fillers.append(functools.partial(make_rows, start))
     for start in range(0, size.cols_pad, block):
-        fillers.append(functools.partial(column_features, start, min(block, size.cols_pad - start)))
-    first, second = feats_p[pl.ds(0, pad), :], feats_p[pl.ds(pad, pad), :]
+        fillers.append(functools.partial(make_columns, start, min(block, size.cols_pad - start)))
+    first, second = panels
     inv0, inv1 = inverse0[...].astype(BF16), inverse1[...].astype(BF16)
     cross = (mm_nt(second, first) * inv_snaps).astype(BF16)
     inner = {}
@@ -236,7 +286,7 @@
     panel_w16[...] = packed.astype(BF16)
     fill(len(fillers))
     for start in range(0, size.rows_feats, chunk):
-        feats = feats_r[pl.ds(start, chunk), :]
+        feats = row_block(start, chunk)
         weight = (feats.astype(F32) - mm(feats, spread)) * inv_snaps
         inside = min(chunk, size.packed - start)
         if inside > 0:
@@ -254,14 +304,15 @@
         for index, (start, count) in enumerate(size.row_blocks):
             kept = min(count, rows - start)
             at = pl.ds(start, kept)
-            full = mm(weights[pl.ds(start, count), :], feats_c[...])[:kept, :cols]
+            every = jnp.concatenate([feats_c0[...], feats_c1[...]], axis=0)
+            full = mm(weights[pl.ds(start, count), :], every)[:kept, :cols]
             row_id = lax.broadcasted_iota(jnp.int32, full.shape, 0)
             col_id = lax.broadcasted_iota(jnp.int32, full.shape, 1)
             full = full + jnp.where(col_id - row_id == delta + start, diag_cols[:, pl.ds(0, cols)], 0.0)
             if first_panel:
                 used = min(size.packed, cols)
                 diag = diag_panel[:, pl.ds(0, used)]
-                left = mm_nt(feats_r[pl.ds(start, count), :], panel_w16[...])[:kept, :used]
+                left = mm_nt(row_block(start, count), panel_w16[...])[:kept, :used]
                 inside = min(kept, size.packed - start)
                 if inside > 0:
                     own = jnp.concatenate([diag_col[pl.ds(start, inside), :]] * (size.packed // LANES), axis=1)
@@ -295,30 +346,25 @@
         self.__dict__.update(entries)
 
 
-def eliminate(size, parts, tables, inverses):
-    rank, snaps = size.rank, size.snaps
+def eliminate(size, parts, tables, diagonals, known, inverses):
     whole = pl.BlockSpec(memory_space=pltpu.VMEM)
     return pl.pallas_call(
         functools.partial(eliminate_kernel, size),
-        in_specs=[whole] * (size.parts + 11),
+        in_specs=[whole] * (size.parts + 14),
         out_specs=pl.BlockSpec(memory_space=pl.ANY),
         out_shape=jax.ShapeDtypeStruct((size.rows, size.cols), F32),
-        scratch_shapes=[
-            pltpu.VMEM((snaps, 2 * rank), BF16),
-            pltpu.VMEM((2 * rank, snaps), BF16),
-            pltpu.VMEM((2 * size.panel_pad, snaps), BF16),
-            pltpu.VMEM((size.rows_feats, snaps), BF16),
-            pltpu.VMEM((snaps, size.cols_pad), BF16),
-            pltpu.VMEM((size.rows_feats, snaps), BF16),
-            pltpu.VMEM((size.packed, snaps), F32),
-            pltpu.VMEM((size.packed, snaps), BF16),
+        scratch_shapes=[pltpu.VMEM(shape, BF16) for shape in feature_shapes(size)]
+        + [
+            pltpu.VMEM((size.rows_feats, size.snaps), BF16),
+            pltpu.VMEM((size.packed, size.snaps), F32),
+            pltpu.VMEM((size.packed, size.snaps), BF16),
             pltpu.VMEM((size.packed, size.packed), F32),
             pltpu.VMEM((size.rows, size.cols), F32),
             pltpu.SemaphoreType.DMA((len(size.row_blocks),)),
         ],
         compiler_params=pltpu.CompilerParams(vmem_limit_bytes=VMEM_LIMIT),
         name="eliminate",
-    )(*parts, *tables, *inverses)
+    )(*parts, *tables, *diagonals, *known, *inverses)
 
 
 def partner(values, axis, distance):
@@ -352,14 +398,14 @@
         rows=rows,
         cols=cols,
         block=block,
-        parts=lax.axis_size("tm"),
+        parts=lax.axis_size("tm") // 2,
         panel_width=width,
         panel_pad=panel_pad,
         panel_total=panels * width,
         packed=width // LANES * LANES + panel_pad,
         rows_pad=round_up(rows, LANES),
         count=count,
-        cols_pad=round_up(cols, 256),
+        cols_pad=round_up(cols, LANES),
         chunk=176,
     )
     size.rows_feats = round_up(rows, size.chunk)
@@ -368,18 +414,24 @@
     gaps = [(0, panel_pad - width)], [(shift, panel_pad - width - shift)]
     inverses = [jnp.pad(panel_inverse[k], gaps[k] * 2) for k in range(2)]
 
-    makers = [prepare_rows, prepare_cols]
-    tables = []
+    makers = [lambda: prepare_rows(size, feature_order, regular), lambda: prepare_cols(size, feature_order, regular)]
+    makers.append(lambda: inverses)
+    made = []
     for distance in distances("node"):
         total = total + partner(total, "node", distance)
         if makers:
-            made = makers.pop(0)(size, feature_order, regular)
-            total, made = lax.optimization_barrier((total, made))
-            tables += made
+            total, ready = lax.optimization_barrier((total, makers.pop(0)()))
+            made += ready
+    made += [array for maker in makers for array in maker()]
+    lead_r, trail_r, one_r, diag_col, diag_panel, lead_c, trail_c, one_c, diag_cols, inverse0, inverse1 = made
+    tables = (lead_r, trail_r, one_r, lead_c, trail_c, one_c)
+
     parts = [total]
-    for distance in reversed(distances("tm")):
+    for distance in distances("tm")[:-1]:
         parts = parts + [partner(part, "tm", distance) for part in parts]
-    return eliminate(size, parts, tables, inverses)
+    others = [partner(part, "tm", distances("tm")[-1]) for part in parts]
+    known = features(size, parts, tables)
+    return eliminate(size, others, tables, (diag_col, diag_panel, diag_cols), known, (inverse0, inverse1))
 
 
 def solution(mesh):

time: 35.7 us -> 34.1 us (0.955)
  local copies, waits for them, and re-layouts: 4 us -> 0.93 us
  Pallas kernels: 15.8 us -> 17.3 us
  other arithmetic: 0.87 us -> 0.03 us
  waiting for transfers between devices: 4 us -> 4.64 us
    slice x1, local copies, waits for them, and re-layouts: 2.17 us -> 0.62 us  [per_device(): inverses = [jnp.pad(panel_inverse[k], gaps[k] * 2) for k in range(2)]]
    unnamed x4 -> x2, local copies, waits for them, and re-layouts: 1.53 us -> 0.01 us
    pallas_call x2, Pallas kernels: 2.16 us -> 3.66 us  [prepare(): pl.pallas_call(functools.partial(kernel, size), in_specs=[pl.BlockSpec(me...]
    pallas_call x0 -> x1, Pallas kernels: none -> 1.28 us  [features(): pl.pallas_call(functools.partial(features_kernel, size), in_specs=[pl.Blo...]
    add x3, other arithmetic: 0.87 us -> 0.03 us  [per_device(): total = total + partner(total, 'node', distance)]
    pallas_call x1, Pallas kernels: 10.8 us -> 10 us  [eliminate(): pl.pallas_call(functools.partial(eliminate_kernel, size), in_specs=[whole...]
    ppermute x6, waiting for transfers between devices: 4 us -> 4.64 us  [partner(): return lax.ppermute(values, axis, [(i, i ^ distance) for i in range(count)])]
    pallas_call x1, Pallas kernels: 2.87 us -> 2.33 us  [project(): pl.pallas_call(project_kernel, grid=(nodes // block,), in_specs=[pl.Block...]
  transfers between devices with their start and end apart: 6 -> 6, of which waited for: 5 -> 4; matrix products, arithmetic and copies ran while one was open for 7% -> 3% of each run, Pallas kernels for 6% -> 15%
where the time goes in v4:
time: 34.1 us; the launch traced here: 33.8 us
  Pallas kernels  17.3 us (51%)
  starting transfers between devices  10.7 us (31%)
  waiting for transfers between devices  4.64 us (14%)
  local copies, waits for them, and re-layouts  0.93 us (3%)
    ppermute x6, starting transfers between devices, partner(): return lax.ppermute(values, axis, [(i, i ^ distance) for i in range(count)])  10.7 us
    pallas_call x1, Pallas kernels, eliminate(): pl.pallas_call(functools.partial(eliminate_kernel, size), in_specs=[whole...  10 us
    ppermute x6, waiting for transfers between devices, partner(): return lax.ppermute(values, axis, [(i, i ^ distance) for i in range(count)])  4.64 us
    pallas_call x2, Pallas kernels, prepare(): pl.pallas_call(functools.partial(kernel, size), in_specs=[pl.BlockSpec(me...  3.66 us
    pallas_call x1, Pallas kernels, project(): pl.pallas_call(project_kernel, grid=(nodes // block,), in_specs=[pl.Block...  2.33 us
    pallas_call x1, Pallas kernels, features(): pl.pallas_call(functools.partial(features_kernel, size), in_specs=[pl.Blo...  1.28 us
  transfers between devices with their start and end apart: 6, of which 4 were waited for; matrix products, arithmetic and copies ran while one was open for 3% of the time, Pallas kernels for 15%

profile of v4, /device:TPU:0, one launch (start us, length us, event | category | flops | bytes accessed | tf_op | source)
XLA Modules:
  0.0 33.8 jit_solution(16729492241600721754)
XLA Ops:
  0.0 0.0 copy-start
  0.0 2.3 %project.1 = f32[128,128]{1,0:T(8,128)S(1)} custom-call(s32[4096,128]{1,0:T(8,128)} %codes_ref.1, f32[1,4096]{1,0:T(1,128)} %bitcast.5, bf16[4096,128]{1,0:T(8,128)(2,1)} %basis_ref.1), custom_call_target="tpu_custom_call" | custom-call | tf_op jit(solution)/shard_map/project/pallas_call | solution.py:53
  2.3 3.0 %collective-permute-start = (f32[128,128]{1,0:T(8,128)S(1)}, f32[128,128]{1,0:T(8,128)S(1)}, u32[]{:S(2)}, u32[]{:S(2)}) collective-permute-start(f32[128,128]{1,0:T(8,128)S(1)} %project.1), channel_id=1, source_target_pairs={{0,4},{4,0},{8,12},{12,8},{16,20},{20,16},{24,28},{28,24},{1,5},{5... | collective-permute-start | bytes 196616 | tf_op jit(solution)/shard_map/ppermute | solution.py:372
  5.3 1.7 %prepare_rows.1 = (bf16[1920,128]{1,0:T(8,128)(2,1)S(1)}, bf16[1920,128]{1,0:T(8,128)(2,1)S(1)}, f32[1920,128]{1,0:T(8,128)S(1)}, f32[640,128]{1,0:T(8,128)S(1)}, f32[1,640]{1,0:T(1,128)S(1)}) custom-call(s32[8384]{0:T(1024)} %order_ref.3, f32[8384]{0:T(1024)} %regular_ref.3), custom_call_target="tpu_custom_call" | custom-call | flops 3000000 | bytes 2000000 | tf_op jit(solution)/shard_map/prepare_rows/pallas_call | solution.py:128
  7.0 0.6 %collective-permute-done = f32[128,128]{1,0:T(8,128)S(1)} collective-permute-done((f32[128,128]{1,0:T(8,128)S(1)}, f32[128,128]{1,0:T(8,128)S(1)}, u32[]{:S(2)}, u32[]{:S(2)}) %collective-permute-start) | collective-permute-done | bytes 65568 | tf_op jit(solution)/shard_map/ppermute | solution.py:372
  7.6 2.2 %collective-permute-start.1 = (f32[128,128]{1,0:T(8,128)S(1)}, f32[128,128]{1,0:T(8,128)S(1)}, u32[]{:S(2)}, u32[]{:S(2)}) collective-permute-start(f32[128,128]{1,0:T(8,128)S(1)} %add.13), channel_id=1, source_target_pairs={{0,8},{4,12},{8,0},{12,4},{16,24},{20,28},{24,16},{28,20},{1,9},{5... | collective-permute-start | bytes 196616 | tf_op jit(solution)/shard_map/ppermute | solution.py:372
  9.8 0.0 copy-done
  9.8 0.6 %fusion = (f32[1,262,262]{2,0,1:T(1,128)S(1)}, f32[1,262,262]{2,0,1:T(1,128)S(1)}) fusion(f32[2,262,262]{2,0,1:T(2,128)S(1)} %copy-done), kind=kLoop, calls=%fused_computation.2 | loop fusion | bytes 1098304 | tf_op jit(solution)/shard_map/slice | solution.py:415
  10.4 2.0 %prepare_cols.1 = (bf16[128,2176]{1,0:T(8,128)(2,1)S(1)}, bf16[128,2176]{1,0:T(8,128)(2,1)S(1)}, f32[1,2176]{1,0:T(1,128)S(1)}, f32[1,2176]{1,0:T(1,128)S(1)}) custom-call(s32[8384]{0:T(1024)} %order_ref.3, f32[8384]{0:T(1024)} %regular_ref.3), custom_call_target="tpu_custom_call" | custom-call | flops 3000000 | bytes 2000000 | tf_op jit(solution)/shard_map/prepare_cols/pallas_call | solution.py:128
  12.4 0.0 collective-permute-done.1
  12.4 2.7 %collective-permute-start.2 = (f32[128,128]{1,0:T(8,128)S(1)}, f32[128,128]{1,0:T(8,128)S(1)}, u32[]{:S(2)}, u32[]{:S(2)}) collective-permute-start(f32[128,128]{1,0:T(8,128)S(1)} %add.14), channel_id=1, source_target_pairs={{0,16},{4,20},{8,24},{12,28},{16,0},{20,4},{24,8},{28,12},{1,17},{... | collective-permute-start | bytes 196616 | tf_op jit(solution)/shard_map/ppermute | solution.py:372
  15.1 0.1 copy_bitcast_fusion
  15.2 0.2 pad.9.refs_15_
  15.5 2.2 %collective-permute-done.2 = f32[128,128]{1,0:T(8,128)S(1)} collective-permute-done((f32[128,128]{1,0:T(8,128)S(1)}, f32[128,128]{1,0:T(8,128)S(1)}, u32[]{:S(2)}, u32[]{:S(2)}) %collective-permute-start.2) | collective-permute-done | bytes 65568 | tf_op jit(solution)/shard_map/ppermute | solution.py:372
  17.7 0.1 collective-permute-start.4
  17.8 1.6 %collective-permute-start.3 = (f32[128,128]{1,0:T(8,128)S(1)}, f32[128,128]{1,0:T(8,128)S(1)}, u32[]{:S(2)}, u32[]{:S(2)}) collective-permute-start(f32[128,128]{1,0:T(8,128)S(1)} %add.15.refs_0_), channel_id=1, source_target_pairs={{0,2},{1,3},{2,0},{3,1},{4,6},{5,7},{6,4},{7,5},{8,10},{9,11},{10,... | collective-permute-start | bytes 196616 | tf_op jit(solution)/shard_map/ppermute | solution.py:372
  19.4 0.0 collective-permute-done.4.refs_1_
  19.4 1.2 %collective-permute-start.5 = (f32[128,128]{1,0:T(8,128)S(1)}, f32[128,128]{1,0:T(8,128)S(1)}, u32[]{:S(2)}, u32[]{:S(2)}) collective-permute-start(f32[128,128]{1,0:T(8,128)S(1)} %collective-permute-done.4.refs_1_), channel_id=1, source_target_pairs={{0,2},{1,3},{2,0},{3,1},{4,6},{5,7},{6,4},{7,5},{8,10},{9,11},{10,... | collective-permute-start | bytes 196616 | tf_op jit(solution)/shard_map/ppermute | solution.py:372
  20.6 1.3 %features.1 = (bf16[768,256]{1,0:T(8,128)(2,1)S(1)}, bf16[1056,256]{1,0:T(8,128)(2,1)S(1)}, bf16[256,2176]{1,0:T(8,128)(2,1)S(1)}) custom-call(f32[128,128]{1,0:T(8,128)S(1)} %add.15.refs_0_, f32[128,128]{1,0:T(8,128)S(1)} %collective-permute-done.4.refs_1_, bf16[1920,128]{1,0:T(8,128)(2,1)S(1)} %get-tuple-element.43.refs_2_, ...), custom_call_target="tpu_custom_call" | custom-call | flops 1000000000 | bytes 2000000 | tf_op jit(solution)/shard_map/features/pallas_call | solution.py:198
  21.8 0.6 %collective-permute-done.3.refs_0_ = f32[128,128]{1,0:T(8,128)S(1)} collective-permute-done((f32[128,128]{1,0:T(8,128)S(1)}, f32[128,128]{1,0:T(8,128)S(1)}, u32[]{:S(2)}, u32[]{:S(2)}) %collective-permute-start.3) | collective-permute-done | bytes 65568 | tf_op jit(solution)/shard_map/ppermute | solution.py:372
  22.4 1.2 %collective-permute-done.5.refs_1_ = f32[128,128]{1,0:T(8,128)S(1)} collective-permute-done((f32[128,128]{1,0:T(8,128)S(1)}, f32[128,128]{1,0:T(8,128)S(1)}, u32[]{:S(2)}, u32[]{:S(2)}) %collective-permute-start.5) | collective-permute-done | bytes 65568 | tf_op jit(solution)/shard_map/ppermute | solution.py:372
  23.7 10.0 %eliminate.1 = f32[1048,2096]{1,0:T(8,128)} custom-call(f32[128,128]{1,0:T(8,128)S(1)} %collective-permute-done.3.refs_0_, f32[128,128]{1,0:T(8,128)S(1)} %collective-permute-done.5.refs_1_, bf16[1920,128]{1,0:T(8,128)(2,1)S(1)} %get-tuple-element.43.refs_2_, bf16[1920,128]{1,0:T(8,128)(2,1)S(1)} %get-tuple-element.44.refs_3_, ...), custom_call_target="tpu_custom_call" | custom-call | tf_op jit(solution)/shard_map/eliminate/pallas_call | solution.py:351
  (4 shorter events, 0.1 us)
Async XLA Ops:
  0.0 9.8 %copy-start = (f32[2,262,262]{2,0,1:T(2,128)S(1)}, f32[2,262,262]{2,0,1:T(2,128)}, u32[]{:S(2)}) copy-start(f32[2,262,262]{2,0,1:T(2,128)} %param.11) | copy-start | bytes 1647460
  2.3 5.3 %collective-permute-start = (f32[128,128]{1,0:T(8,128)S(1)}, f32[128,128]{1,0:T(8,128)S(1)}, u32[]{:S(2)}, u32[]{:S(2)}) collective-permute-start(f32[128,128]{1,0:T(8,128)S(1)} %project.1), channel_id=1, source_target_pairs={{0,4},{4,0},{8,12},{12,8},{16,20},{20,16},{24,28},{28,24},{1,5},{5... | collective-permute-start | bytes 196616 | tf_op jit(solution)/shard_map/ppermute | solution.py:372
  7.6 4.8 %collective-permute-start.1 = (f32[128,128]{1,0:T(8,128)S(1)}, f32[128,128]{1,0:T(8,128)S(1)}, u32[]{:S(2)}, u32[]{:S(2)}) collective-permute-start(f32[128,128]{1,0:T(8,128)S(1)} %add.13), channel_id=1, source_target_pairs={{0,8},{4,12},{8,0},{12,4},{16,24},{20,28},{24,16},{28,20},{1,9},{5... | collective-permute-start | bytes 196616 | tf_op jit(solution)/shard_map/ppermute | solution.py:372
  12.4 5.2 %collective-permute-start.2 = (f32[128,128]{1,0:T(8,128)S(1)}, f32[128,128]{1,0:T(8,128)S(1)}, u32[]{:S(2)}, u32[]{:S(2)}) collective-permute-start(f32[128,128]{1,0:T(8,128)S(1)} %add.14), channel_id=1, source_target_pairs={{0,16},{4,20},{8,24},{12,28},{16,0},{20,4},{24,8},{28,12},{1,17},{... | collective-permute-start | bytes 196616 | tf_op jit(solution)/shard_map/ppermute | solution.py:372
  17.7 1.7 %collective-permute-start.4 = (f32[128,128]{1,0:T(8,128)S(1)}, f32[128,128]{1,0:T(8,128)S(1)}, u32[]{:S(2)}, u32[]{:S(2)}) collective-permute-start(f32[128,128]{1,0:T(8,128)S(1)} %add.15.refs_0_), channel_id=1, source_target_pairs={{0,1},{1,0},{2,3},{3,2},{4,5},{5,4},{6,7},{7,6},{8,9},{9,8},{10,11... | collective-permute-start | bytes 196616 | tf_op jit(solution)/shard_map/ppermute | solution.py:372
  17.8 4.7 %collective-permute-start.3 = (f32[128,128]{1,0:T(8,128)S(1)}, f32[128,128]{1,0:T(8,128)S(1)}, u32[]{:S(2)}, u32[]{:S(2)}) collective-permute-start(f32[128,128]{1,0:T(8,128)S(1)} %add.15.refs_0_), channel_id=1, source_target_pairs={{0,2},{1,3},{2,0},{3,1},{4,6},{5,7},{6,4},{7,5},{8,10},{9,11},{10,... | collective-permute-start | bytes 196616 | tf_op jit(solution)/shard_map/ppermute | solution.py:372
  19.4 4.3 %collective-permute-start.5 = (f32[128,128]{1,0:T(8,128)S(1)}, f32[128,128]{1,0:T(8,128)S(1)}, u32[]{:S(2)}, u32[]{:S(2)}) collective-permute-start(f32[128,128]{1,0:T(8,128)S(1)} %collective-permute-done.4.refs_1_), channel_id=1, source_target_pairs={{0,2},{1,3},{2,0},{3,1},{4,6},{5,7},{6,4},{7,5},{8,10},{9,11},{10,... | collective-permute-start | bytes 196616 | tf_op jit(solution)/shard_map/ppermute | solution.py:372

commit v5 on v4

--- a/solution.py
+++ b/solution.py
@@ -10,8 +10,10 @@
 F32 = jnp.float32
 BF16 = jnp.bfloat16
 LANES = 128
-VMEM_LIMIT = 32 * 1024 * 1024
+VMEM_LIMIT = 36 * 1024 * 1024
+VMEM_LIMIT_LONG = 54 * 1024 * 1024
 SMALL_VMEM = 16 * 1024 * 1024
+OWN_AT = 0
 FILL = (3, 4, 4, 4)
 JOIN = (0, 3, 6, 9)
 
@@ -209,7 +211,7 @@
     parts, refs = refs[: size.parts], refs[size.parts :]
     tables, refs = refs[:6], refs[6:]
     diag_col, diag_panel, diag_cols, feats_p0, feats_r0, feats_c0, inverse0, inverse1 = refs[:8]
-    out, feats_p1, feats_r1, feats_c1, weights, panel_w, panel_w16, schur_q, block_sum, sems = refs[8:]
+    out, feats_p1, feats_r1, feats_c1, weights, panel_w, panel_w16, schur_q, block_own, factor, block_sum, sems = refs[8:]
     row_offset = lax.axis_index("node") * size.rows
     col_offset = lax.axis_index("tm") * size.cols
     snaps, block, rows, cols = size.snaps, size.block, size.rows, size.cols
@@ -280,52 +282,74 @@
     spread = mm_tn(jnp.concatenate([first, left1], axis=0), jnp.concatenate([scaled0, scaled1_16], axis=0))
     spread = (spread * inv_snaps).astype(BF16)
     fill(FILL[3])
+    fill(len(fillers))
+    def make_weights(start, count):
+        feats = row_block(start, count)
+        weight = (feats.astype(F32) - mm(feats, spread)) * inv_snaps
+        inside = min(count, size.packed - start)
+        if inside > 0:
+            own = panel_w[pl.ds(start, inside), :]
+            own = own * jnp.concatenate([diag_col[pl.ds(start, inside), :]] * (snaps // LANES), axis=1)
+            if inside < count:
+                own = jnp.concatenate([own, jnp.zeros((count - inside, snaps), F32)], axis=0)
+            weight = weight - own
+        weights[pl.ds(start, count), :] = weight.astype(BF16)
+
+    make_weights(*size.row_blocks[0])
     back = first.astype(F32) - mm_tn(cross, scaled1_16)
     packed = pack(mm(inv0, back.astype(BF16)), scaled1, 0) * inv_snaps
     panel_w[...] = packed
     panel_w16[...] = packed.astype(BF16)
-    fill(len(fillers))
-    for start in range(0, size.rows_feats, chunk):
-        feats = row_block(start, chunk)
-        weight = (feats.astype(F32) - mm(feats, spread)) * inv_snaps
-        inside = min(chunk, size.packed - start)
-        if inside > 0:
-            own = panel_w[pl.ds(start, inside), :]
-            own = own * jnp.concatenate([diag_col[pl.ds(start, inside), :]] * (snaps // LANES), axis=1)
-            if inside < chunk:
-                own = jnp.concatenate([own, jnp.zeros((chunk - inside, snaps), F32)], axis=0)
-            weight = weight - own
-        weights[pl.ds(start, chunk), :] = weight.astype(BF16)
-
     delta = row_offset - col_offset
 
     def write(first_panel):
+        used = min(size.packed, cols) if first_panel else 0
+        edge = round_up(used, LANES)
+        here = pl.ds(0, edge)
+
+        def panel_columns():
+            return jnp.concatenate([feats_c0[:, here], feats_c1[:, here]], axis=0)
+
+        def make_factor():
+            near = panel_columns()
+            weighted = (near.astype(F32) - mm(spread, near)) * inv_snaps
+            factor[:, here] = (weighted - panel_w[...].T[:, :edge] * diag_panel[:, here]).astype(BF16)
+
+        def make_own():
+            own = mm(panel_w16[...], panel_columns()) + schur_q[:, here] * diag_panel[:, here]
+            block_own[:, here] = own * jnp.concatenate([diag_col[...]] * (edge // LANES), axis=1)
+
         copies = []
         for index, (start, count) in enumerate(size.row_blocks):
+            if index + 1 < len(size.row_blocks):
+                make_weights(*size.row_blocks[index + 1])
             kept = min(count, rows - start)
             at = pl.ds(start, kept)
-            every = jnp.concatenate([feats_c0[...], feats_c1[...]], axis=0)
-            full = mm(weights[pl.ds(start, count), :], every)[:kept, :cols]
-            row_id = lax.broadcasted_iota(jnp.int32, full.shape, 0)
-            col_id = lax.broadcasted_iota(jnp.int32, full.shape, 1)
-            full = full + jnp.where(col_id - row_id == delta + start, diag_cols[:, pl.ds(0, cols)], 0.0)
+
+            def with_diagonal(values, first_col):
+                row_id = lax.broadcasted_iota(jnp.int32, values.shape, 0)
+                col_id = lax.broadcasted_iota(jnp.int32, values.shape, 1)
+                there = col_id - row_id == delta + (start - first_col)
+                return values + jnp.where(there, diag_cols[:, pl.ds(first_col, values.shape[1])], 0.0)
+
+            if used < cols:
+                rest = pl.ds(edge, size.cols_pad - edge)
+                every = jnp.concatenate([feats_c0[:, rest], feats_c1[:, rest]], axis=0)
+                right = mm(weights[pl.ds(start, count), :], every)[:kept, : cols - edge]
+                block_sum[at, pl.ds(edge, cols - edge)] = with_diagonal(right, edge)
             if first_panel:
-                used = min(size.packed, cols)
-                diag = diag_panel[:, pl.ds(0, used)]
-                left = mm_nt(row_block(start, count), panel_w16[...])[:kept, :used]
+                if index == 0:
+                    make_factor()
+                if index == OWN_AT:
+                    make_own()
+                left = mm(row_block(start, count), factor[:, here])[:kept, :used]
                 inside = min(kept, size.packed - start)
                 if inside > 0:
-                    own = jnp.concatenate([diag_col[pl.ds(start, inside), :]] * (size.packed // LANES), axis=1)
-                    own = (own * schur_q[pl.ds(start, inside), :])[:, :used]
+                    mine = block_own[pl.ds(start, inside), pl.ds(0, used)]
                     if inside < kept:
-                        own = jnp.concatenate([own, jnp.zeros((kept - inside, used), F32)], axis=0)
-                    left = left + own
-                part = full[:, :used] - left * diag
-                block_sum[at, pl.ds(0, used)] = part
-                if used < cols:
-                    block_sum[at, pl.ds(used, cols - used)] = full[:, used:]
-            else:
-                block_sum[at, :] = full
+                        mine = jnp.concatenate([mine, jnp.zeros((kept - inside, used), F32)], axis=0)
+                    left = left - mine
+                block_sum[at, pl.ds(0, used)] = with_diagonal(left, 0)
             copy = pltpu.make_async_copy(block_sum.at[at, :], out.at[at, :], sems.at[index])
             copy.start()
             copies.append(copy)
@@ -359,10 +383,12 @@
             pltpu.VMEM((size.packed, size.snaps), F32),
             pltpu.VMEM((size.packed, size.snaps), BF16),
             pltpu.VMEM((size.packed, size.packed), F32),
+            pltpu.VMEM((size.packed, size.packed), F32),
+            pltpu.VMEM((size.snaps, size.packed), BF16),
             pltpu.VMEM((size.rows, size.cols), F32),
             pltpu.SemaphoreType.DMA((len(size.row_blocks),)),
         ],
-        compiler_params=pltpu.CompilerParams(vmem_limit_bytes=VMEM_LIMIT),
+        compiler_params=pltpu.CompilerParams(vmem_limit_bytes=VMEM_LIMIT if size.snaps <= 512 else VMEM_LIMIT_LONG),
         name="eliminate",
     )(*parts, *tables, *diagonals, *known, *inverses)
 
@@ -379,7 +405,7 @@
 
 
 def row_blocks(rows):
-    return [(start, min(176, rows - start)) for start in range(0, rows, 176)]
+    return [(start, min(176, rows - start)) for start in range(0, rows, 176)][::-1]
 
 
 def per_device(codes, node_scale, basis, regular, feature_order, panel_inverse):
@@ -411,27 +437,30 @@
     size.rows_feats = round_up(rows, size.chunk)
     size.row_blocks = row_blocks(size.rows_feats)
     total = project(codes, node_scale, basis)
+
+    made = []
+    for turn, distance in enumerate(distances("node")):
+        total = total + partner(total, "node", distance)
+        if turn == 0:
+            total, ready = lax.optimization_barrier((total, prepare_rows(size, feature_order, regular)))
+            made += ready
+        elif turn == 1:
+            ready = prepare_cols(size, feature_order, regular)
+            total, ready, panel_inverse = lax.optimization_barrier((total, ready, panel_inverse))
+            made += ready
+    lead_r, trail_r, one_r, diag_col, diag_panel, lead_c, trail_c, one_c, diag_cols = made
+    tables = (lead_r, trail_r, one_r, lead_c, trail_c, one_c)
     gaps = [(0, panel_pad - width)], [(shift, panel_pad - width - shift)]
     inverses = [jnp.pad(panel_inverse[k], gaps[k] * 2) for k in range(2)]
 
-    makers = [lambda: prepare_rows(size, feature_order, regular), lambda: prepare_cols(size, feature_order, regular)]
-    makers.append(lambda: inverses)
-    made = []
-    for distance in distances("node"):
-        total = total + partner(total, "node", distance)
-        if makers:
-            total, ready = lax.optimization_barrier((total, makers.pop(0)()))
-            made += ready
-    made += [array for maker in makers for array in maker()]
-    lead_r, trail_r, one_r, diag_col, diag_panel, lead_c, trail_c, one_c, diag_cols, inverse0, inverse1 = made
-    tables = (lead_r, trail_r, one_r, lead_c, trail_c, one_c)
-
-    parts = [total]
-    for distance in distances("tm")[:-1]:
+    *near, last = distances("tm")
+    parts, others = [total], [partner(total, "tm", last)]
+    for distance in near:
         parts = parts + [partner(part, "tm", distance) for part in parts]
-    others = [partner(part, "tm", distances("tm")[-1]) for part in parts]
     known = features(size, parts, tables)
-    return eliminate(size, others, tables, (diag_col, diag_panel, diag_cols), known, (inverse0, inverse1))
+    for distance in near:
+        others = others + [partner(part, "tm", distance) for part in others]
+    return eliminate(size, others, tables, (diag_col, diag_panel, diag_cols), known, inverses)
 
 
 def solution(mesh):

time: 34.1 us -> 33.6 us (0.985)
  waiting for transfers between devices: 4.64 us -> 5.41 us
  local copies, waits for them, and re-layouts: 0.93 us -> 0.34 us
  starting transfers between devices: 10.7 us -> 10.3 us
    ppermute x6, waiting for transfers between devices: 4.64 us -> 5.41 us  [partner(): return lax.ppermute(values, axis, [(i, i ^ distance) for i in range(count)])]
    slice x1 -> x0, local copies, waits for them, and re-layouts: 0.62 us -> none  [per_device(): inverses = [jnp.pad(panel_inverse[k], gaps[k] * 2) for k in range(2)]]
    ppermute x6, starting transfers between devices: 10.7 us -> 10.3 us  [partner(): return lax.ppermute(values, axis, [(i, i ^ distance) for i in range(count)])]
  transfers between devices with their start and end apart: 6 -> 6, of which waited for: 4 -> 4; matrix products, arithmetic and copies ran while one was open for 3% -> 1% of each run, Pallas kernels for 15% -> 15%
where the time goes in v5:
time: 33.6 us; the launch traced here: 33.4 us
  Pallas kernels  17.1 us (51%)
  starting transfers between devices  10.3 us (31%)
  waiting for transfers between devices  5.41 us (16%)
  local copies, waits for them, and re-layouts  0.34 us (1%)
    ppermute x6, starting transfers between devices, partner(): return lax.ppermute(values, axis, [(i, i ^ distance) for i in range(count)])  10.3 us
    pallas_call x1, Pallas kernels, eliminate(): pl.pallas_call(functools.partial(eliminate_kernel, size), in_specs=[whole...  9.83 us
    ppermute x6, waiting for transfers between devices, partner(): return lax.ppermute(values, axis, [(i, i ^ distance) for i in range(count)])  5.41 us
    pallas_call x2, Pallas kernels, prepare(): pl.pallas_call(functools.partial(kernel, size), in_specs=[pl.BlockSpec(me...  3.65 us
    pallas_call x1, Pallas kernels, project(): pl.pallas_call(project_kernel, grid=(nodes // block,), in_specs=[pl.Block...  2.33 us
    pallas_call x1, Pallas kernels, features(): pl.pallas_call(functools.partial(features_kernel, size), in_specs=[pl.Blo...  1.28 us
  transfers between devices with their start and end apart: 6, of which 4 were waited for; matrix products, arithmetic and copies ran while one was open for 1% of the time, Pallas kernels for 15%

profile of v5, /device:TPU:0, one launch (start us, length us, event | category | flops | bytes accessed | tf_op | source)
XLA Modules:
  0.0 33.4 jit_solution(9332645151632091551)
XLA Ops:
  0.0 0.0 copy-start
  0.0 2.3 %project.1 = f32[128,128]{1,0:T(8,128)S(1)} custom-call(s32[4096,128]{1,0:T(8,128)} %codes_ref.1, f32[1,4096]{1,0:T(1,128)} %bitcast.5, bf16[4096,128]{1,0:T(8,128)(2,1)} %basis_ref.1), custom_call_target="tpu_custom_call" | custom-call | tf_op jit(solution)/shard_map/project/pallas_call | solution.py:55
  2.3 3.0 %collective-permute-start = (f32[128,128]{1,0:T(8,128)S(1)}, f32[128,128]{1,0:T(8,128)S(1)}, u32[]{:S(2)}, u32[]{:S(2)}) collective-permute-start(f32[128,128]{1,0:T(8,128)S(1)} %project.1), channel_id=1, source_target_pairs={{0,4},{4,0},{8,12},{12,8},{16,20},{20,16},{24,28},{28,24},{1,5},{5... | collective-permute-start | bytes 196616 | tf_op jit(solution)/shard_map/ppermute | solution.py:398
  5.3 1.7 %prepare_rows.1 = (bf16[1920,128]{1,0:T(8,128)(2,1)S(1)}, bf16[1920,128]{1,0:T(8,128)(2,1)S(1)}, f32[1920,128]{1,0:T(8,128)S(1)}, f32[640,128]{1,0:T(8,128)S(1)}, f32[1,640]{1,0:T(1,128)S(1)}) custom-call(s32[8384]{0:T(1024)} %order_ref.3, f32[8384]{0:T(1024)} %regular_ref.3), custom_call_target="tpu_custom_call" | custom-call | flops 3000000 | bytes 2000000 | tf_op jit(solution)/shard_map/prepare_rows/pallas_call | solution.py:130
  7.0 0.6 %collective-permute-done = f32[128,128]{1,0:T(8,128)S(1)} collective-permute-done((f32[128,128]{1,0:T(8,128)S(1)}, f32[128,128]{1,0:T(8,128)S(1)}, u32[]{:S(2)}, u32[]{:S(2)}) %collective-permute-start) | collective-permute-done | bytes 65568 | tf_op jit(solution)/shard_map/ppermute | solution.py:398
  7.6 2.2 %collective-permute-start.1 = (f32[128,128]{1,0:T(8,128)S(1)}, f32[128,128]{1,0:T(8,128)S(1)}, u32[]{:S(2)}, u32[]{:S(2)}) collective-permute-start(f32[128,128]{1,0:T(8,128)S(1)} %add.13), channel_id=1, source_target_pairs={{0,8},{4,12},{8,0},{12,4},{16,24},{20,28},{24,16},{28,20},{1,9},{5... | collective-permute-start | bytes 196616 | tf_op jit(solution)/shard_map/ppermute | solution.py:398
  9.8 2.0 %prepare_cols.1 = (bf16[128,2176]{1,0:T(8,128)(2,1)S(1)}, bf16[128,2176]{1,0:T(8,128)(2,1)S(1)}, f32[1,2176]{1,0:T(1,128)S(1)}, f32[1,2176]{1,0:T(1,128)S(1)}) custom-call(s32[8384]{0:T(1024)} %order_ref.3, f32[8384]{0:T(1024)} %regular_ref.3), custom_call_target="tpu_custom_call" | custom-call | flops 3000000 | bytes 2000000 | tf_op jit(solution)/shard_map/prepare_cols/pallas_call | solution.py:130
  11.8 0.2 collective-permute-done.1
  12.0 3.1 %collective-permute-start.2 = (f32[128,128]{1,0:T(8,128)S(1)}, f32[128,128]{1,0:T(8,128)S(1)}, u32[]{:S(2)}, u32[]{:S(2)}) collective-permute-start(f32[128,128]{1,0:T(8,128)S(1)} %add.14), channel_id=1, source_target_pairs={{0,16},{4,20},{8,24},{12,28},{16,0},{20,4},{24,8},{28,12},{1,17},{... | collective-permute-start | bytes 196616 | tf_op jit(solution)/shard_map/ppermute | solution.py:398
  15.1 0.0 copy-done
  15.1 0.1 copy.7
  15.2 2.2 %collective-permute-done.2 = f32[128,128]{1,0:T(8,128)S(1)} collective-permute-done((f32[128,128]{1,0:T(8,128)S(1)}, f32[128,128]{1,0:T(8,128)S(1)}, u32[]{:S(2)}, u32[]{:S(2)}) %collective-permute-start.2) | collective-permute-done | bytes 65568 | tf_op jit(solution)/shard_map/ppermute | solution.py:398
  17.4 0.1 collective-permute-start.5
  17.5 1.9 %collective-permute-start.3 = (f32[128,128]{1,0:T(8,128)S(1)}, f32[128,128]{1,0:T(8,128)S(1)}, u32[]{:S(2)}, u32[]{:S(2)}) collective-permute-start(f32[128,128]{1,0:T(8,128)S(1)} %add.15.refs_0_), channel_id=1, source_target_pairs={{0,2},{1,3},{2,0},{3,1},{4,6},{5,7},{6,4},{7,5},{8,10},{9,11},{10,... | collective-permute-start | bytes 196616 | tf_op jit(solution)/shard_map/ppermute | solution.py:398
  19.4 0.1 slice_bitcast_fusion
  19.4 0.2 pad.9.refs_15_
  19.7 2.4 %collective-permute-done.3.refs_0_ = f32[128,128]{1,0:T(8,128)S(1)} collective-permute-done((f32[128,128]{1,0:T(8,128)S(1)}, f32[128,128]{1,0:T(8,128)S(1)}, u32[]{:S(2)}, u32[]{:S(2)}) %collective-permute-start.3) | collective-permute-done | bytes 65568 | tf_op jit(solution)/shard_map/ppermute | solution.py:398
  22.1 0.0 collective-permute-start.4
  22.1 0.0 collective-permute-done.5.refs_1_
  22.1 1.3 %features.1 = (bf16[768,256]{1,0:T(8,128)(2,1)S(1)}, bf16[1056,256]{1,0:T(8,128)(2,1)S(1)}, bf16[256,2176]{1,0:T(8,128)(2,1)S(1)}) custom-call(f32[128,128]{1,0:T(8,128)S(1)} %add.15.refs_0_, f32[128,128]{1,0:T(8,128)S(1)} %collective-permute-done.5.refs_1_, bf16[1920,128]{1,0:T(8,128)(2,1)S(1)} %get-tuple-element.40.refs_2_, ...), custom_call_target="tpu_custom_call" | custom-call | flops 1000000000 | bytes 2000000 | tf_op jit(solution)/shard_map/features/pallas_call | solution.py:200
  23.4 0.0 collective-permute-done.4.refs_1_
  23.4 9.8 %eliminate.1 = f32[1048,2096]{1,0:T(8,128)} custom-call(f32[128,128]{1,0:T(8,128)S(1)} %collective-permute-done.3.refs_0_, f32[128,128]{1,0:T(8,128)S(1)} %collective-permute-done.4.refs_1_, bf16[1920,128]{1,0:T(8,128)(2,1)S(1)} %get-tuple-element.40.refs_2_, bf16[1920,128]{1,0:T(8,128)(2,1)S(1)} %get-tuple-element.41.refs_3_, ...), custom_call_target="tpu_custom_call" | custom-call | tf_op jit(solution)/shard_map/eliminate/pallas_call | solution.py:375
  (4 shorter events, 0.1 us)
Async XLA Ops:
  0.0 15.1 %copy-start = (f32[2,262,262]{2,0,1:T(2,128)S(1)}, f32[2,262,262]{2,0,1:T(2,128)}, u32[]{:S(2)}) copy-start(f32[2,262,262]{2,0,1:T(2,128)} %param.11) | copy-start | bytes 1647460
  2.3 5.3 %collective-permute-start = (f32[128,128]{1,0:T(8,128)S(1)}, f32[128,128]{1,0:T(8,128)S(1)}, u32[]{:S(2)}, u32[]{:S(2)}) collective-permute-start(f32[128,128]{1,0:T(8,128)S(1)} %project.1), channel_id=1, source_target_pairs={{0,4},{4,0},{8,12},{12,8},{16,20},{20,16},{24,28},{28,24},{1,5},{5... | collective-permute-start | bytes 196616 | tf_op jit(solution)/shard_map/ppermute | solution.py:398
  7.6 4.4 %collective-permute-start.1 = (f32[128,128]{1,0:T(8,128)S(1)}, f32[128,128]{1,0:T(8,128)S(1)}, u32[]{:S(2)}, u32[]{:S(2)}) collective-permute-start(f32[128,128]{1,0:T(8,128)S(1)} %add.13), channel_id=1, source_target_pairs={{0,8},{4,12},{8,0},{12,4},{16,24},{20,28},{24,16},{28,20},{1,9},{5... | collective-permute-start | bytes 196616 | tf_op jit(solution)/shard_map/ppermute | solution.py:398
  12.0 5.3 %collective-permute-start.2 = (f32[128,128]{1,0:T(8,128)S(1)}, f32[128,128]{1,0:T(8,128)S(1)}, u32[]{:S(2)}, u32[]{:S(2)}) collective-permute-start(f32[128,128]{1,0:T(8,128)S(1)} %add.14), channel_id=1, source_target_pairs={{0,16},{4,20},{8,24},{12,28},{16,0},{20,4},{24,8},{28,12},{1,17},{... | collective-permute-start | bytes 196616 | tf_op jit(solution)/shard_map/ppermute | solution.py:398
  17.4 4.7 %collective-permute-start.5 = (f32[128,128]{1,0:T(8,128)S(1)}, f32[128,128]{1,0:T(8,128)S(1)}, u32[]{:S(2)}, u32[]{:S(2)}) collective-permute-start(f32[128,128]{1,0:T(8,128)S(1)} %add.15.refs_0_), channel_id=1, source_target_pairs={{0,1},{1,0},{2,3},{3,2},{4,5},{5,4},{6,7},{7,6},{8,9},{9,8},{10,11... | collective-permute-start | bytes 196616 | tf_op jit(solution)/shard_map/ppermute | solution.py:398
  17.5 4.6 %collective-permute-start.3 = (f32[128,128]{1,0:T(8,128)S(1)}, f32[128,128]{1,0:T(8,128)S(1)}, u32[]{:S(2)}, u32[]{:S(2)}) collective-permute-start(f32[128,128]{1,0:T(8,128)S(1)} %add.15.refs_0_), channel_id=1, source_target_pairs={{0,2},{1,3},{2,0},{3,1},{4,6},{5,7},{6,4},{7,5},{8,10},{9,11},{10,... | collective-permute-start | bytes 196616 | tf_op jit(solution)/shard_map/ppermute | solution.py:398
  22.1 1.3 %collective-permute-start.4 = (f32[128,128]{1,0:T(8,128)S(1)}, f32[128,128]{1,0:T(8,128)S(1)}, u32[]{:S(2)}, u32[]{:S(2)}) collective-permute-start(f32[128,128]{1,0:T(8,128)S(1)} %collective-permute-done.3.refs_0_), channel_id=1, source_target_pairs={{0,1},{1,0},{2,3},{3,2},{4,5},{5,4},{6,7},{7,6},{8,9},{9,8},{10,11... | collective-permute-start | bytes 196616 | tf_op jit(solution)/shard_map/ppermute | solution.py:398

commit v6 on v5

--- a/solution.py
+++ b/solution.py
@@ -178,8 +178,8 @@
     return row_features, column_features
 
 
-def features_kernel(size, *refs):
-    parts, refs = refs[: size.parts], refs[size.parts :]
+def features_kernel(size, count, *refs):
+    parts, refs = refs[:count], refs[count:]
     tables, (feats_p, feats_r, feats_c) = refs[:6], refs[6:]
     row_features, column_features = feature_makers(parts, *tables)
     for start in range(0, 2 * size.panel_pad, size.panel_pad):
@@ -187,31 +187,32 @@
     for start in range(0, size.rows_feats, size.chunk):
         feats_r[pl.ds(start, size.chunk), :] = row_features(start, size.chunk)
     for start in range(0, size.cols_pad, size.block):
-        count = min(size.block, size.cols_pad - start)
-        feats_c[:, pl.ds(start, count)] = column_features(start, count)
-
-
-def feature_shapes(size):
-    half = size.snaps // 2
-    return [(2 * size.panel_pad, half), (size.rows_feats, half), (half, size.cols_pad)]
+        width = min(size.block, size.cols_pad - start)
+        feats_c[:, pl.ds(start, width)] = column_features(start, width)
+
+
+def feature_shapes(size, parts):
+    snaps = sum(part.shape[1] for part in parts)
+    return [(2 * size.panel_pad, snaps), (size.rows_feats, snaps), (snaps, size.cols_pad)]
 
 
 def features(size, parts, tables):
     return pl.pallas_call(
-        functools.partial(features_kernel, size),
-        in_specs=[pl.BlockSpec(memory_space=pltpu.VMEM)] * (size.parts + 6),
-        out_shape=[jax.ShapeDtypeStruct(shape, BF16) for shape in feature_shapes(size)],
+        functools.partial(features_kernel, size, len(parts)),
+        in_specs=[pl.BlockSpec(memory_space=pltpu.VMEM)] * (len(parts) + 6),
+        out_shape=[jax.ShapeDtypeStruct(shape, BF16) for shape in feature_shapes(size, parts)],
         compiler_params=pltpu.CompilerParams(vmem_limit_bytes=SMALL_VMEM),
-        cost_estimate=pl.CostEstimate(flops=1_000_000_000, bytes_accessed=2_000_000, transcendentals=0),
+        cost_estimate=pl.CostEstimate(flops=500_000_000 * len(parts), bytes_accessed=2_000_000, transcendentals=0),
         name="features",
     )(*parts, *tables)
 
 
-def eliminate_kernel(size, *refs):
-    parts, refs = refs[: size.parts], refs[size.parts :]
+def eliminate_kernel(size, count, *refs):
+    parts, refs = refs[:count], refs[count:]
     tables, refs = refs[:6], refs[6:]
-    diag_col, diag_panel, diag_cols, feats_p0, feats_r0, feats_c0, inverse0, inverse1 = refs[:8]
-    out, feats_p1, feats_r1, feats_c1, weights, panel_w, panel_w16, schur_q, block_own, factor, block_sum, sems = refs[8:]
+    (diag_col, diag_panel, diag_cols), known, (inverse0, inverse1) = refs[:3], refs[3:9], refs[9:11]
+    out, feats_p, feats_r, feats_c, weights, panel_w, panel_w16, schur_q, block_own, factor, block_sum, sems = refs[11:]
+    all_p, all_r, all_c = (*known[0::3], feats_p), (*known[1::3], feats_r), (*known[2::3], feats_c)
     row_offset = lax.axis_index("node") * size.rows
     col_offset = lax.axis_index("tm") * size.cols
     snaps, block, rows, cols = size.snaps, size.block, size.rows, size.cols
@@ -220,8 +221,10 @@
     row_features, column_features = feature_makers(parts, *tables)
 
     def row_block(start, count):
-        at = pl.ds(start, count)
-        return jnp.concatenate([feats_r0[at, :], feats_r1[at, :]], axis=1)
+        return jnp.concatenate([feats[pl.ds(start, count), :] for feats in all_r], axis=1)
+
+    def column_block(start, count):
+        return jnp.concatenate([feats[:, pl.ds(start, count)] for feats in all_c], axis=0)
 
     joint = size.panel_width // LANES * LANES
     over = pad - joint
@@ -240,16 +243,15 @@
             count -= 1
 
     def make_rows(start):
-        feats_r1[pl.ds(start, chunk), :] = row_features(start, chunk)
+        feats_r[pl.ds(start, chunk), :] = row_features(start, chunk)
 
     def make_columns(start, count):
-        feats_c1[:, pl.ds(start, count)] = column_features(start, count)
+        feats_c[:, pl.ds(start, count)] = column_features(start, count)
 
     panels = []
     for start in range(0, 2 * pad, pad):
-        at = pl.ds(start, pad)
-        feats_p1[at, :] = row_features(size.rows_pad + start, pad)
-        panels.append(jnp.concatenate([feats_p0[at, :], feats_p1[at, :]], axis=1))
+        feats_p[pl.ds(start, pad), :] = row_features(size.rows_pad + start, pad)
+        panels.append(jnp.concatenate([feats[pl.ds(start, pad), :] for feats in all_p], axis=1))
     for start in range(0, size.rows_feats, chunk):
         fillers.append(functools.partial(make_rows, start))
     for start in range(0, size.cols_pad, block):
@@ -308,7 +310,7 @@
         here = pl.ds(0, edge)
 
         def panel_columns():
-            return jnp.concatenate([feats_c0[:, here], feats_c1[:, here]], axis=0)
+            return column_block(0, edge)
 
         def make_factor():
             near = panel_columns()
@@ -333,8 +335,7 @@
                 return values + jnp.where(there, diag_cols[:, pl.ds(first_col, values.shape[1])], 0.0)
 
             if used < cols:
-                rest = pl.ds(edge, size.cols_pad - edge)
-                every = jnp.concatenate([feats_c0[:, rest], feats_c1[:, rest]], axis=0)
+                every = column_block(edge, size.cols_pad - edge)
                 right = mm(weights[pl.ds(start, count), :], every)[:kept, : cols - edge]
                 block_sum[at, pl.ds(edge, cols - edge)] = with_diagonal(right, edge)
             if first_panel:
@@ -373,11 +374,11 @@
 def eliminate(size, parts, tables, diagonals, known, inverses):
     whole = pl.BlockSpec(memory_space=pltpu.VMEM)
     return pl.pallas_call(
-        functools.partial(eliminate_kernel, size),
-        in_specs=[whole] * (size.parts + 14),
+        functools.partial(eliminate_kernel, size, len(parts)),
+        in_specs=[whole] * (len(parts) + 17),
         out_specs=pl.BlockSpec(memory_space=pl.ANY),
         out_shape=jax.ShapeDtypeStruct((size.rows, size.cols), F32),
-        scratch_shapes=[pltpu.VMEM(shape, BF16) for shape in feature_shapes(size)]
+        scratch_shapes=[pltpu.VMEM(shape, BF16) for shape in feature_shapes(size, parts)]
         + [
             pltpu.VMEM((size.rows_feats, size.snaps), BF16),
             pltpu.VMEM((size.packed, size.snaps), F32),
@@ -424,7 +425,6 @@
         rows=rows,
         cols=cols,
         block=block,
-        parts=lax.axis_size("tm") // 2,
         panel_width=width,
         panel_pad=panel_pad,
         panel_total=panels * width,
@@ -438,6 +438,8 @@
     size.row_blocks = row_blocks(size.rows_feats)
     total = project(codes, node_scale, basis)
 
+    gaps = [(0, panel_pad - width)], [(shift, panel_pad - width - shift)]
+
     made = []
     for turn, distance in enumerate(distances("node")):
         total = total + partner(total, "node", distance)
@@ -448,19 +450,22 @@
             ready = prepare_cols(size, feature_order, regular)
             total, ready, panel_inverse = lax.optimization_barrier((total, ready, panel_inverse))
             made += ready
+            inverses = [jnp.pad(panel_inverse[k], gaps[k] * 2) for k in range(2)]
+        elif turn == 2:
+            total, inverses = lax.optimization_barrier((total, inverses))
     lead_r, trail_r, one_r, diag_col, diag_panel, lead_c, trail_c, one_c, diag_cols = made
     tables = (lead_r, trail_r, one_r, lead_c, trail_c, one_c)
-    gaps = [(0, panel_pad - width)], [(shift, panel_pad - width - shift)]
-    inverses = [jnp.pad(panel_inverse[k], gaps[k] * 2) for k in range(2)]
-
     *near, last = distances("tm")
     parts, others = [total], [partner(total, "tm", last)]
     for distance in near:
         parts = parts + [partner(part, "tm", distance) for part in parts]
     known = features(size, parts, tables)
-    for distance in near:
+    others, known = lax.optimization_barrier((others, known))
+    for distance in near[:-1]:
         others = others + [partner(part, "tm", distance) for part in others]
-    return eliminate(size, others, tables, (diag_col, diag_panel, diag_cols), known, inverses)
+    rest = [partner(part, "tm", near[-1]) for part in others]
+    known = [*known, *features(size, others, tables)]
+    return eliminate(size, rest, tables, (diag_col, diag_panel, diag_cols), known, inverses)
 
 
 def solution(mesh):

time: 33.6 us -> 33.4 us (level)
  waiting for transfers between devices: 5.41 us -> 4.39 us
  Pallas kernels: 17.1 us -> 17.9 us
    ppermute x6, waiting for transfers between devices: 5.41 us -> 4.39 us  [partner(): return lax.ppermute(values, axis, [(i, i ^ distance) for i in range(count)])]
    pallas_call x2 -> x3, Pallas kernels: 11.1 us -> 12 us  [the longest x1 9.7 us: eliminate(): pl.pallas_call(functools.partial(eliminate_kernel, size, len(parts)), in_...]
  transfers between devices with their start and end apart: 6 -> 6, of which waited for: 4 -> 5; matrix products, arithmetic and copies ran while one was open for 1% -> 1% of each run, Pallas kernels for 15% -> 18%
where the time goes in v6:
time: 33.4 us; the launch traced here: 33.2 us
  Pallas kernels  17.9 us (54%)
  starting transfers between devices  10.3 us (31%)
  waiting for transfers between devices  4.39 us (13%)
  local copies, waits for them, and re-layouts  0.34 us (1%)
    ppermute x6, starting transfers between devices, partner(): return lax.ppermute(values, axis, [(i, i ^ distance) for i in range(count)])  10.3 us
    pallas_call x1, Pallas kernels, eliminate(): pl.pallas_call(functools.partial(eliminate_kernel, size, len(parts)), in_...  9.7 us
    ppermute x6, waiting for transfers between devices, partner(): return lax.ppermute(values, axis, [(i, i ^ distance) for i in range(count)])  4.39 us
    pallas_call x2, Pallas kernels, prepare(): pl.pallas_call(functools.partial(kernel, size), in_specs=[pl.BlockSpec(me...  3.65 us
    pallas_call x1, Pallas kernels, project(): pl.pallas_call(project_kernel, grid=(nodes // block,), in_specs=[pl.Block...  2.33 us
    pallas_call x2, Pallas kernels, features(): pl.pallas_call(functools.partial(features_kernel, size, len(parts)), in_s...  2.25 us
  transfers between devices with their start and end apart: 6, of which 5 were waited for; matrix products, arithmetic and copies ran while one was open for 1% of the time, Pallas kernels for 18%

profile of v6, /device:TPU:0, one launch (start us, length us, event | category | flops | bytes accessed | tf_op | source)
XLA Modules:
  0.0 33.2 jit_solution(8076001093226164162)
XLA Ops:
  0.0 0.0 copy-start
  0.0 2.3 %project.1 = f32[128,128]{1,0:T(8,128)S(1)} custom-call(s32[4096,128]{1,0:T(8,128)} %codes_ref.1, f32[1,4096]{1,0:T(1,128)} %bitcast.5, bf16[4096,128]{1,0:T(8,128)(2,1)} %basis_ref.1), custom_call_target="tpu_custom_call" | custom-call | tf_op jit(solution)/shard_map/project/pallas_call | solution.py:55
  2.3 3.0 %collective-permute-start = (f32[128,128]{1,0:T(8,128)S(1)}, f32[128,128]{1,0:T(8,128)S(1)}, u32[]{:S(2)}, u32[]{:S(2)}) collective-permute-start(f32[128,128]{1,0:T(8,128)S(1)} %project.1), channel_id=1, source_target_pairs={{0,4},{4,0},{8,12},{12,8},{16,20},{20,16},{24,28},{28,24},{1,5},{5... | collective-permute-start | bytes 196616 | tf_op jit(solution)/shard_map/ppermute | solution.py:399
  5.3 1.7 %prepare_rows.1 = (bf16[1920,128]{1,0:T(8,128)(2,1)S(1)}, bf16[1920,128]{1,0:T(8,128)(2,1)S(1)}, f32[1920,128]{1,0:T(8,128)S(1)}, f32[640,128]{1,0:T(8,128)S(1)}, f32[1,640]{1,0:T(1,128)S(1)}) custom-call(s32[8384]{0:T(1024)} %order_ref.3, f32[8384]{0:T(1024)} %regular_ref.3), custom_call_target="tpu_custom_call" | custom-call | flops 3000000 | bytes 2000000 | tf_op jit(solution)/shard_map/prepare_rows/pallas_call | solution.py:130
  7.0 0.6 %collective-permute-done = f32[128,128]{1,0:T(8,128)S(1)} collective-permute-done((f32[128,128]{1,0:T(8,128)S(1)}, f32[128,128]{1,0:T(8,128)S(1)}, u32[]{:S(2)}, u32[]{:S(2)}) %collective-permute-start) | collective-permute-done | bytes 65568 | tf_op jit(solution)/shard_map/ppermute | solution.py:399
  7.6 2.2 %collective-permute-start.1 = (f32[128,128]{1,0:T(8,128)S(1)}, f32[128,128]{1,0:T(8,128)S(1)}, u32[]{:S(2)}, u32[]{:S(2)}) collective-permute-start(f32[128,128]{1,0:T(8,128)S(1)} %add.13), channel_id=1, source_target_pairs={{0,8},{4,12},{8,0},{12,4},{16,24},{20,28},{24,16},{28,20},{1,9},{5... | collective-permute-start | bytes 196616 | tf_op jit(solution)/shard_map/ppermute | solution.py:399
  9.8 2.0 %prepare_cols.1 = (bf16[128,2176]{1,0:T(8,128)(2,1)S(1)}, bf16[128,2176]{1,0:T(8,128)(2,1)S(1)}, f32[1,2176]{1,0:T(1,128)S(1)}, f32[1,2176]{1,0:T(1,128)S(1)}) custom-call(s32[8384]{0:T(1024)} %order_ref.3, f32[8384]{0:T(1024)} %regular_ref.3), custom_call_target="tpu_custom_call" | custom-call | flops 3000000 | bytes 2000000 | tf_op jit(solution)/shard_map/prepare_cols/pallas_call | solution.py:130
  11.8 0.2 collective-permute-done.1
  12.0 3.1 %collective-permute-start.2 = (f32[128,128]{1,0:T(8,128)S(1)}, f32[128,128]{1,0:T(8,128)S(1)}, u32[]{:S(2)}, u32[]{:S(2)}) collective-permute-start(f32[128,128]{1,0:T(8,128)S(1)} %add.14), channel_id=1, source_target_pairs={{0,16},{4,20},{8,24},{12,28},{16,0},{20,4},{24,8},{28,12},{1,17},{... | collective-permute-start | bytes 196616 | tf_op jit(solution)/shard_map/ppermute | solution.py:399
  15.1 0.0 copy-done
  15.1 0.1 copy.7
  15.2 0.1 slice_bitcast_fusion
  15.3 0.2 pad.9.refs_17_
  15.5 1.9 %collective-permute-done.2 = f32[128,128]{1,0:T(8,128)S(1)} collective-permute-done((f32[128,128]{1,0:T(8,128)S(1)}, f32[128,128]{1,0:T(8,128)S(1)}, u32[]{:S(2)}, u32[]{:S(2)}) %collective-permute-start.2) | collective-permute-done | bytes 65568 | tf_op jit(solution)/shard_map/ppermute | solution.py:399
  17.4 0.1 collective-permute-start.4
  17.5 1.9 %collective-permute-start.3 = (f32[128,128]{1,0:T(8,128)S(1)}, f32[128,128]{1,0:T(8,128)S(1)}, u32[]{:S(2)}, u32[]{:S(2)}) collective-permute-start(f32[128,128]{1,0:T(8,128)S(1)} %add.15.refs_0_), channel_id=1, source_target_pairs={{0,2},{1,3},{2,0},{3,1},{4,6},{5,7},{6,4},{7,5},{8,10},{9,11},{10,... | collective-permute-start | bytes 196616 | tf_op jit(solution)/shard_map/ppermute | solution.py:399
  19.4 0.0 collective-permute-done.4.refs_1_
  19.4 1.3 %features.2 = (bf16[768,256]{1,0:T(8,128)(2,1)S(1)}, bf16[1056,256]{1,0:T(8,128)(2,1)S(1)}, bf16[256,2176]{1,0:T(8,128)(2,1)S(1)}) custom-call(f32[128,128]{1,0:T(8,128)S(1)} %add.15.refs_0_, f32[128,128]{1,0:T(8,128)S(1)} %collective-permute-done.4.refs_1_, bf16[1920,128]{1,0:T(8,128)(2,1)S(1)} %get-tuple-element.52.refs_2_.refs_1_, ...), custom_call_target="tpu_custom_call" | custom-call | flops 1000000000 | bytes 2000000 | tf_op jit(solution)/shard_map/features/pallas_call | solution.py:200
  20.7 1.4 %collective-permute-done.3.refs_0_ = f32[128,128]{1,0:T(8,128)S(1)} collective-permute-done((f32[128,128]{1,0:T(8,128)S(1)}, f32[128,128]{1,0:T(8,128)S(1)}, u32[]{:S(2)}, u32[]{:S(2)}) %collective-permute-start.3) | collective-permute-done | bytes 65568 | tf_op jit(solution)/shard_map/ppermute | solution.py:399
  22.1 0.0 collective-permute-start.5
  22.1 1.0 %features.3 = (bf16[768,128]{1,0:T(8,128)(2,1)S(1)}, bf16[1056,128]{1,0:T(8,128)(2,1)S(1)}, bf16[128,2176]{1,0:T(8,128)(2,1)S(1)}) custom-call(f32[128,128]{1,0:T(8,128)S(1)} %collective-permute-done.3.refs_0_, bf16[1920,128]{1,0:T(8,128)(2,1)S(1)} %get-tuple-element.52.refs_2_.refs_1_, bf16[1920,128]{1,0:T(8,128)(2,1)S(1)} %get-tuple-element.53.refs_3_.refs_2_, ...), custom_call_target="tpu_custom_call" | custom-call | flops 500000000 | bytes 2000000 | tf_op jit(solution)/shard_map/features/pallas_call | solution.py:200
  23.0 0.3 collective-permute-done.5.refs_0_
  23.3 9.7 %eliminate.1 = f32[1048,2096]{1,0:T(8,128)} custom-call(f32[128,128]{1,0:T(8,128)S(1)} %collective-permute-done.5.refs_0_, bf16[1920,128]{1,0:T(8,128)(2,1)S(1)} %get-tuple-element.52.refs_2_.refs_1_, bf16[1920,128]{1,0:T(8,128)(2,1)S(1)} %get-tuple-element.53.refs_3_.refs_2_, f32[1920,128]{1,0:T(8,128)S(1)} %get-tuple-element.54.refs_4_.refs_3_, ...), custom_call_target="tpu_custom_call" | custom-call | tf_op jit(solution)/shard_map/eliminate/pallas_call | solution.py:376
  (4 shorter events, 0.1 us)
Async XLA Ops:
  0.0 15.1 %copy-start = (f32[2,262,262]{2,0,1:T(2,128)S(1)}, f32[2,262,262]{2,0,1:T(2,128)}, u32[]{:S(2)}) copy-start(f32[2,262,262]{2,0,1:T(2,128)} %param.11) | copy-start | bytes 1647460
  2.3 5.3 %collective-permute-start = (f32[128,128]{1,0:T(8,128)S(1)}, f32[128,128]{1,0:T(8,128)S(1)}, u32[]{:S(2)}, u32[]{:S(2)}) collective-permute-start(f32[128,128]{1,0:T(8,128)S(1)} %project.1), channel_id=1, source_target_pairs={{0,4},{4,0},{8,12},{12,8},{16,20},{20,16},{24,28},{28,24},{1,5},{5... | collective-permute-start | bytes 196616 | tf_op jit(solution)/shard_map/ppermute | solution.py:399
  7.6 4.4 %collective-permute-start.1 = (f32[128,128]{1,0:T(8,128)S(1)}, f32[128,128]{1,0:T(8,128)S(1)}, u32[]{:S(2)}, u32[]{:S(2)}) collective-permute-start(f32[128,128]{1,0:T(8,128)S(1)} %add.13), channel_id=1, source_target_pairs={{0,8},{4,12},{8,0},{12,4},{16,24},{20,28},{24,16},{28,20},{1,9},{5... | collective-permute-start | bytes 196616 | tf_op jit(solution)/shard_map/ppermute | solution.py:399
  12.0 5.3 %collective-permute-start.2 = (f32[128,128]{1,0:T(8,128)S(1)}, f32[128,128]{1,0:T(8,128)S(1)}, u32[]{:S(2)}, u32[]{:S(2)}) collective-permute-start(f32[128,128]{1,0:T(8,128)S(1)} %add.14), channel_id=1, source_target_pairs={{0,16},{4,20},{8,24},{12,28},{16,0},{20,4},{24,8},{28,12},{1,17},{... | collective-permute-start | bytes 196616 | tf_op jit(solution)/shard_map/ppermute | solution.py:399
  17.4 2.0 %collective-permute-start.4 = (f32[128,128]{1,0:T(8,128)S(1)}, f32[128,128]{1,0:T(8,128)S(1)}, u32[]{:S(2)}, u32[]{:S(2)}) collective-permute-start(f32[128,128]{1,0:T(8,128)S(1)} %add.15.refs_0_), channel_id=1, source_target_pairs={{0,1},{1,0},{2,3},{3,2},{4,5},{5,4},{6,7},{7,6},{8,9},{9,8},{10,11... | collective-permute-start | bytes 196616 | tf_op jit(solution)/shard_map/ppermute | solution.py:399
  17.5 4.6 %collective-permute-start.3 = (f32[128,128]{1,0:T(8,128)S(1)}, f32[128,128]{1,0:T(8,128)S(1)}, u32[]{:S(2)}, u32[]{:S(2)}) collective-permute-start(f32[128,128]{1,0:T(8,128)S(1)} %add.15.refs_0_), channel_id=1, source_target_pairs={{0,2},{1,3},{2,0},{3,1},{4,6},{5,7},{6,4},{7,5},{8,10},{9,11},{10,... | collective-permute-start | bytes 196616 | tf_op jit(solution)/shard_map/ppermute | solution.py:399
  22.1 1.3 %collective-permute-start.5 = (f32[128,128]{1,0:T(8,128)S(1)}, f32[128,128]{1,0:T(8,128)S(1)}, u32[]{:S(2)}, u32[]{:S(2)}) collective-permute-start(f32[128,128]{1,0:T(8,128)S(1)} %collective-permute-done.3.refs_0_), channel_id=1, source_target_pairs={{0,1},{1,0},{2,3},{3,2},{4,5},{5,4},{6,7},{7,6},{8,9},{9,8},{10,11... | collective-permute-start | bytes 196616 | tf_op jit(solution)/shard_map/ppermute | solution.py:399

commit v7 on v6

--- a/solution.py
+++ b/solution.py
@@ -13,7 +13,6 @@
 VMEM_LIMIT = 36 * 1024 * 1024
 VMEM_LIMIT_LONG = 54 * 1024 * 1024
 SMALL_VMEM = 16 * 1024 * 1024
-OWN_AT = 0
 FILL = (3, 4, 4, 4)
 JOIN = (0, 3, 6, 9)
 
@@ -302,25 +301,20 @@
     packed = pack(mm(inv0, back.astype(BF16)), scaled1, 0) * inv_snaps
     panel_w[...] = packed
     panel_w16[...] = packed.astype(BF16)
+    panel_cols = min(size.packed, size.cols_pad)
+    here = pl.ds(0, panel_cols)
+    near = column_block(0, panel_cols)
+    own = mm(panel_w16[...], near) + schur_q[:, here] * diag_panel[:, here]
+    block_own[:, here] = own * jnp.concatenate([diag_col[...]] * (panel_cols // LANES), axis=1)
+    weighted = (near.astype(F32) - mm(spread, near)) * inv_snaps
+    factor[:, here] = (weighted - panel_w[...].T[:, :panel_cols] * diag_panel[:, here]).astype(BF16)
+
     delta = row_offset - col_offset
 
     def write(first_panel):
         used = min(size.packed, cols) if first_panel else 0
         edge = round_up(used, LANES)
         here = pl.ds(0, edge)
-
-        def panel_columns():
-            return column_block(0, edge)
-
-        def make_factor():
-            near = panel_columns()
-            weighted = (near.astype(F32) - mm(spread, near)) * inv_snaps
-            factor[:, here] = (weighted - panel_w[...].T[:, :edge] * diag_panel[:, here]).astype(BF16)
-
-        def make_own():
-            own = mm(panel_w16[...], panel_columns()) + schur_q[:, here] * diag_panel[:, here]
-            block_own[:, here] = own * jnp.concatenate([diag_col[...]] * (edge // LANES), axis=1)
-
         copies = []
         for index, (start, count) in enumerate(size.row_blocks):
             if index + 1 < len(size.row_blocks):
@@ -339,10 +333,6 @@
                 right = mm(weights[pl.ds(start, count), :], every)[:kept, : cols - edge]
                 block_sum[at, pl.ds(edge, cols - edge)] = with_diagonal(right, edge)
             if first_panel:
-                if index == 0:
-                    make_factor()
-                if index == OWN_AT:
-                    make_own()
                 left = mm(row_block(start, count), factor[:, here])[:kept, :used]
                 inside = min(kept, size.packed - start)
                 if inside > 0:

time: 33.4 us -> 33.4 us (level)
  no operation moved by 1% of the time
where the time goes in v7:
time: 33.4 us; the launch traced here: 33.1 us
  Pallas kernels  17.9 us (54%)
  starting transfers between devices  10.3 us (31%)
  waiting for transfers between devices  4.39 us (13%)
  local copies, waits for them, and re-layouts  0.34 us (1%)
    ppermute x6, starting transfers between devices, partner(): return lax.ppermute(values, axis, [(i, i ^ distance) for i in range(count)])  10.3 us
    pallas_call x1, Pallas kernels, eliminate(): pl.pallas_call(functools.partial(eliminate_kernel, size, len(parts)), in_...  9.63 us
    ppermute x6, waiting for transfers between devices, partner(): return lax.ppermute(values, axis, [(i, i ^ distance) for i in range(count)])  4.39 us
    pallas_call x2, Pallas kernels, prepare(): pl.pallas_call(functools.partial(kernel, size), in_specs=[pl.BlockSpec(me...  3.65 us
    pallas_call x1, Pallas kernels, project(): pl.pallas_call(project_kernel, grid=(nodes // block,), in_specs=[pl.Block...  2.33 us
    pallas_call x2, Pallas kernels, features(): pl.pallas_call(functools.partial(features_kernel, size, len(parts)), in_s...  2.25 us
  transfers between devices with their start and end apart: 6, of which 5 were waited for; matrix products, arithmetic and copies ran while one was open for 1% of the time, Pallas kernels for 18%

profile of v7, /device:TPU:0, one launch (start us, length us, event | category | flops | bytes accessed | tf_op | source)
XLA Modules:
  0.0 33.1 jit_solution(6193591817836195978)
XLA Ops:
  0.0 0.0 copy-start
  0.0 2.3 %project.1 = f32[128,128]{1,0:T(8,128)S(1)} custom-call(s32[4096,128]{1,0:T(8,128)} %codes_ref.1, f32[1,4096]{1,0:T(1,128)} %bitcast.5, bf16[4096,128]{1,0:T(8,128)(2,1)} %basis_ref.1), custom_call_target="tpu_custom_call" | custom-call | tf_op jit(solution)/shard_map/project/pallas_call | solution.py:54
  2.3 3.0 %collective-permute-start = (f32[128,128]{1,0:T(8,128)S(1)}, f32[128,128]{1,0:T(8,128)S(1)}, u32[]{:S(2)}, u32[]{:S(2)}) collective-permute-start(f32[128,128]{1,0:T(8,128)S(1)} %project.1), channel_id=1, source_target_pairs={{0,4},{4,0},{8,12},{12,8},{16,20},{20,16},{24,28},{28,24},{1,5},{5... | collective-permute-start | bytes 196616 | tf_op jit(solution)/shard_map/ppermute | solution.py:389
  5.3 1.7 %prepare_rows.1 = (bf16[1920,128]{1,0:T(8,128)(2,1)S(1)}, bf16[1920,128]{1,0:T(8,128)(2,1)S(1)}, f32[1920,128]{1,0:T(8,128)S(1)}, f32[640,128]{1,0:T(8,128)S(1)}, f32[1,640]{1,0:T(1,128)S(1)}) custom-call(s32[8384]{0:T(1024)} %order_ref.3, f32[8384]{0:T(1024)} %regular_ref.3), custom_call_target="tpu_custom_call" | custom-call | flops 3000000 | bytes 2000000 | tf_op jit(solution)/shard_map/prepare_rows/pallas_call | solution.py:129
  7.0 0.6 %collective-permute-done = f32[128,128]{1,0:T(8,128)S(1)} collective-permute-done((f32[128,128]{1,0:T(8,128)S(1)}, f32[128,128]{1,0:T(8,128)S(1)}, u32[]{:S(2)}, u32[]{:S(2)}) %collective-permute-start) | collective-permute-done | bytes 65568 | tf_op jit(solution)/shard_map/ppermute | solution.py:389
  7.6 2.2 %collective-permute-start.1 = (f32[128,128]{1,0:T(8,128)S(1)}, f32[128,128]{1,0:T(8,128)S(1)}, u32[]{:S(2)}, u32[]{:S(2)}) collective-permute-start(f32[128,128]{1,0:T(8,128)S(1)} %add.13), channel_id=1, source_target_pairs={{0,8},{4,12},{8,0},{12,4},{16,24},{20,28},{24,16},{28,20},{1,9},{5... | collective-permute-start | bytes 196616 | tf_op jit(solution)/shard_map/ppermute | solution.py:389
  9.8 2.0 %prepare_cols.1 = (bf16[128,2176]{1,0:T(8,128)(2,1)S(1)}, bf16[128,2176]{1,0:T(8,128)(2,1)S(1)}, f32[1,2176]{1,0:T(1,128)S(1)}, f32[1,2176]{1,0:T(1,128)S(1)}) custom-call(s32[8384]{0:T(1024)} %order_ref.3, f32[8384]{0:T(1024)} %regular_ref.3), custom_call_target="tpu_custom_call" | custom-call | flops 3000000 | bytes 2000000 | tf_op jit(solution)/shard_map/prepare_cols/pallas_call | solution.py:129
  11.8 0.2 collective-permute-done.1
  12.0 3.1 %collective-permute-start.2 = (f32[128,128]{1,0:T(8,128)S(1)}, f32[128,128]{1,0:T(8,128)S(1)}, u32[]{:S(2)}, u32[]{:S(2)}) collective-permute-start(f32[128,128]{1,0:T(8,128)S(1)} %add.14), channel_id=1, source_target_pairs={{0,16},{4,20},{8,24},{12,28},{16,0},{20,4},{24,8},{28,12},{1,17},{... | collective-permute-start | bytes 196616 | tf_op jit(solution)/shard_map/ppermute | solution.py:389
  15.1 0.0 copy-done
  15.1 0.1 copy.7
  15.2 0.1 slice_bitcast_fusion
  15.3 0.2 pad.9.refs_17_
  15.5 1.9 %collective-permute-done.2 = f32[128,128]{1,0:T(8,128)S(1)} collective-permute-done((f32[128,128]{1,0:T(8,128)S(1)}, f32[128,128]{1,0:T(8,128)S(1)}, u32[]{:S(2)}, u32[]{:S(2)}) %collective-permute-start.2) | collective-permute-done | bytes 65568 | tf_op jit(solution)/shard_map/ppermute | solution.py:389
  17.4 0.1 collective-permute-start.4
  17.5 1.9 %collective-permute-start.3 = (f32[128,128]{1,0:T(8,128)S(1)}, f32[128,128]{1,0:T(8,128)S(1)}, u32[]{:S(2)}, u32[]{:S(2)}) collective-permute-start(f32[128,128]{1,0:T(8,128)S(1)} %add.15.refs_0_), channel_id=1, source_target_pairs={{0,2},{1,3},{2,0},{3,1},{4,6},{5,7},{6,4},{7,5},{8,10},{9,11},{10,... | collective-permute-start | bytes 196616 | tf_op jit(solution)/shard_map/ppermute | solution.py:389
  19.4 0.0 collective-permute-done.4.refs_1_
  19.4 1.3 %features.2 = (bf16[768,256]{1,0:T(8,128)(2,1)S(1)}, bf16[1056,256]{1,0:T(8,128)(2,1)S(1)}, bf16[256,2176]{1,0:T(8,128)(2,1)S(1)}) custom-call(f32[128,128]{1,0:T(8,128)S(1)} %add.15.refs_0_, f32[128,128]{1,0:T(8,128)S(1)} %collective-permute-done.4.refs_1_, bf16[1920,128]{1,0:T(8,128)(2,1)S(1)} %get-tuple-element.52.refs_2_.refs_1_, ...), custom_call_target="tpu_custom_call" | custom-call | flops 1000000000 | bytes 2000000 | tf_op jit(solution)/shard_map/features/pallas_call | solution.py:199
  20.7 1.4 %collective-permute-done.3.refs_0_ = f32[128,128]{1,0:T(8,128)S(1)} collective-permute-done((f32[128,128]{1,0:T(8,128)S(1)}, f32[128,128]{1,0:T(8,128)S(1)}, u32[]{:S(2)}, u32[]{:S(2)}) %collective-permute-start.3) | collective-permute-done | bytes 65568 | tf_op jit(solution)/shard_map/ppermute | solution.py:389
  22.1 0.0 collective-permute-start.5
  22.1 1.0 %features.3 = (bf16[768,128]{1,0:T(8,128)(2,1)S(1)}, bf16[1056,128]{1,0:T(8,128)(2,1)S(1)}, bf16[128,2176]{1,0:T(8,128)(2,1)S(1)}) custom-call(f32[128,128]{1,0:T(8,128)S(1)} %collective-permute-done.3.refs_0_, bf16[1920,128]{1,0:T(8,128)(2,1)S(1)} %get-tuple-element.52.refs_2_.refs_1_, bf16[1920,128]{1,0:T(8,128)(2,1)S(1)} %get-tuple-element.53.refs_3_.refs_2_, ...), custom_call_target="tpu_custom_call" | custom-call | flops 500000000 | bytes 2000000 | tf_op jit(solution)/shard_map/features/pallas_call | solution.py:199
  23.0 0.3 collective-permute-done.5.refs_0_
  23.3 9.6 %eliminate.1 = f32[1048,2096]{1,0:T(8,128)} custom-call(f32[128,128]{1,0:T(8,128)S(1)} %collective-permute-done.5.refs_0_, bf16[1920,128]{1,0:T(8,128)(2,1)S(1)} %get-tuple-element.52.refs_2_.refs_1_, bf16[1920,128]{1,0:T(8,128)(2,1)S(1)} %get-tuple-element.53.refs_3_.refs_2_, f32[1920,128]{1,0:T(8,128)S(1)} %get-tuple-element.54.refs_4_.refs_3_, ...), custom_call_target="tpu_custom_call" | custom-call | tf_op jit(solution)/shard_map/eliminate/pallas_call | solution.py:366
  (4 shorter events, 0.1 us)
Async XLA Ops:
  0.0 15.1 %copy-start = (f32[2,262,262]{2,0,1:T(2,128)S(1)}, f32[2,262,262]{2,0,1:T(2,128)}, u32[]{:S(2)}) copy-start(f32[2,262,262]{2,0,1:T(2,128)} %param.11) | copy-start | bytes 1647460
  2.3 5.3 %collective-permute-start = (f32[128,128]{1,0:T(8,128)S(1)}, f32[128,128]{1,0:T(8,128)S(1)}, u32[]{:S(2)}, u32[]{:S(2)}) collective-permute-start(f32[128,128]{1,0:T(8,128)S(1)} %project.1), channel_id=1, source_target_pairs={{0,4},{4,0},{8,12},{12,8},{16,20},{20,16},{24,28},{28,24},{1,5},{5... | collective-permute-start | bytes 196616 | tf_op jit(solution)/shard_map/ppermute | solution.py:389
  7.6 4.4 %collective-permute-start.1 = (f32[128,128]{1,0:T(8,128)S(1)}, f32[128,128]{1,0:T(8,128)S(1)}, u32[]{:S(2)}, u32[]{:S(2)}) collective-permute-start(f32[128,128]{1,0:T(8,128)S(1)} %add.13), channel_id=1, source_target_pairs={{0,8},{4,12},{8,0},{12,4},{16,24},{20,28},{24,16},{28,20},{1,9},{5... | collective-permute-start | bytes 196616 | tf_op jit(solution)/shard_map/ppermute | solution.py:389
  12.0 5.3 %collective-permute-start.2 = (f32[128,128]{1,0:T(8,128)S(1)}, f32[128,128]{1,0:T(8,128)S(1)}, u32[]{:S(2)}, u32[]{:S(2)}) collective-permute-start(f32[128,128]{1,0:T(8,128)S(1)} %add.14), channel_id=1, source_target_pairs={{0,16},{4,20},{8,24},{12,28},{16,0},{20,4},{24,8},{28,12},{1,17},{... | collective-permute-start | bytes 196616 | tf_op jit(solution)/shard_map/ppermute | solution.py:389
  17.4 2.0 %collective-permute-start.4 = (f32[128,128]{1,0:T(8,128)S(1)}, f32[128,128]{1,0:T(8,128)S(1)}, u32[]{:S(2)}, u32[]{:S(2)}) collective-permute-start(f32[128,128]{1,0:T(8,128)S(1)} %add.15.refs_0_), channel_id=1, source_target_pairs={{0,1},{1,0},{2,3},{3,2},{4,5},{5,4},{6,7},{7,6},{8,9},{9,8},{10,11... | collective-permute-start | bytes 196616 | tf_op jit(solution)/shard_map/ppermute | solution.py:389
  17.5 4.6 %collective-permute-start.3 = (f32[128,128]{1,0:T(8,128)S(1)}, f32[128,128]{1,0:T(8,128)S(1)}, u32[]{:S(2)}, u32[]{:S(2)}) collective-permute-start(f32[128,128]{1,0:T(8,128)S(1)} %add.15.refs_0_), channel_id=1, source_target_pairs={{0,2},{1,3},{2,0},{3,1},{4,6},{5,7},{6,4},{7,5},{8,10},{9,11},{10,... | collective-permute-start | bytes 196616 | tf_op jit(solution)/shard_map/ppermute | solution.py:389
  22.1 1.3 %collective-permute-start.5 = (f32[128,128]{1,0:T(8,128)S(1)}, f32[128,128]{1,0:T(8,128)S(1)}, u32[]{:S(2)}, u32[]{:S(2)}) collective-permute-start(f32[128,128]{1,0:T(8,128)S(1)} %collective-permute-done.3.refs_0_), channel_id=1, source_target_pairs={{0,1},{1,0},{2,3},{3,2},{4,5},{5,4},{6,7},{7,6},{8,9},{9,8},{10,11... | collective-permute-start | bytes 196616 | tf_op jit(solution)/shard_map/ppermute | solution.py:389

commit v8 on v7

--- a/solution.py
+++ b/solution.py
@@ -42,7 +42,7 @@
     def _():
         out_ref[...] = jnp.zeros_like(out_ref)
 
-    modes = basis_ref[...].astype(F32).T * scale_ref[...]
+    modes = basis_ref[...].T.astype(F32) * scale_ref[...]
     out_ref[...] += mm(modes.astype(BF16), codes_ref[...].astype(F32).astype(BF16))
 
 

time: 33.4 us -> 33.4 us (level)
  no operation moved by 1% of the time
where the time goes in v8:
time: 33.4 us; the launch traced here: 33.1 us
  Pallas kernels  17.9 us (54%)
  starting transfers between devices  10.3 us (31%)
  waiting for transfers between devices  4.39 us (13%)
  local copies, waits for them, and re-layouts  0.34 us (1%)
    ppermute x6, starting transfers between devices, partner(): return lax.ppermute(values, axis, [(i, i ^ distance) for i in range(count)])  10.3 us
    pallas_call x1, Pallas kernels, eliminate(): pl.pallas_call(functools.partial(eliminate_kernel, size, len(parts)), in_...  9.64 us
    ppermute x6, waiting for transfers between devices, partner(): return lax.ppermute(values, axis, [(i, i ^ distance) for i in range(count)])  4.39 us
    pallas_call x2, Pallas kernels, prepare(): pl.pallas_call(functools.partial(kernel, size), in_specs=[pl.BlockSpec(me...  3.65 us
    pallas_call x1, Pallas kernels, project(): pl.pallas_call(project_kernel, grid=(nodes // block,), in_specs=[pl.Block...  2.31 us
    pallas_call x2, Pallas kernels, features(): pl.pallas_call(functools.partial(features_kernel, size, len(parts)), in_s...  2.25 us
  transfers between devices with their start and end apart: 6, of which 5 were waited for; matrix products, arithmetic and copies ran while one was open for 1% of the time, Pallas kernels for 18%

profile of v8, /device:TPU:0, one launch (start us, length us, event | category | flops | bytes accessed | tf_op | source)
XLA Modules:
  0.0 33.1 jit_solution(10829494656813746665)
XLA Ops:
  0.0 0.0 copy-start
  0.0 2.3 %project.1 = f32[128,128]{1,0:T(8,128)S(1)} custom-call(s32[4096,128]{1,0:T(8,128)} %codes_ref.1, f32[1,4096]{1,0:T(1,128)} %bitcast.5, bf16[4096,128]{1,0:T(8,128)(2,1)} %basis_ref.1), custom_call_target="tpu_custom_call" | custom-call | tf_op jit(solution)/shard_map/project/pallas_call | solution.py:54
  2.3 3.0 %collective-permute-start = (f32[128,128]{1,0:T(8,128)S(1)}, f32[128,128]{1,0:T(8,128)S(1)}, u32[]{:S(2)}, u32[]{:S(2)}) collective-permute-start(f32[128,128]{1,0:T(8,128)S(1)} %project.1), channel_id=1, source_target_pairs={{0,4},{4,0},{8,12},{12,8},{16,20},{20,16},{24,28},{28,24},{1,5},{5... | collective-permute-start | bytes 196616 | tf_op jit(solution)/shard_map/ppermute | solution.py:389
  5.3 1.7 %prepare_rows.1 = (bf16[1920,128]{1,0:T(8,128)(2,1)S(1)}, bf16[1920,128]{1,0:T(8,128)(2,1)S(1)}, f32[1920,128]{1,0:T(8,128)S(1)}, f32[640,128]{1,0:T(8,128)S(1)}, f32[1,640]{1,0:T(1,128)S(1)}) custom-call(s32[8384]{0:T(1024)} %order_ref.3, f32[8384]{0:T(1024)} %regular_ref.3), custom_call_target="tpu_custom_call" | custom-call | flops 3000000 | bytes 2000000 | tf_op jit(solution)/shard_map/prepare_rows/pallas_call | solution.py:129
  7.0 0.6 %collective-permute-done = f32[128,128]{1,0:T(8,128)S(1)} collective-permute-done((f32[128,128]{1,0:T(8,128)S(1)}, f32[128,128]{1,0:T(8,128)S(1)}, u32[]{:S(2)}, u32[]{:S(2)}) %collective-permute-start) | collective-permute-done | bytes 65568 | tf_op jit(solution)/shard_map/ppermute | solution.py:389
  7.6 2.2 %collective-permute-start.1 = (f32[128,128]{1,0:T(8,128)S(1)}, f32[128,128]{1,0:T(8,128)S(1)}, u32[]{:S(2)}, u32[]{:S(2)}) collective-permute-start(f32[128,128]{1,0:T(8,128)S(1)} %add.13), channel_id=1, source_target_pairs={{0,8},{4,12},{8,0},{12,4},{16,24},{20,28},{24,16},{28,20},{1,9},{5... | collective-permute-start | bytes 196616 | tf_op jit(solution)/shard_map/ppermute | solution.py:389
  9.8 2.0 %prepare_cols.1 = (bf16[128,2176]{1,0:T(8,128)(2,1)S(1)}, bf16[128,2176]{1,0:T(8,128)(2,1)S(1)}, f32[1,2176]{1,0:T(1,128)S(1)}, f32[1,2176]{1,0:T(1,128)S(1)}) custom-call(s32[8384]{0:T(1024)} %order_ref.3, f32[8384]{0:T(1024)} %regular_ref.3), custom_call_target="tpu_custom_call" | custom-call | flops 3000000 | bytes 2000000 | tf_op jit(solution)/shard_map/prepare_cols/pallas_call | solution.py:129
  11.8 0.2 collective-permute-done.1
  12.0 3.1 %collective-permute-start.2 = (f32[128,128]{1,0:T(8,128)S(1)}, f32[128,128]{1,0:T(8,128)S(1)}, u32[]{:S(2)}, u32[]{:S(2)}) collective-permute-start(f32[128,128]{1,0:T(8,128)S(1)} %add.14), channel_id=1, source_target_pairs={{0,16},{4,20},{8,24},{12,28},{16,0},{20,4},{24,8},{28,12},{1,17},{... | collective-permute-start | bytes 196616 | tf_op jit(solution)/shard_map/ppermute | solution.py:389
  15.1 0.0 copy-done
  15.1 0.1 copy.7
  15.2 0.1 slice_bitcast_fusion
  15.2 0.2 pad.9.refs_17_
  15.5 1.9 %collective-permute-done.2 = f32[128,128]{1,0:T(8,128)S(1)} collective-permute-done((f32[128,128]{1,0:T(8,128)S(1)}, f32[128,128]{1,0:T(8,128)S(1)}, u32[]{:S(2)}, u32[]{:S(2)}) %collective-permute-start.2) | collective-permute-done | bytes 65568 | tf_op jit(solution)/shard_map/ppermute | solution.py:389
  17.4 0.1 collective-permute-start.4
  17.4 1.9 %collective-permute-start.3 = (f32[128,128]{1,0:T(8,128)S(1)}, f32[128,128]{1,0:T(8,128)S(1)}, u32[]{:S(2)}, u32[]{:S(2)}) collective-permute-start(f32[128,128]{1,0:T(8,128)S(1)} %add.15.refs_0_), channel_id=1, source_target_pairs={{0,2},{1,3},{2,0},{3,1},{4,6},{5,7},{6,4},{7,5},{8,10},{9,11},{10,... | collective-permute-start | bytes 196616 | tf_op jit(solution)/shard_map/ppermute | solution.py:389
  19.4 0.0 collective-permute-done.4.refs_1_
  19.4 1.3 %features.2 = (bf16[768,256]{1,0:T(8,128)(2,1)S(1)}, bf16[1056,256]{1,0:T(8,128)(2,1)S(1)}, bf16[256,2176]{1,0:T(8,128)(2,1)S(1)}) custom-call(f32[128,128]{1,0:T(8,128)S(1)} %add.15.refs_0_, f32[128,128]{1,0:T(8,128)S(1)} %collective-permute-done.4.refs_1_, bf16[1920,128]{1,0:T(8,128)(2,1)S(1)} %get-tuple-element.52.refs_2_.refs_1_, ...), custom_call_target="tpu_custom_call" | custom-call | flops 1000000000 | bytes 2000000 | tf_op jit(solution)/shard_map/features/pallas_call | solution.py:199
  20.7 1.4 %collective-permute-done.3.refs_0_ = f32[128,128]{1,0:T(8,128)S(1)} collective-permute-done((f32[128,128]{1,0:T(8,128)S(1)}, f32[128,128]{1,0:T(8,128)S(1)}, u32[]{:S(2)}, u32[]{:S(2)}) %collective-permute-start.3) | collective-permute-done | bytes 65568 | tf_op jit(solution)/shard_map/ppermute | solution.py:389
  22.1 0.0 collective-permute-start.5
  22.1 1.0 %features.3 = (bf16[768,128]{1,0:T(8,128)(2,1)S(1)}, bf16[1056,128]{1,0:T(8,128)(2,1)S(1)}, bf16[128,2176]{1,0:T(8,128)(2,1)S(1)}) custom-call(f32[128,128]{1,0:T(8,128)S(1)} %collective-permute-done.3.refs_0_, bf16[1920,128]{1,0:T(8,128)(2,1)S(1)} %get-tuple-element.52.refs_2_.refs_1_, bf16[1920,128]{1,0:T(8,128)(2,1)S(1)} %get-tuple-element.53.refs_3_.refs_2_, ...), custom_call_target="tpu_custom_call" | custom-call | flops 500000000 | bytes 2000000 | tf_op jit(solution)/shard_map/features/pallas_call | solution.py:199
  23.0 0.3 collective-permute-done.5.refs_0_
  23.3 9.6 %eliminate.1 = f32[1048,2096]{1,0:T(8,128)} custom-call(f32[128,128]{1,0:T(8,128)S(1)} %collective-permute-done.5.refs_0_, bf16[1920,128]{1,0:T(8,128)(2,1)S(1)} %get-tuple-element.52.refs_2_.refs_1_, bf16[1920,128]{1,0:T(8,128)(2,1)S(1)} %get-tuple-element.53.refs_3_.refs_2_, f32[1920,128]{1,0:T(8,128)S(1)} %get-tuple-element.54.refs_4_.refs_3_, ...), custom_call_target="tpu_custom_call" | custom-call | tf_op jit(solution)/shard_map/eliminate/pallas_call | solution.py:366
  (4 shorter events, 0.1 us)
Async XLA Ops:
  0.0 15.1 %copy-start = (f32[2,262,262]{2,0,1:T(2,128)S(1)}, f32[2,262,262]{2,0,1:T(2,128)}, u32[]{:S(2)}) copy-start(f32[2,262,262]{2,0,1:T(2,128)} %param.11) | copy-start | bytes 1647460
  2.3 5.2 %collective-permute-start = (f32[128,128]{1,0:T(8,128)S(1)}, f32[128,128]{1,0:T(8,128)S(1)}, u32[]{:S(2)}, u32[]{:S(2)}) collective-permute-start(f32[128,128]{1,0:T(8,128)S(1)} %project.1), channel_id=1, source_target_pairs={{0,4},{4,0},{8,12},{12,8},{16,20},{20,16},{24,28},{28,24},{1,5},{5... | collective-permute-start | bytes 196616 | tf_op jit(solution)/shard_map/ppermute | solution.py:389
  7.6 4.4 %collective-permute-start.1 = (f32[128,128]{1,0:T(8,128)S(1)}, f32[128,128]{1,0:T(8,128)S(1)}, u32[]{:S(2)}, u32[]{:S(2)}) collective-permute-start(f32[128,128]{1,0:T(8,128)S(1)} %add.13), channel_id=1, source_target_pairs={{0,8},{4,12},{8,0},{12,4},{16,24},{20,28},{24,16},{28,20},{1,9},{5... | collective-permute-start | bytes 196616 | tf_op jit(solution)/shard_map/ppermute | solution.py:389
  12.0 5.3 %collective-permute-start.2 = (f32[128,128]{1,0:T(8,128)S(1)}, f32[128,128]{1,0:T(8,128)S(1)}, u32[]{:S(2)}, u32[]{:S(2)}) collective-permute-start(f32[128,128]{1,0:T(8,128)S(1)} %add.14), channel_id=1, source_target_pairs={{0,16},{4,20},{8,24},{12,28},{16,0},{20,4},{24,8},{28,12},{1,17},{... | collective-permute-start | bytes 196616 | tf_op jit(solution)/shard_map/ppermute | solution.py:389
  17.4 2.0 %collective-permute-start.4 = (f32[128,128]{1,0:T(8,128)S(1)}, f32[128,128]{1,0:T(8,128)S(1)}, u32[]{:S(2)}, u32[]{:S(2)}) collective-permute-start(f32[128,128]{1,0:T(8,128)S(1)} %add.15.refs_0_), channel_id=1, source_target_pairs={{0,1},{1,0},{2,3},{3,2},{4,5},{5,4},{6,7},{7,6},{8,9},{9,8},{10,11... | collective-permute-start | bytes 196616 | tf_op jit(solution)/shard_map/ppermute | solution.py:389
  17.4 4.6 %collective-permute-start.3 = (f32[128,128]{1,0:T(8,128)S(1)}, f32[128,128]{1,0:T(8,128)S(1)}, u32[]{:S(2)}, u32[]{:S(2)}) collective-permute-start(f32[128,128]{1,0:T(8,128)S(1)} %add.15.refs_0_), channel_id=1, source_target_pairs={{0,2},{1,3},{2,0},{3,1},{4,6},{5,7},{6,4},{7,5},{8,10},{9,11},{10,... | collective-permute-start | bytes 196616 | tf_op jit(solution)/shard_map/ppermute | solution.py:389
  22.1 1.3 %collective-permute-start.5 = (f32[128,128]{1,0:T(8,128)S(1)}, f32[128,128]{1,0:T(8,128)S(1)}, u32[]{:S(2)}, u32[]{:S(2)}) collective-permute-start(f32[128,128]{1,0:T(8,128)S(1)} %collective-permute-done.3.refs_0_), channel_id=1, source_target_pairs={{0,1},{1,0},{2,3},{3,2},{4,5},{5,4},{6,7},{7,6},{8,9},{9,8},{10,11... | collective-permute-start | bytes 196616 | tf_op jit(solution)/shard_map/ppermute | solution.py:389
